TPU v7x, 128 devices: a whole 4x4x4 slice. The times are simulated.
128 devices in a mesh: turn: 8 (over x, core), river: 16 (over z, y).
Axes of the slice: x: 4, y: 4, z: 4, core: 2. Of those that a mesh axis runs over, the one named last changes fastest.
Arguments:
- river_regret: float32 [9216, 256], P(('turn', 'river')), may hold values from -8 to 8
- turn_regret: float32 [1024, 128], P(('turn', 'river')), may hold values from -8 to 8
- river_bucket: int32 [24, 32, 1081], P('turn', 'river'), may hold values from 0 to 9215
- turn_bucket: int32 [24, 1081], P('turn'), may hold values from 0 to 1023
- ranks: int32 [24, 32, 1081], P('turn', 'river'), may hold values from 0 to 7461
- turn_card: int32 [24], P('turn'), may hold values from 0 to 46, as said below
- river_card: int32 [24, 32], P('turn', 'river'), may hold values from 0 to 46, as said below
- player_range: float32 [64, 1081], replicated, may hold values from 0.1 to 1
- opp_range: float32 [64, 1081], replicated, may hold values from 0.1 to 1
- call_prob: bfloat16 [24, 32, 128, 1081], P('turn', 'river'), may hold values from 0 to 1
- base_pot: float32 [64], replicated, may hold values from 2 to 24
Outputs:
- new_river_regret: float32 [9216, 256], P(('turn', 'river'))
- new_turn_regret: float32 [1024, 128], P(('turn', 'river'))
- br_value: float32 [24, 64, 1081], P('turn', 'river')
Inputs may be any that keep to these rules, and one draw needn't show every extreme that they name: `turn_card`: turn cards are distinct cards of 0 to 46. `river_card`: the river cards of one turn are distinct and differ from that turn's card.
All inputs are finite; a program needn't handle non-finite values.
Results may differ from a plain program's by a relative error of at most 0.0003.
Values sent between devices are 32-bit elements; how exact they have to be, the bound alone decides.
No kernel may reach another device: no remote copies, remote signals or barrier semaphores. Data moves between devices by JAX's collectives and lax.ppermute only.
A program may use at most 128 MiB of HBM per device.

v0:
```python
import jax
import jax.numpy as jnp
import numpy as np
from jax import lax
from jax.sharding import PartitionSpec as P

CARDS = 47


def matching(regret):
    positive = jnp.maximum(regret, 0.0)
    weight_sum = jnp.sum(positive, axis=-1, keepdims=True)
    safe_sum = jnp.where(weight_sum > 0.0, weight_sum, 1.0)
    return jnp.where(weight_sum > 0.0, positive / safe_sum, 0.5)


def board_payoffs(hand_first, hand_second, rank_row, turn_value, river_value):
    playable = (
        (hand_first != turn_value)
        & (hand_second != turn_value)
        & (hand_first != river_value)
        & (hand_second != river_value)
    )
    disjoint = (
        (hand_first[:, None] != hand_first[None, :])
        & (hand_first[:, None] != hand_second[None, :])
        & (hand_second[:, None] != hand_first[None, :])
        & (hand_second[:, None] != hand_second[None, :])
    )
    usable = disjoint & playable[:, None] & playable[None, :]
    direct = jnp.where(usable, 1.0, 0.0).astype(jnp.float32)
    rank_sign = jnp.sign((rank_row[:, None] - rank_row[None, :]).astype(jnp.float32))
    return ((direct * rank_sign).astype(jnp.bfloat16), direct.astype(jnp.bfloat16))


def board_values(
    signed, direct, regret_rows, turn_strat, mine_reach, theirs, called, stakes, folding
):
    hand_count, columns = regret_rows.shape
    group_count = columns // 4
    river_strat = matching(regret_rows.reshape(hand_count, group_count, 2, 2))
    player_reach = (mine_reach[:, :, None, None] * turn_strat[:, :, :, None] * river_strat).astype(
        jnp.bfloat16
    )
    call_share = called.T.astype(jnp.float32).reshape(hand_count, group_count, 2)
    show_reach = jnp.stack(
        [
            jnp.broadcast_to(theirs[:, :, None], (hand_count, group_count, 2)),
            theirs[:, :, None] * call_share,
        ],
        axis=-1,
    ).astype(jnp.bfloat16)
    fold_reach = (theirs[:, :, None] * (1.0 - call_share)).astype(jnp.bfloat16)
    show_sums = jnp.dot(
        signed,
        jnp.concatenate(
            [show_reach.reshape(hand_count, columns), player_reach.reshape(hand_count, columns)],
            axis=1,
        ),
        preferred_element_type=jnp.float32,
    )
    fold_sums = jnp.dot(
        direct,
        jnp.concatenate(
            [
                fold_reach.reshape(hand_count, 2 * group_count),
                player_reach[:, :, :, 1].reshape(hand_count, 2 * group_count),
            ],
            axis=1,
        ),
        preferred_element_type=jnp.float32,
    )
    showdown = show_sums[:, :columns].reshape(hand_count, group_count, 2, 2)
    against = show_sums[:, columns:].reshape(hand_count, group_count, 2, 2)
    fold_total = fold_sums[:, : 2 * group_count].reshape(hand_count, group_count, 2)
    against_bet = fold_sums[:, 2 * group_count :].reshape(hand_count, group_count, 2)
    fold_gain = jnp.stack([jnp.zeros_like(fold_total), folding * fold_total], axis=-1)
    payoff = (stakes * showdown + fold_gain) / hand_count
    node_value = jnp.sum(river_strat * payoff, axis=-1)
    root_value = jnp.sum(turn_strat * node_value, axis=-1)
    river_inc = (payoff - node_value[..., None]).reshape(hand_count, columns)
    turn_inc = (node_value - root_value[..., None]).reshape(hand_count, 2 * group_count)
    check_value = stakes[..., 0] * against[..., 0]
    call_value = stakes[..., 1] * against[..., 1]
    fold_value = -folding * against_bet
    reply = jnp.sum(check_value + jnp.maximum(call_value, fold_value), axis=-1) / hand_count
    return (river_inc, turn_inc, reply.T)


def bucket_sums(count, values, buckets):
    inside = (buckets >= 0) & (buckets < count)
    target = jnp.where(inside, buckets, count)
    return jax.ops.segment_sum(values, target, num_segments=count + 1)[:count]


def per_device(
    river_regret,
    turn_regret,
    river_bucket,
    turn_bucket,
    ranks,
    turn_card,
    river_card,
    player_range,
    opp_range,
    call_prob,
    base_pot,
):
    turn_local, river_local, hand_count = river_bucket.shape
    group_count = player_range.shape[0]
    boards = turn_local * river_local
    river_total = river_local * lax.axis_size("river")
    first_np, second_np = np.triu_indices(CARDS, 1)
    hand_first = jnp.asarray(first_np.astype(np.int32))
    hand_second = jnp.asarray(second_np.astype(np.int32))
    mine_reach = player_range.T
    theirs = opp_range.T
    halves = 0.5 * base_pot
    stakes = halves[:, None, None] + jnp.array([[0.0, 2.0], [2.0, 4.0]], jnp.float32)
    folding = halves[:, None] + jnp.array([0.0, 2.0], jnp.float32)
    turn_table = lax.all_gather(turn_regret, ("turn", "river"), axis=0, tiled=True)
    river_table = lax.all_gather(river_regret, ("turn", "river"), axis=0, tiled=True)
    local_ids = river_bucket.reshape(boards, hand_count)
    turn_strat = matching(
        jnp.take(turn_table, turn_bucket.reshape(-1), axis=0).reshape(
            turn_local, hand_count, group_count, 2
        )
    )
    board_turn = jnp.repeat(turn_strat, river_local, axis=0)
    board_turn_card = jnp.repeat(turn_card, river_local)

    def one_board(board_items):
        bucket_row, strat, rank_row, turn_value, river_value, called = board_items
        signed, direct = board_payoffs(hand_first, hand_second, rank_row, turn_value, river_value)
        regret_rows = jnp.take(river_table, bucket_row, axis=0)
        return board_values(
            signed, direct, regret_rows, strat, mine_reach, theirs, called, stakes, folding
        )

    river_inc, turn_inc, replies = lax.map(
        one_board,
        (
            local_ids,
            board_turn,
            ranks.reshape(boards, hand_count),
            board_turn_card,
            river_card.reshape(boards),
            call_prob.reshape(boards, 2 * group_count, hand_count),
        ),
    )
    flat_inc = river_inc.reshape(boards * hand_count, 4 * group_count)
    flat_ids = local_ids.reshape(-1)
    owned = river_regret.shape[0]
    river_sums = lax.psum_scatter(
        bucket_sums(owned * lax.axis_size(("turn", "river")), flat_inc, flat_ids),
        ("turn", "river"),
        scatter_dimension=0,
        tiled=True,
    )
    new_river_regret = jnp.maximum(river_regret + river_sums / river_total, 0.0)
    turn_parts = jnp.sum(
        turn_inc.reshape(turn_local, river_local, hand_count, 2 * group_count), axis=1
    ).reshape(-1, 2 * group_count)
    turn_ids = turn_bucket.reshape(-1)
    turn_sums = lax.psum_scatter(
        bucket_sums(turn_regret.shape[0] * lax.axis_size(("turn", "river")), turn_parts, turn_ids),
        ("turn", "river"),
        scatter_dimension=0,
        tiled=True,
    )
    new_turn_regret = jnp.maximum(turn_regret + turn_sums / river_total, 0.0)
    reply_local = jnp.sum(replies.reshape(turn_local, river_local, group_count, hand_count), axis=1)
    br_value = lax.psum_scatter(reply_local, "river", scatter_dimension=1, tiled=True) / river_total
    return (new_river_regret, new_turn_regret, br_value)


def solution(mesh):
    placed = (
        P(("turn", "river"), None),
        P(("turn", "river"), None),
        P("turn", "river", None),
        P("turn", None),
        P("turn", "river", None),
        P("turn"),
        P("turn", "river"),
        P(),
        P(),
        P("turn", "river", None, None),
        P(),
    )
    return jax.shard_map(
        per_device,
        mesh=mesh,
        in_specs=placed,
        out_specs=(
            P(("turn", "river"), None),
            P(("turn", "river"), None),
            P("turn", "river", None),
        ),
        check_vma=False,
    )
```

profile of v0, /device:TPU:0, one launch (start us, length us, event | category | flops | bytes accessed | tf_op | source)
XLA Modules:
  0.0 1161.8 jit_solution(11895810817966483208)
XLA Ops:
  9.5 56.4 %all_gather.6 = f32[1024,128]{1,0:T(8,128)S(1)} all-gather(f32[8,128]{1,0:T(8,128)} %param.18), channel_id=1, replica_groups=mesh['turn'=8,'river'=16] {'turn','river'}, dimensions={0}, use_global_device_ids=true | all-gather | bytes 528384 | tf_op jit(solution)/shard_map/all_gather | solution.py:121
  65.8 5.6 gather_fusion.1
  80.8 5.5 copy.112
  92.1 584.2 %while.19 = (s32[]{:T(128)}, f32[6,1081,256]{2,1,0:T(8,128)}, f32[6,1081,128]{1,2,0:T(8,128)}, f32[6,64,1081]{2,1,0:T(8,128)}, f32[64,2,2]{0,1,2:T(2,128)S(1)}, ...) while((s32[]{:T(128)}, f32[6,1081,256]{2,1,0:T(8,128)}, ...), condition=%wide.wide.region_6.7_spmd.clone.clone.clone, body=%wide.wide.region_1.6_spmd.sunk.clone.clone.clone.sunk | while | flops 1838941184 | bytes 106584344 | solution.py:140
  92.7 6.9 gather_fusion
  135.1 5.0 fusion.72
  175.1 5.2 multiply_reduce_fusion.2
  189.1 6.9 gather_fusion
  231.2 5.0 fusion.72
  257.4 4.0 fusion.76
  271.2 5.3 multiply_reduce_fusion.2
  285.2 6.9 gather_fusion
  327.4 5.0 fusion.72
  367.6 5.1 multiply_reduce_fusion.2
  381.4 6.9 gather_fusion
  423.7 5.0 fusion.72
  449.8 4.0 fusion.76
  463.7 5.2 multiply_reduce_fusion.2
  477.7 6.9 gather_fusion
  519.8 5.0 fusion.72
  546.0 4.0 fusion.76
  559.8 5.3 multiply_reduce_fusion.2
  573.8 6.9 gather_fusion
  616.0 5.0 fusion.72
  656.2 5.1 multiply_reduce_fusion.2
  681.2 20.2 %scatter_custom_fusion.1 = f32[1025,128]{1,0:T(8,128)S(1)} fusion(s32[3243]{0:T(1024)} %get-tuple-element.371, f32[3243,128]{1,0:T(8,128)} %reshape.430, f32[]{:T(128)} %constant.59.clone.1), kind=kCustom, calls=%fused_computation.82 | custom fusion | flops 415104 | bytes 525312 | tf_op jit(solution)/shard_map/scatter-add | solution.py:93
  703.8 6.7 reshape.422
  710.5 37.4 %scatter_custom_fusion = f32[9217,256]{1,0:T(8,128)} fusion(s32[6486]{0:T(1024)S(1)} %fusion.43, f32[6486,256]{1,0:T(8,128)} %reshape.422, f32[]{:T(128)} %constant.59.clone.1), kind=kCustom, calls=%fused_computation.75 | custom fusion | flops 1660416 | bytes 9438720 | tf_op jit(solution)/shard_map/scatter-add | solution.py:93
  747.8 6.5 slice.100
  756.2 86.9 %all-reduce.6.cloned.1.call-done = f32[1024,128]{1,0:T(8,128)} async-done(((f32[1024,128]{1,0:T(8,128)}), f32[1024,128]{1,0:T(8,128)}) %all-reduce.6.cloned.1.call-update) | async-done | bytes 524304
  844.4 87.7 %all-reduce.8.cloned.1.call-done = f32[3,64,1081]{2,1,0:T(8,128)} async-done(((f32[3,64,1081]{2,1,0:T(8,128)}), f32[3,64,1081]{2,1,0:T(8,128)}) %all-reduce.8.cloned.1.call-update) | async-done | bytes 830224
  933.6 219.9 %reduce-scatter.3.cloned.1.call-done = f32[72,256]{1,0:T(8,128)} async-done(((f32[9216,256]{1,0:T(8,128)}), f32[72,256]{1,0:T(8,128)}) %reduce-scatter.3.cloned.1.call-update) | async-done | bytes 73744 | tf_op jit(solution)/shard_map/reduce_scatter | solution.py:154
  (701 shorter events, 488.3 us)
Async XLA Ops:
  7.2 82.3 %all-gather.2.cloned.1.call-start = ((), (), s32[]{:S(2)}) async-start(), calls=%async_computation.1 | async-start | bytes 9510912 | tf_op jit(solution)/shard_map/all_gather | solution.py:122
  7.9 835.2 %all-reduce.6.cloned.1.call-start = ((), (), s32[]{:S(2)}) async-start(), calls=%async_computation.3 | async-start | bytes 1048576
  80.7 5.5 copy-start.25
  80.7 5.6 copy-start.16
  80.7 5.6 copy-start.29
  80.7 6.3 copy-start.27
  80.7 7.0 copy-start.32
  80.7 7.0 copy-start.28
  92.1 7.5 copy-start.14
  92.1 7.5 copy-start.21
  161.2 4.8 copy-start.2
  175.1 6.0 copy-start.5
  188.5 7.5 copy-start.14
  188.5 7.5 copy-start.21
  271.2 6.2 copy-start.5
  284.6 7.5 copy-start.14
  284.6 7.5 copy-start.21
  367.6 5.9 copy-start.5
  380.7 7.5 copy-start.14
  380.8 7.5 copy-start.21
  463.7 6.0 copy-start.5
  477.1 7.5 copy-start.14
  477.1 7.5 copy-start.21
  559.8 6.2 copy-start.5
  573.2 7.5 copy-start.14
  573.3 7.5 copy-start.21
  656.2 5.9 copy-start.5
  681.2 21.2 %copy-start.7 = (f32[6,64,1081]{2,1,0:T(8,128)S(1)}, f32[6,64,1081]{2,1,0:T(8,128)}, u32[]{:S(2)}) copy-start(f32[6,64,1081]{2,1,0:T(8,128)} %get-tuple-element.636) | copy-start | bytes 4981252
  702.3 229.8 %all-reduce.8.cloned.1.call-start = ((), (), s32[]{:S(2)}) async-start(), calls=%async_computation.4 | async-start | bytes 1769472
  703.5 450.0 %reduce-scatter.3.cloned.1.call-start = ((), (), s32[]{:S(2)}) async-start(), calls=%async_computation.2 | async-start | bytes 9510912 | tf_op jit(solution)/shard_map/reduce_scatter | solution.py:154
  754.3 88.8 %copy-start.26 = (f32[8,128]{1,0:T(8,128)S(1)}, f32[8,128]{1,0:T(8,128)}, u32[]{:S(2)}) copy-start(f32[8,128]{1,0:T(8,128)} %param.18) | copy-start | bytes 12292
  754.3 399.2 %copy-start.9 = (f32[72,256]{1,0:T(8,128)S(1)}, f32[72,256]{1,0:T(8,128)}, u32[]{:S(2)}) copy-start(f32[72,256]{1,0:T(8,128)} %param.17) | copy-start | bytes 221188
  (101 other events, 169.3 us)
Sparse Core Ops, SparseCore 0:
  10.8 73.5 all-gather.1
  702.4 140.6 all-reduce.5
  846.8 85.1 all-reduce.7
  937.7 215.7 reduce-scatter.2
where the time goes:
time: 1170 us; the launch traced here: 1160 us
  waiting for transfers between devices  395 us (34%)
  local copies, waits for them, and re-layouts  364 us (31%)
  other arithmetic  271 us (23%)
  blocking collectives  56.4 us (5%)
  matrix products  48.6 us (4%)
  between operations  14.9 us (1%)
    reduce_scatter x1, waiting for transfers between devices, per_device(): lax.psum_scatter(bucket_sums(owned * lax.axis_size(('turn', 'river')), fl...  220 us
    unnamed x6, waiting for transfers between devices  175 us
    scatter-add x2, other arithmetic, bucket_sums(): return jax.ops.segment_sum(values, target, num_segments=count + 1)[:count]  57.6 us
    all_gather x1, blocking collectives, per_device(): lax.all_gather(turn_regret, ('turn', 'river'), axis=0, tiled=True)  56.4 us
    gather x18, local copies, waits for them, and re-layouts, one_board(): regret_rows = jnp.take(river_table, bucket_row, axis=0)  47.8 us
    mul x18, local copies, waits for them, and re-layouts, board_values(): mine_reach[:, :, None, None] * turn_strat[:, :, :, None] * river_strat  43.7 us
    div x18, local copies, waits for them, and re-layouts, matching(): return jnp.where(weight_sum > 0.0, positive / safe_sum, 0.5)  42.6 us
    reduce_sum x6, other arithmetic, board_values(): node_value = jnp.sum(river_strat * payoff, axis=-1)  31.2 us
  transfers between devices with their start and end apart: 4, of which 3 were waited for; matrix products, arithmetic and copies ran while one was open for 7% of the time, Pallas kernels for 0%

commit v1 on v0

v1 whole, which is shorter than its diff:
```python
import functools

import jax
import jax.numpy as jnp
import ml_dtypes
import numpy as np
from jax import lax
from jax.experimental import pallas as pl
from jax.experimental.pallas import tpu as pltpu
from jax.sharding import Mesh
from jax.sharding import PartitionSpec as P

CARDS = 47
H = CARDS * (CARDS - 1) // 2
HP = 1152
G = 64
C = 2 * G
BF = jnp.bfloat16
F32 = jnp.float32
NT = (((1,), (1,)), ((), ()))
NN = (((1,), (0,)), ((), ()))
TABLES = 4
VMEM_LIMIT = 60 * 1024 * 1024


def constants():
    first, second = np.triu_indices(CARDS, 1)
    share = (
        (first[:, None] == first[None, :])
        | (first[:, None] == second[None, :])
        | (second[:, None] == first[None, :])
        | (second[:, None] == second[None, :])
    )
    disjoint = np.zeros((HP, HP), np.float32)
    disjoint[:H, :H] = ~share
    rows = np.full((8, HP), -1, np.int32)
    rows[0, :H] = first
    rows[1, :H] = second
    cols = np.full((2, HP, 128), -1, np.int32)
    cols[0, :H] = first[:, None]
    cols[1, :H] = second[:, None]
    river_perm = np.zeros((4 * G, 4 * G), np.float32)
    turn_perm = np.zeros((2 * G, 2 * G), np.float32)
    for g in range(G):
        for a in range(2):
            turn_perm[g * 2 + a, a * G + g] = 1
            for b in range(2):
                river_perm[g * 4 + a * 2 + b, b * C + a * G + g] = 1
    return (
        disjoint.astype(ml_dtypes.bfloat16),
        rows,
        cols,
        river_perm.astype(ml_dtypes.bfloat16),
        turn_perm.astype(ml_dtypes.bfloat16),
    )


def parts(x, count):
    out = []
    for _ in range(count):
        piece = x.astype(BF)
        out.append(piece)
        x = x - piece.astype(F32)
    return out


def permuted(x, perm, dims):
    hi, mid, lo = [
        lax.dot_general(piece, perm, dims, preferred_element_type=F32) for piece in parts(x, 3)
    ]
    return (hi + mid) + lo


def first_share(pos0, pos1):
    total = pos0 + pos1
    some = total > 0.0
    safe = jnp.where(some, total, 1.0)
    return jnp.where(some, pos0 / safe, 0.5), jnp.where(some, pos1 / safe, 0.5)


def river_shares(permuted_regret):
    pos = jnp.maximum(permuted_regret, 0.0)
    return first_share(pos[:, :C], pos[:, C:])


def turn_shares(permuted_regret):
    pos = jnp.maximum(permuted_regret, 0.0)
    return first_share(pos, pltpu.roll(pos, G, 1))


def strategy_kernel(river_ref, turn_ref, rperm_ref, tperm_ref, out_ref):
    owned = river_ref.shape[0]
    share, _ = river_shares(permuted(river_ref[...], rperm_ref[...], NN))
    out_ref[:owned, :] = share
    tshare, _ = turn_shares(permuted(turn_ref[...], tperm_ref[...], NN))
    out_ref[owned:, :] = tshare


def update_kernel(
    scale, river_ref, turn_ref, rsum_ref, tsum_ref, rperm_ref, tperm_ref, river_out, turn_out
):
    rp = permuted(river_ref[...], rperm_ref[...], NN)
    s0, s1 = river_shares(rp)
    gain = rsum_ref[...] * scale
    new = jnp.maximum(rp + jnp.concatenate([s1 * gain, -(s0 * gain)], axis=1), 0.0)
    river_out[...] = permuted(new, rperm_ref[...], NT)
    tp = permuted(turn_ref[...], tperm_ref[...], NN)
    _, other = turn_shares(tp)
    new = jnp.maximum(tp + other * (tsum_ref[...] * scale), 0.0)
    turn_out[...] = permuted(new, tperm_ref[...], NT)


def stake_rows(pot_ref):
    pot = pot_ref[...]
    lane = lax.broadcasted_iota(jnp.int32, (1, C), 1)
    bet = 0.5 * jnp.concatenate([pot, pot], axis=1) + jnp.where(lane >= G, 2.0, 0.0)
    return bet * (1.0 / H), (bet + 2.0) * (1.0 / H)


def playable(first, second, turn_value, river_value):
    return (
        (first != turn_value)
        & (second != turn_value)
        & (first != river_value)
        & (second != river_value)
    )


def payoff_kernel(
    rivers,
    bucket_ref,
    tcard_ref,
    rcard_ref,
    rank_ref,
    call_ref,
    opp_ref,
    pot_ref,
    disjoint_ref,
    rows_ref,
    cols_ref,
    signed_ref,
    delta_ref,
    bet_ref,
    table_ref,
    rank_s,
    call_s,
    opp_s,
    show_s,
    fold_s,
    *extra,
):
    board = pl.program_id(0)
    t, r = board // rivers, board % rivers
    tables = (table_ref,) + extra

    @pl.when(board == 0)
    def _():
        rank_s[...] = jnp.zeros_like(rank_s)
        call_s[...] = jnp.zeros_like(call_s)
        opp_s[...] = jnp.zeros_like(opp_s)
        opp_s[:, :H] = opp_ref[...]
        for table in tables:
            table[...] = jnp.zeros_like(table)

    turn_value, river_value = tcard_ref[t], rcard_ref[t, r]
    row_ok = playable(rows_ref[0:1, :], rows_ref[1:2, :], turn_value, river_value)
    col_ok = playable(cols_ref[0], cols_ref[1], turn_value, river_value)

    rank_s[0:1, :H] = rank_ref[0, pl.ds(r, 1), :]
    rank_row = rank_s[0:1, :].astype(F32)
    rank_col = jnp.transpose(jnp.broadcast_to(rank_row, (128, HP)))
    for j in range(HP // 128):
        lanes = slice(j * 128, (j + 1) * 128)
        sign = jnp.clip(rank_col - rank_row[:, lanes], -1.0, 1.0)
        signed_ref[0, :, lanes] = sign.astype(BF) * disjoint_ref[:, lanes]

    theirs = jnp.where(row_ok, opp_s[...], 0.0)
    for j in range(HP // 128):
        lanes = slice(j * 128, (j + 1) * 128)
        width = min(128, H - j * 128)
        call_s[j, :, :width] = call_ref[0, :, j * 128 : j * 128 + width].astype(F32)
        theirs_j = theirs[:, lanes]
        for a in range(2):
            called = call_s[j, pl.ds(a, G, stride=2), :]
            rows = slice(a * G, (a + 1) * G)
            show_s[rows, lanes] = theirs_j.astype(BF)
            show_s[C + a * G : C + (a + 1) * G, lanes] = (theirs_j * called).astype(BF)
            fold_s[rows, lanes] = (theirs_j * (1.0 - called)).astype(BF)

    show = lax.dot_general(signed_ref[0], show_s[...], NT, preferred_element_type=F32)
    fold = lax.dot_general(disjoint_ref[...], fold_s[...], NT, preferred_element_type=F32)
    low, high = stake_rows(pot_ref)
    bet = high * show[:, C:] + low * fold
    bet_ref[0] = jnp.where(col_ok, bet, 0.0)
    delta_ref[0] = jnp.where(col_ok, low * show[:, :C] - bet, 0.0)

    def add_row(h, table):
        k = bucket_ref[t, r, h]
        table[pl.ds(k, 1), :] += delta_ref[0, pl.ds(h, 1), :]

    step = 4 * TABLES

    def add_rows(i, _):
        for j in range(step):
            add_row(i * step + j, tables[j % TABLES])
        return 0

    lax.fori_loop(0, H // step, add_rows, 0)
    for h in range(H // step * step, H):
        add_row(h, tables[h % TABLES])

    @pl.when(board == pl.num_programs(0) - 1)
    def _():
        total = table_ref[...]
        for table in extra:
            total = total + table[...]
        table_ref[...] = total


def reply_kernel(
    rivers,
    river_total,
    bucket_ref,
    tbucket_ref,
    tcard_ref,
    rcard_ref,
    table_ref,
    trow_ref,
    signed_ref,
    delta_ref,
    bet_ref,
    mine_ref,
    pot_ref,
    disjoint_ref,
    cols_ref,
    br_ref,
    gain_ref,
    mine_s,
    turn_s,
    river_s,
    reach_s,
    reply_s,
    node_s,
    trow_s,
    wide_s,
):
    board = pl.program_id(0)
    t, r = board // rivers, board % rivers

    @pl.when(board == 0)
    def _():
        wide_s[...] = jnp.zeros_like(wide_s)
        wide_s[:G, :H] = mine_ref[...]
        wide_s[G:, :H] = mine_ref[...]
        mine_s[...] = jnp.transpose(wide_s[...])
        reply_s[...] = jnp.zeros_like(reply_s)
        node_s[...] = jnp.zeros_like(node_s)
        turn_s[...] = jnp.zeros_like(turn_s)
        river_s[...] = jnp.zeros_like(river_s)
        trow_s[...] = jnp.full_like(trow_s, -1)
        gain_ref[...] = jnp.zeros_like(gain_ref)

    step = 16

    def gather(dst, index):
        def rows(i, _):
            for j in range(step):
                h = i * step + j
                dst[pl.ds(h, 1), :] = table_ref[pl.ds(index(h), 1), :]
            return 0

        lax.fori_loop(0, H // step, rows, 0)
        for h in range(H // step * step, H):
            dst[pl.ds(h, 1), :] = table_ref[pl.ds(index(h), 1), :]

    @pl.when(r == 0)
    def _():
        gather(turn_s, lambda h: tbucket_ref[t, h])

    gather(river_s, lambda h: bucket_ref[t, r, h])

    turn_value, river_value = tcard_ref[t], rcard_ref[t, r]
    col_ok = playable(cols_ref[0], cols_ref[1], turn_value, river_value)
    first = river_s[...]
    reach = jnp.where(col_ok, mine_s[...] * turn_s[...], 0.0)
    reach_s[:, :C] = (reach * first).astype(BF)
    reach_s[:, C:] = (reach * (1.0 - first)).astype(BF)
    against = lax.dot_general(signed_ref[0], reach_s[...], NN, preferred_element_type=F32)
    against_bet = lax.dot_general(
        disjoint_ref[...], reach_s[:, C:], NN, preferred_element_type=F32
    )
    low, high = stake_rows(pot_ref)
    reply = low * against[:, :C] + jnp.maximum(high * against[:, C:], -(low * against_bet))
    reply = jnp.where(col_ok, reply, 0.0)
    node = bet_ref[0] + first * delta_ref[0]

    reply_s[...] = jnp.where(r == 0, reply, reply_s[...] + reply)
    node_s[...] = jnp.where(r == 0, node, node_s[...] + node)

    @pl.when(r == rivers - 1)
    def _():
        flat = jnp.transpose(reply_s[...])
        br_ref[0] = ((flat[:G] + flat[G:]) * (1.0 / river_total))[:, :H]
        nodes = node_s[...]
        diff = nodes - pltpu.roll(nodes, G, 1)
        hi, lo = parts(diff, 2)
        trow_s[0:1, :H] = trow_ref[pl.ds(t, 1), :]
        ids = lax.broadcasted_iota(jnp.int32, (gain_ref.shape[0], HP), 0)
        hot = jnp.where(ids == trow_s[0:1, :], 1.0, 0.0).astype(BF)
        gain_ref[...] += lax.dot_general(hot, hi, NN, preferred_element_type=F32) + lax.dot_general(
            hot, lo, NN, preferred_element_type=F32
        )


def per_device(
    river_regret,
    turn_regret,
    river_bucket,
    turn_bucket,
    ranks,
    turn_card,
    river_card,
    player_range,
    opp_range,
    call_prob,
    base_pot,
):
    turns, rivers, _ = river_bucket.shape
    boards = turns * rivers
    devices = lax.axis_size(("turn", "river"))
    river_total = rivers * lax.axis_size("river")
    owned, towned = river_regret.shape[0], turn_regret.shape[0]
    buckets, tbuckets = owned * devices, towned * devices
    disjoint, rows, cols, rperm, tperm = constants()
    params = pltpu.CompilerParams(vmem_limit_bytes=VMEM_LIMIT)
    pot = base_pot.reshape(1, G)
    calls = call_prob.reshape(boards, C, H)
    rest = owned + towned

    with jax.named_scope("strategies"):
        strategies = pl.pallas_call(
            strategy_kernel,
            out_shape=jax.ShapeDtypeStruct((rest, C), F32),
            compiler_params=params,
            name="strategies",
        )(river_regret, turn_regret, rperm, tperm)
        table = lax.all_gather(strategies, ("turn", "river"), axis=0, tiled=True)

    def whole(shape):
        return pl.BlockSpec(shape, lambda i, *_: (0,) * len(shape))

    def per_board(shape):
        return pl.BlockSpec((1,) + shape, lambda i, *_: (i,) + (0,) * len(shape))

    def per_turn(shape):
        return pl.BlockSpec((1,) + shape, lambda i, *_: (i // rivers,) + (0,) * len(shape))

    with jax.named_scope("payoffs"):
        signed, delta, bet, sums = pl.pallas_call(
            functools.partial(payoff_kernel, rivers),
            grid_spec=pltpu.PrefetchScalarGridSpec(
                num_scalar_prefetch=3,
                grid=(boards,),
                in_specs=[
                    per_turn((rivers, H)),
                    per_board((C, H)),
                    whole((G, H)),
                    whole((1, G)),
                    whole((HP, HP)),
                    whole((8, HP)),
                    whole((2, HP, 128)),
                ],
                out_specs=[
                    per_board((HP, HP)),
                    per_board((HP, C)),
                    per_board((HP, C)),
                    whole((buckets, C)),
                ],
                scratch_shapes=[
                    pltpu.VMEM((8, HP), jnp.int32),
                    pltpu.VMEM((HP // 128, C, 128), F32),
                    pltpu.VMEM((G, HP), F32),
                    pltpu.VMEM((2 * C, HP), BF),
                    pltpu.VMEM((C, HP), BF),
                ]
                + [pltpu.VMEM((buckets, C), F32)] * (TABLES - 1),
            ),
            out_shape=[
                jax.ShapeDtypeStruct((boards, HP, HP), BF),
                jax.ShapeDtypeStruct((boards, HP, C), F32),
                jax.ShapeDtypeStruct((boards, HP, C), F32),
                jax.ShapeDtypeStruct((buckets, C), F32),
            ],
            compiler_params=params,
            name="payoffs",
        )(
            river_bucket,
            turn_card,
            river_card,
            ranks,
            calls,
            opp_range,
            pot,
            disjoint,
            rows,
            cols,
        )

    with jax.named_scope("river_sums"):
        river_sums = lax.psum_scatter(sums, ("turn", "river"), scatter_dimension=0, tiled=True)

    river_at = river_bucket // owned * rest + river_bucket % owned
    turn_at = turn_bucket // towned * rest + owned + turn_bucket % towned
    with jax.named_scope("replies"):
        replies, gains = pl.pallas_call(
            functools.partial(reply_kernel, rivers, river_total),
            grid_spec=pltpu.PrefetchScalarGridSpec(
                num_scalar_prefetch=4,
                grid=(boards,),
                in_specs=[
                    whole((rest * devices, C)),
                    whole((turns, H)),
                    per_board((HP, HP)),
                    per_board((HP, C)),
                    per_board((HP, C)),
                    whole((G, H)),
                    whole((1, G)),
                    whole((HP, HP)),
                    whole((2, HP, 128)),
                ],
                out_specs=[
                    per_turn((G, H)),
                    whole((tbuckets, C)),
                ],
                scratch_shapes=[
                    pltpu.VMEM((HP, C), F32),
                    pltpu.VMEM((HP, C), F32),
                    pltpu.VMEM((HP, C), F32),
                    pltpu.VMEM((HP, 2 * C), BF),
                    pltpu.VMEM((HP, C), F32),
                    pltpu.VMEM((HP, C), F32),
                    pltpu.VMEM((8, HP), jnp.int32),
                    pltpu.VMEM((C, HP), F32),
                ],
            ),
            out_shape=[
                jax.ShapeDtypeStruct((turns, G, H), F32),
                jax.ShapeDtypeStruct((tbuckets, C), F32),
            ],
            compiler_params=params,
            name="replies",
        )(
            river_at,
            turn_at,
            turn_card,
            river_card,
            table,
            turn_bucket,
            signed,
            delta,
            bet,
            player_range,
            pot,
            disjoint,
            cols,
        )

    with jax.named_scope("br_value"):
        br_value = lax.psum_scatter(replies, "river", scatter_dimension=1, tiled=True)
    with jax.named_scope("turn_sums"):
        turn_sums = lax.psum_scatter(gains, ("turn", "river"), scatter_dimension=0, tiled=True)

    with jax.named_scope("update"):
        new_river, new_turn = pl.pallas_call(
            functools.partial(update_kernel, 1.0 / river_total),
            out_shape=[
                jax.ShapeDtypeStruct(river_regret.shape, F32),
                jax.ShapeDtypeStruct(turn_regret.shape, F32),
            ],
            compiler_params=params,
            name="update",
        )(river_regret, turn_regret, river_sums, turn_sums, rperm, tperm)
    return new_river, new_turn, br_value


def solution(mesh):
    both = ("turn", "river")
    placed = (
        P(both, None),
        P(both, None),
        P("turn", "river", None),
        P("turn", None),
        P("turn", "river", None),
        P("turn"),
        P("turn", "river"),
        P(),
        P(),
        P("turn", "river", None, None),
        P(),
    )
    return jax.shard_map(
        per_device,
        mesh=mesh,
        in_specs=placed,
        out_specs=(P(both, None), P(both, None), P("turn", "river", None)),
        check_vma=False,
    )
```

time: 1170 us -> 588 us (0.50)
  local copies, waits for them, and re-layouts: 364 us -> 11.3 us
  other arithmetic: 271 us -> 1.37 us
  Pallas kernels: 0 us -> 101 us
  waiting for transfers between devices: 395 us -> 460 us
  blocking collectives: 56.4 us -> 0 us
  matrix products: 48.6 us -> 0 us
    unnamed x6 -> x7, waiting for transfers between devices: 175 us -> 441 us
    reduce_scatter x1 -> x0, waiting for transfers between devices: 220 us -> none  [per_device(): lax.psum_scatter(bucket_sums(owned * lax.axis_size(('turn', 'river')), fl...]
    pallas_call x0 -> x4, Pallas kernels: none -> 101 us  [the longest x1 52.1 us: per_device(): pl.pallas_call(functools.partial(reply_kernel, rivers, river_total), grid...]
    reduce_sum x21 -> x0, other arithmetic: 71.6 us -> none  [the longest x6 31.2 us: board_values(): node_value = jnp.sum(river_strat * payoff, axis=-1)]
    mul x54 -> x0, local copies, waits for them, and re-layouts: 58.6 us -> none  [the longest x18 43.7 us: board_values(): mine_reach[:, :, None, None] * turn_strat[:, :, :, None] * river_strat]
    gather x21 -> x0, local copies, waits for them, and re-layouts: 58.3 us -> none  [the longest x18 47.8 us: one_board(): regret_rows = jnp.take(river_table, bucket_row, axis=0)]
    scatter-add x2 -> x0, other arithmetic: 57.6 us -> none  [bucket_sums(): return jax.ops.segment_sum(values, target, num_segments=count + 1)[:count]]
    all_gather x1 -> x0, blocking collectives: 56.4 us -> none  [per_device(): lax.all_gather(turn_regret, ('turn', 'river'), axis=0, tiled=True)]
  transfers between devices with their start and end apart: 4 -> 4, of which waited for: 3 -> 4; matrix products, arithmetic and copies ran while one was open for 7% -> 2% of each run, Pallas kernels for 0% -> 8%
where the time goes in v1:
time: 588 us
  waiting for transfers between devices  460 us (78%)
  Pallas kernels  101 us (17%)
  between operations  14.4 us (2%)
  local copies, waits for them, and re-layouts  11.3 us (2%)
    unnamed x7, waiting for transfers between devices  441 us
    pallas_call x1, Pallas kernels, per_device(): pl.pallas_call(functools.partial(reply_kernel, rivers, river_total), grid...  52.1 us
    pallas_call x1, Pallas kernels, per_device(): pl.pallas_call(functools.partial(payoff_kernel, rivers), grid_spec=pltpu....  44.7 us
    all_gather x1, waiting for transfers between devices, per_device(): table = lax.all_gather(strategies, ('turn', 'river'), axis=0, tiled=True)  18.3 us
  transfers between devices with their start and end apart: 4, of which 4 were waited for; matrix products, arithmetic and copies ran while one was open for 2% of the time, Pallas kernels for 8%

profile of v1, /device:TPU:0, one launch (start us, length us, event | category | flops | bytes accessed | tf_op | source)
XLA Modules:
  0.0 587.9 jit_solution(975134677591020604)
XLA Ops:
  7.2 0.0 all-gather.2.cloned.1.call-start
  7.2 1.9 strategies.1
  9.1 0.0 all-gather.2.cloned.1.call-update
  9.1 0.0 all-reduce.6.cloned.1.call-start
  9.2 1.3 copy.23.rcard_ref
  10.5 6.6 %copy.22 = bf16[3,2,128,1081]{3,2,1,0:T(8,128)(2,1)} copy(bf16[3,2,128,1081]{2,1,3,0:T(2,128)(2,1)} %param.25) | data formatting | bytes 3320832 | tf_op args[9]
  17.1 0.0 copy-start.1
  17.1 0.0 copy-start
  17.1 44.7 %payoffs.1 = (bf16[6,1152,1152]{2,1,0:T(8,128)(2,1)}, f32[6,1152,128]{2,1,0:T(8,128)}, f32[6,1152,128]{2,1,0:T(8,128)}, f32[9216,128]{1,0:T(8,128)}) custom-call(s32[3,2,1081]{2,1,0:T(2,128)} %bucket_ref.1, s32[3]{0:T(128)} %tcard_ref.3, s32[3,2]{1,0:T(4,128)} %copy.23.rcard_ref, s32[3,2,1081]{2,1,0:T(2,128)} %rank_ref.1, bf16[6,128,1081]{2,1,0:T(8,128)(2,1)} %bitcast.5, ...), custom_call_target="tpu_custom_call" | custom-call | tf_op jit(solution)/shard_map/payoffs/payoffs/pallas_call | solution.py:359
  61.8 0.0 copy-done.1
  61.8 0.6 fusion.3.tbucket_ref
  62.5 0.0 copy-done
  62.5 0.7 fusion.bucket_ref
  63.2 18.3 %all-gather.2.cloned.1.call-done.table_ref = f32[10240,128]{1,0:T(8,128)} async-done(((f32[80,128]{1,0:T(8,128)}), f32[10240,128]{1,0:T(8,128)}) %all-gather.2.cloned.1.call-update) | async-done | bytes 5242896 | tf_op jit(solution)/shard_map/strategies/all_gather | solution.py:347
  81.5 52.1 %replies.1 = (f32[3,64,1081]{2,1,0:T(8,128)}, f32[1024,128]{1,0:T(8,128)}) custom-call(s32[3,2,1081]{2,1,0:T(2,128)} %fusion.bucket_ref, s32[3,1081]{1,0:T(4,128)} %fusion.3.tbucket_ref, s32[3]{0:T(128)} %tcard_ref.3, s32[3,2]{1,0:T(4,128)} %copy.23.rcard_ref, f32[10240,128]{1,0:T(8,128)} %all-gather.2.cloned.1.call-done.table_ref, s32[3,1081]{1,0:T(4,128)} %trow_ref.1, ...), custom_call_target="tpu_custom_call" | custom-call | tf_op jit(solution)/shard_map/replies/replies/pallas_call | solution.py:415
  133.7 0.0 copy-start.2
  133.7 0.0 all-reduce.6.cloned.1.call-update
  133.7 0.0 reduce-scatter.5.cloned.1.call-start
  133.7 0.7 reduce-scatter.5.cloned.1.call-update
  134.4 0.0 all-reduce.8.cloned.1.call-start
  134.5 0.5 all-reduce.8.cloned.1.call-update
  135.0 0.0 copy-done.2
  135.0 0.6 dynamic-slice.2
  136.3 139.8 %all-reduce.6.cloned.1.call-done = f32[1024,128]{1,0:T(8,128)} async-done(((f32[1024,128]{1,0:T(8,128)}), f32[1024,128]{1,0:T(8,128)}) %all-reduce.6.cloned.1.call-update) | async-done | bytes 524304
  276.1 1.3 constant_dynamic-slice_fusion.tsum_ref
  277.3 215.6 %reduce-scatter.5.cloned.1.call-done.rsum_ref = f32[72,128]{1,0:T(8,128)} async-done(((f32[9216,128]{1,0:T(8,128)}), f32[72,128]{1,0:T(8,128)}) %reduce-scatter.5.cloned.1.call-update) | async-done | bytes 36880
  493.0 2.1 update.1
  495.1 84.8 %all-reduce.8.cloned.1.call-done = f32[3,64,1081]{2,1,0:T(8,128)} async-done(((f32[3,64,1081]{2,1,0:T(8,128)}), f32[3,64,1081]{2,1,0:T(8,128)}) %all-reduce.8.cloned.1.call-update) | async-done | bytes 830224
  579.9 1.5 constant_dynamic-slice_fusion.1
Async XLA Ops:
  7.2 74.4 %all-gather.2.cloned.1.call-start = ((), (), s32[]{:S(2)}) async-start(), calls=%async_computation.1 | async-start | bytes 5283840 | tf_op jit(solution)/shard_map/strategies/all_gather | solution.py:347
  9.1 266.9 %all-reduce.6.cloned.1.call-start = ((), (), s32[]{:S(2)}) async-start(), calls=%async_computation.2 | async-start | bytes 1048576
  17.1 44.7 %copy-start.1 = (s32[3,1081]{1,0:T(4,128)S(1)}, s32[3,1081]{1,0:T(4,128)}, u32[]{:S(2)}) copy-start(s32[3,1081]{1,0:T(4,128)} %trow_ref.1) | copy-start | bytes 38920
  17.1 45.4 %copy-start = (s32[3,2,1081]{2,1,0:T(2,128)S(1)}, s32[3,2,1081]{2,1,0:T(2,128)}, u32[]{:S(2)}) copy-start(s32[3,2,1081]{2,1,0:T(2,128)} %bucket_ref.1) | copy-start | bytes 77836
  133.7 1.4 copy-start.2
  133.7 359.3 %reduce-scatter.5.cloned.1.call-start = ((), (), s32[]{:S(2)}) async-start(), calls=%async_computation.4 | async-start | bytes 4755456
  134.4 445.4 %all-reduce.8.cloned.1.call-start = ((), (), s32[]{:S(2)}) async-start(), calls=%async_computation.3 | async-start | bytes 1769472
Sparse Core Ops, SparseCore 0:
  11.5 69.9 all-gather.1
  133.8 142.1 all-reduce.5
  281.7 211.1 reduce-scatter.4
  496.5 83.3 all-reduce.7

commit v2 on v1

v2 whole, which is shorter than its diff:
```python
import functools

import jax
import jax.numpy as jnp
import ml_dtypes
import numpy as np
from jax import lax
from jax.experimental import pallas as pl
from jax.experimental.pallas import tpu as pltpu
from jax.sharding import Mesh
from jax.sharding import PartitionSpec as P

CARDS = 47
H = CARDS * (CARDS - 1) // 2
HP = 1152
G = 64
C = 2 * G
BF = jnp.bfloat16
F32 = jnp.float32
NT = (((1,), (1,)), ((), ()))
NN = (((1,), (0,)), ((), ()))
TABLES = 6
UNROLL = 47
INDEX_ROW = 2048
AXES = ("x", "core", "z", "y")
VMEM_LIMIT = 60 * 1024 * 1024


def constants():
    first, second = np.triu_indices(CARDS, 1)
    share = (
        (first[:, None] == first[None, :])
        | (first[:, None] == second[None, :])
        | (second[:, None] == first[None, :])
        | (second[:, None] == second[None, :])
    )
    disjoint = np.zeros((HP, HP), np.float32)
    disjoint[:H, :H] = ~share
    cols = np.full((2, HP, 128), -1, np.int32)
    cols[0, :H] = first[:, None]
    cols[1, :H] = second[:, None]
    holds = np.zeros((64, HP), np.float32)
    holds[first, np.arange(H)] = 1
    holds[second, np.arange(H)] = 1
    holds[CARDS, :H] = 1
    spread_out = np.zeros((HP, 64), np.float32)
    spread_out[:H, :CARDS] = -holds[:CARDS, :H].T
    spread_out[:H, CARDS] = 1
    spread_out = np.concatenate([spread_out] * 3 + [np.zeros_like(spread_out)], axis=1)
    river_perm = np.zeros((4 * G, 4 * G), np.float32)
    turn_perm = np.zeros((2 * G, 2 * G), np.float32)
    for g in range(G):
        for a in range(2):
            turn_perm[g * 2 + a, a * G + g] = 1
            for b in range(2):
                river_perm[g * 4 + a * 2 + b, b * C + a * G + g] = 1
    halves = [m.astype(ml_dtypes.bfloat16) for m in (disjoint, holds, spread_out, river_perm, turn_perm)]
    return halves + [cols]


def others(x, holds_ref, out_of_ref):
    sums = lax.dot_general(holds_ref[...], x, NN, preferred_element_type=F32)
    pieces = parts(sums, 3)
    pieces = jnp.concatenate(pieces + [jnp.zeros_like(pieces[0])], axis=0)
    return x.astype(F32) + lax.dot_general(
        out_of_ref[...], pieces, NN, preferred_element_type=F32
    )


def parts(x, count):
    out = []
    for _ in range(count):
        piece = x.astype(BF)
        out.append(piece)
        x = x - piece.astype(F32)
    return out


def permuted(x, perm, dims):
    hi, mid, lo = [
        lax.dot_general(piece, perm, dims, preferred_element_type=F32) for piece in parts(x, 3)
    ]
    return (hi + mid) + lo


def first_share(pos0, pos1):
    total = pos0 + pos1
    some = total > 0.0
    safe = jnp.where(some, total, 1.0)
    return jnp.where(some, pos0 / safe, 0.5), jnp.where(some, pos1 / safe, 0.5)


def river_shares(permuted_regret):
    pos = jnp.maximum(permuted_regret, 0.0)
    return first_share(pos[:, :C], pos[:, C:])


def turn_shares(permuted_regret):
    pos = jnp.maximum(permuted_regret, 0.0)
    return first_share(pos, pltpu.roll(pos, G, 1))


def strategy_kernel(
    place_ref,
    river_ref,
    turn_ref,
    rperm_ref,
    tperm_ref,
    bucket_ref,
    tbucket_ref,
    out_ref,
    index_ref,
    at_ref,
    tat_ref,
):
    owned, towned = river_ref.shape[0], turn_ref.shape[0]
    rest = owned + towned
    share, _ = river_shares(permuted(river_ref[...], rperm_ref[...], NN))
    out_ref[:owned, :] = share
    tshare, _ = turn_shares(permuted(turn_ref[...], tperm_ref[...], NN))
    out_ref[owned:, :] = tshare

    turns, rivers, _ = bucket_ref.shape
    index_ref[...] = jnp.zeros_like(index_ref)
    tat_ref[...] = jnp.zeros_like(tat_ref)
    for j in range(HP // 128):
        width = min(128, H - j * 128)
        lanes = slice(j * 128, j * 128 + width)
        for t in range(turns):
            tat_ref[t, j : j + 1, :width] = tbucket_ref[t : t + 1, lanes]
            for r in range(rivers):
                index_ref[t * rivers + r, j : j + 1, :width] = bucket_ref[t, r : r + 1, lanes]

    x, core, z, y = (place_ref[i] for i in range(4))

    def placed(bucket, count, offset):
        owner = ((bucket.astype(F32) + 0.5) * (1.0 / count)).astype(jnp.int32)
        row = bucket - owner * count
        down_y = (y - owner) & 3
        down_z = (z - (owner >> 2)) & 3
        other = (core - (owner >> 4)) & 1
        down_x = (x - (owner >> 5)) & 3
        slot = ((other * 4 + down_x) * 4 + down_z) * 4 + down_y
        return slot * rest + offset + row

    at_ref[...] = placed(index_ref[...], owned, 0)
    tat_ref[...] = placed(tat_ref[...], towned, owned)


def update_kernel(
    scale, each, came_ref, river_ref, turn_ref, rperm_ref, tperm_ref, river_out, turn_out, br_out
):
    turns = br_out.shape[0]
    blocks = HP // 128
    came = came_ref[0]
    for source in range(1, came_ref.shape[0]):
        came = came + came_ref[source]
    for t in range(turns):
        for j in range(blocks):
            row = (t * blocks + j) * each
            width = min(128, H - j * 128)
            br_out[t, :, j * 128 : j * 128 + width] = came[row : row + each, :width]
    at = turns * blocks * each
    rsum = came[at + 4 : at + 4 + river_ref.shape[0]]
    tsum = came[at : at + 4]
    rp = permuted(river_ref[...], rperm_ref[...], NN)
    s0, s1 = river_shares(rp)
    gain = rsum * scale
    new = jnp.maximum(rp + jnp.concatenate([s1 * gain, -(s0 * gain)], axis=1), 0.0)
    river_out[...] = permuted(new, rperm_ref[...], NT)
    tp = permuted(turn_ref[...], tperm_ref[...], NN)
    _, other = turn_shares(tp)
    lane = lax.broadcasted_iota(jnp.int32, tsum.shape, 1)
    swapped = pltpu.roll(tsum, G, 1)
    low = jnp.where(lane < G, tsum, -swapped)
    high = jnp.where(lane < G, swapped, -tsum)
    gain = jnp.concatenate([low, high], axis=0) * scale
    turn_out[...] = permuted(jnp.maximum(tp + other * gain, 0.0), tperm_ref[...], NT)


def stake_rows(pot_ref):
    pot = pot_ref[...]
    lane = lax.broadcasted_iota(jnp.int32, (1, C), 1)
    bet = 0.5 * jnp.concatenate([pot, pot], axis=1) + jnp.where(lane >= G, 2.0, 0.0)
    return bet * (1.0 / H), (bet + 2.0) * (1.0 / H)


def playable(first, second, turn_value, river_value):
    return (
        (first != turn_value)
        & (second != turn_value)
        & (first != river_value)
        & (second != river_value)
    )


def for_each_hand(index_ref, board, body):
    base = board * INDEX_ROW

    def some(i, _):
        for j in range(UNROLL):
            h = i * UNROLL + j
            body(h, index_ref[base + h], j)
        return 0

    lax.fori_loop(0, H // UNROLL, some, 0)


def widen(wide_s, narrow_ref, out_s):
    wide_s[...] = jnp.zeros_like(wide_s)
    wide_s[:G, :H] = narrow_ref[...]
    wide_s[G:, :H] = narrow_ref[...]
    out_s[...] = jnp.transpose(wide_s[...])


def payoff_kernel(
    rivers,
    tcard_ref,
    rcard_ref,
    rank_ref,
    call_ref,
    opp_ref,
    pot_ref,
    disjoint_ref,
    holds_ref,
    out_of_ref,
    tperm_ref,
    cols_ref,
    signed_ref,
    delta_ref,
    bet_ref,
    rank_s,
    call_s,
    wide_s,
    opp_s,
    show_s,
):
    board = pl.program_id(0)
    t, r = board // rivers, board % rivers

    @pl.when(board == 0)
    def _():
        rank_s[...] = jnp.zeros_like(rank_s)
        call_s[rivers * H :, :] = jnp.zeros((rivers * (HP - H), C), F32)
        widen(wide_s, opp_ref, opp_s)

    @pl.when(r == 0)
    def _():
        called = call_ref[0].reshape(rivers * H, C)
        call_s[: rivers * H, :] = lax.dot_general(
            called, tperm_ref[...], NN, preferred_element_type=F32
        )

    col_ok = playable(cols_ref[0], cols_ref[1], tcard_ref[t], rcard_ref[r, t])
    rank_s[0:1, :H] = rank_ref[0, pl.ds(r, 1), :]
    rank_row = rank_s[0:1, :].astype(F32)
    rank_col = jnp.transpose(jnp.broadcast_to(rank_row, (128, HP)))
    for j in range(HP // 128):
        lanes = slice(j * 128, (j + 1) * 128)
        sign = jnp.clip(rank_col - rank_row[:, lanes], -1.0, 1.0)
        signed_ref[0, :, lanes] = sign.astype(BF) * disjoint_ref[:, lanes]

    called = call_s[pl.ds(r, HP, stride=rivers), :]
    theirs = jnp.where(col_ok, opp_s[...], 0.0)
    show_s[:, :C] = theirs.astype(BF)
    show_s[:, C:] = (theirs * called).astype(BF)
    show = lax.dot_general(signed_ref[0], show_s[...], NN, preferred_element_type=F32)
    fold = others((theirs * (1.0 - called)).astype(BF), holds_ref, out_of_ref)
    low, high = stake_rows(pot_ref)
    bet = high * show[:, C:] + low * fold
    bet_ref[0] = jnp.where(col_ok, bet, 0.0)
    delta_ref[0] = jnp.where(col_ok, low * show[:, :C] - bet, 0.0)


def sum_kernel(index_ref, place_ref, delta_ref, mine_ref, theirs_ref, *tables):
    board = pl.program_id(0)

    @pl.when(board == 0)
    def _():
        for table in tables:
            table[...] = jnp.zeros_like(table)

    def add_row(h, k, j):
        table = tables[j % TABLES]
        table[pl.ds(k, 1), :] += delta_ref[0, pl.ds(h, 1), :]

    for_each_hand(index_ref, board, add_row)

    @pl.when(board == pl.num_programs(0) - 1)
    def _():
        x, core = place_ref[0], place_ref[1]
        half = mine_ref.shape[1] // 2
        order = ((2, 0), (1, 1), (2, 1), (3, 0), (1, 0), (3, 1), (0, 0), (0, 1))
        for i, (s, part) in enumerate(order):
            for out_ref, c in ((mine_ref, core), (theirs_ref, 1 - core)):
                at = pl.multiple_of((((x + s) & 3) * 4 + c * 2 + part) * half, 8)
                total = tables[0][pl.ds(at, half), :]
                for table in tables[1:]:
                    total = total + table[pl.ds(at, half), :]
                out_ref[i // 2, i % 2 * half : (i % 2 + 1) * half, :] = total


def node_kernel(
    rivers,
    pieces,
    bucket_ref,
    tbucket_ref,
    trow_ref,
    delta_ref,
    bet_ref,
    *refs,
):
    piece_refs, (first_ref, strat_ref, gain_ref, table_s, node_s, trow_s, sem) = (
        refs[:pieces],
        refs[pieces:],
    )
    board = pl.program_id(0)
    t, r = board // rivers, board % rivers

    @pl.when(board == 0)
    def _():
        at, copies = 0, []
        for i, piece in enumerate(piece_refs):
            rows = piece.shape[0]
            copies.append(pltpu.make_async_copy(piece, table_s.at[pl.ds(at, rows)], sem.at[i]))
            copies[-1].start()
            at += rows
        node_s[...] = jnp.zeros_like(node_s)
        trow_s[...] = jnp.full_like(trow_s, -1)
        gain_ref[...] = jnp.zeros_like(gain_ref)
        for copy in copies:
            copy.wait()

    def gather(dst, index, at):
        dst[0, H:, :] = jnp.zeros((HP - H, C), F32)

        def take(h, k, j):
            dst[0, pl.ds(h, 1), :] = table_s[pl.ds(k, 1), :]

        for_each_hand(index, at, take)

    @pl.when(r == 0)
    def _():
        gather(strat_ref, tbucket_ref, t)

    gather(first_ref, bucket_ref, board)
    node = bet_ref[0] + first_ref[0] * delta_ref[0]
    node_s[...] = jnp.where(r == 0, node, node_s[...] + node)

    @pl.when(r == rivers - 1)
    def _():
        nodes = node_s[...]
        hi, lo = parts(nodes - pltpu.roll(nodes, G, 1), 2)
        both = jnp.concatenate([hi[:, :G], lo[:, :G]], axis=1)
        trow_s[0:1, :H] = trow_ref[pl.ds(t, 1), :]
        trow = trow_s[0:1, :]
        row = lax.broadcasted_iota(jnp.int32, (gain_ref.shape[0], HP), 0)
        bucket = row // 4 * 8 + row % 4

        def sums(ids):
            hot = jnp.where(ids == trow, 1.0, 0.0).astype(BF)
            out = lax.dot_general(hot, both, NN, preferred_element_type=F32)
            return out + pltpu.roll(out, G, 1)

        lane = lax.broadcasted_iota(jnp.int32, gain_ref.shape, 1)
        gain_ref[...] += jnp.where(lane < G, sums(bucket), sums(bucket + 4))


def reply_kernel(
    turns,
    rivers,
    river_total,
    tcard_ref,
    rcard_ref,
    first_ref,
    strat_ref,
    signed_ref,
    mine_ref,
    pot_ref,
    holds_ref,
    out_of_ref,
    cols_ref,
    out_ref,
    mine_s,
    reach_s,
    reply_s,
    wide_s,
):
    board = pl.program_id(0)
    t, r = board // rivers, board % rivers

    @pl.when(board == 0)
    def _():
        widen(wide_s, mine_ref, mine_s)
        reply_s[...] = jnp.zeros_like(reply_s)

    col_ok = playable(cols_ref[0], cols_ref[1], tcard_ref[t], rcard_ref[r, t])
    first = first_ref[0]
    reach = jnp.where(col_ok, mine_s[...] * strat_ref[0], 0.0)
    reach_s[:, :C] = (reach * first).astype(BF)
    reach_s[:, C:] = (reach * (1.0 - first)).astype(BF)
    against = lax.dot_general(signed_ref[0], reach_s[...], NN, preferred_element_type=F32)
    against_bet = others(reach_s[:, C:], holds_ref, out_of_ref)
    low, high = stake_rows(pot_ref)
    reply = low * against[:, :C] + jnp.maximum(high * against[:, C:], -(low * against_bet))
    reply = jnp.where(col_ok, reply, 0.0)
    reply_s[...] = jnp.where(r == 0, reply, reply_s[...] + reply)

    @pl.when(r == rivers - 1)
    def _():
        flat = jnp.transpose(reply_s[...])
        flat = (flat[:G] + flat[G:]) * (1.0 / river_total)
        owners = out_ref.shape[0]
        each = G // owners
        blocks = HP // 128
        for turn in range(turns):

            @pl.when(t == turn)
            def _():
                for j in range(blocks):
                    piece = flat[:, j * 128 : (j + 1) * 128].reshape(owners, each, 128)
                    row = (turn * blocks + j) * each
                    out_ref[:, row : row + each, :] = piece


def shifted(x, axis, shift):
    return lax.ppermute(x, axis, [(i, (i + shift) % 4) for i in range(4)])


def spread(x, axis):
    return jnp.concatenate([x] + [shifted(x, axis, s) for s in (1, 2, 3)], axis=0)


def block(x, at):
    return lax.dynamic_index_in_dim(x, at, 0, keepdims=False)


def per_device(
    river_regret,
    turn_regret,
    river_bucket,
    turn_bucket,
    ranks,
    turn_card,
    river_card,
    player_range,
    opp_range,
    call_prob,
    base_pot,
):
    turns, rivers, _ = river_bucket.shape
    boards = turns * rivers
    devices = 128
    owners = 16
    each = G // owners
    river_total = rivers * owners
    owned, towned = river_regret.shape[0], turn_regret.shape[0]
    buckets, tbuckets = owned * devices, towned * devices
    disjoint, holds, out_of, rperm, tperm, cols = constants()
    params = pltpu.CompilerParams(vmem_limit_bytes=VMEM_LIMIT)
    pot = base_pot.reshape(1, G)
    calls = jnp.transpose(call_prob, (0, 3, 1, 2))
    river_at_turn = river_card.T
    place = jnp.stack([lax.axis_index(a) for a in AXES]).astype(jnp.int32)
    rest = owned + towned
    turn_row = turns * (HP // 128) * each
    river_row = turn_row + towned // 2
    sent_rows = river_row + owned
    vmem, smem = (pl.BlockSpec(memory_space=space) for space in (pltpu.VMEM, pltpu.SMEM))

    with jax.named_scope("strategies"):
        strategies, *indices = pl.pallas_call(
            strategy_kernel,
            in_specs=[smem] + [vmem] * 6,
            out_shape=[
                jax.ShapeDtypeStruct((rest, C), F32),
                jax.ShapeDtypeStruct((boards, INDEX_ROW // 128, 128), jnp.int32),
                jax.ShapeDtypeStruct((boards, INDEX_ROW // 128, 128), jnp.int32),
                jax.ShapeDtypeStruct((turns, INDEX_ROW // 128, 128), jnp.int32),
            ],
            compiler_params=params,
            name="strategies",
        )(place, river_regret, turn_regret, rperm, tperm, river_bucket, turn_bucket)
        index, river_at, turn_at = (a.reshape(-1) for a in indices)
        plane = spread(spread(strategies, "y"), "z")
        far, up, down = (shifted(plane, "x", s) for s in (2, 1, 3))
        calls, _ = lax.optimization_barrier((calls, plane))

    def whole(shape):
        return pl.BlockSpec(shape, lambda i, *_: (0,) * len(shape))

    def per_board(shape):
        return pl.BlockSpec((1,) + shape, lambda i, *_: (i,) + (0,) * len(shape))

    def per_turn(shape):
        return pl.BlockSpec((1,) + shape, lambda i, *_: (i // rivers,) + (0,) * len(shape))

    with jax.named_scope("payoffs"):
        signed, delta, bet = pl.pallas_call(
            functools.partial(payoff_kernel, rivers),
            grid_spec=pltpu.PrefetchScalarGridSpec(
                num_scalar_prefetch=2,
                grid=(boards,),
                in_specs=[
                    per_turn((rivers, H)),
                    per_turn((H, rivers, C)),
                    whole((G, H)),
                    whole((1, G)),
                    whole((HP, HP)),
                    whole((64, HP)),
                    whole((HP, 256)),
                    whole((C, C)),
                    whole((2, HP, 128)),
                ],
                out_specs=[
                    per_board((HP, HP)),
                    per_board((HP, C)),
                    per_board((HP, C)),
                ],
                scratch_shapes=[
                    pltpu.VMEM((8, HP), jnp.int32),
                    pltpu.VMEM((rivers * HP, C), F32),
                    pltpu.VMEM((C, HP), F32),
                    pltpu.VMEM((HP, C), F32),
                    pltpu.VMEM((HP, 2 * C), BF),
                ],
            ),
            out_shape=[
                jax.ShapeDtypeStruct((boards, HP, HP), BF),
                jax.ShapeDtypeStruct((boards, HP, C), F32),
                jax.ShapeDtypeStruct((boards, HP, C), F32),
            ],
            compiler_params=params,
            cost_estimate=pl.CostEstimate(
                flops=22 * 10**9, bytes_accessed=10**6, transcendentals=0
            ),
            name="payoffs",
        )(
            turn_card,
            river_at_turn,
            ranks,
            calls,
            opp_range,
            pot,
            disjoint,
            holds,
            out_of,
            tperm,
            cols,
        )

    with jax.named_scope("river_sums"):
        mine, theirs = pl.pallas_call(
            sum_kernel,
            grid_spec=pltpu.PrefetchScalarGridSpec(
                num_scalar_prefetch=2,
                grid=(boards,),
                in_specs=[per_board((HP, C))],
                out_specs=[whole((4, owners * owned, C))] * 2,
                scratch_shapes=[pltpu.VMEM((buckets, C), F32)] * TABLES,
            ),
            out_shape=[jax.ShapeDtypeStruct((4, owners * owned, C), F32)] * 2,
            compiler_params=params,
            cost_estimate=pl.CostEstimate(
                flops=22 * 10**9, bytes_accessed=10**6, transcendentals=0
            ),
            name="sums",
        )(index, place, delta)
        theirs, up, far, down = lax.optimization_barrier((theirs, up, far, down))
        own = [plane, up, far, down]
        pieces = own + [lax.ppermute(piece, "core", [(0, 1), (1, 0)]) for piece in own]
        got = lax.ppermute(theirs, "core", [(0, 1), (1, 0)])
        up_now, down_now, later, kept = (mine[i] + got[i] for i in range(4))
        from_below, from_above = shifted(up_now, "x", 1), shifted(down_now, "x", 3)
        later, delta = lax.optimization_barrier((later, delta))

    with jax.named_scope("nodes"):
        first, strat, gains = pl.pallas_call(
            functools.partial(node_kernel, rivers, len(pieces)),
            grid_spec=pltpu.PrefetchScalarGridSpec(
                num_scalar_prefetch=2,
                grid=(boards,),
                in_specs=[
                    whole((turns, H)),
                    per_board((HP, C)),
                    per_board((HP, C)),
                ]
                + [pl.BlockSpec(memory_space=pl.ANY)] * len(pieces),
                out_specs=[
                    per_board((HP, C)),
                    per_turn((HP, C)),
                    whole((tbuckets // 2, C)),
                ],
                scratch_shapes=[
                    pltpu.VMEM((rest * devices, C), F32),
                    pltpu.VMEM((HP, C), F32),
                    pltpu.VMEM((8, HP), jnp.int32),
                    pltpu.SemaphoreType.DMA((len(pieces),)),
                ],
            ),
            out_shape=[
                jax.ShapeDtypeStruct((boards, HP, C), F32),
                jax.ShapeDtypeStruct((turns, HP, C), F32),
                jax.ShapeDtypeStruct((tbuckets // 2, C), F32),
            ],
            compiler_params=params,
            cost_estimate=pl.CostEstimate(
                flops=22 * 10**9, bytes_accessed=10**6, transcendentals=0
            ),
            name="nodes",
        )(river_at, turn_at, turn_bucket, delta, bet, *pieces)

    with jax.named_scope("river_sums"):
        gains, from_below, from_above = lax.optimization_barrier((gains, from_below, from_above))
        half = owners * owned // 2
        below = shifted(later[:half] + from_below[:half], "x", 1)
        above = shifted(later[half:] + from_above[:half], "x", 3)

    with jax.named_scope("turn_sums"):
        x, core = place[0], place[1]
        pairs = gains.reshape(4, 2, -1, C)
        held = lax.dynamic_index_in_dim(pairs, core, 1, keepdims=False)
        lent = lax.dynamic_index_in_dim(pairs, 1 - core, 1, keepdims=False)
        held = held + lax.ppermute(lent, "core", [(0, 1), (1, 0)])
        turn_parts = [block(held, x)]
        turn_parts += [shifted(block(held, (x + s) % 4), "x", s) for s in (2, 1, 3)]

    with jax.named_scope("replies"):
        replies = pl.pallas_call(
            functools.partial(reply_kernel, turns, rivers, river_total),
            grid_spec=pltpu.PrefetchScalarGridSpec(
                num_scalar_prefetch=2,
                grid=(boards,),
                in_specs=[
                    per_board((HP, C)),
                    per_turn((HP, C)),
                    per_board((HP, HP)),
                    whole((G, H)),
                    whole((1, G)),
                    whole((64, HP)),
                    whole((HP, 256)),
                    whole((2, HP, 128)),
                ],
                out_specs=whole((owners, sent_rows, 128)),
                scratch_shapes=[
                    pltpu.VMEM((HP, C), F32),
                    pltpu.VMEM((HP, 2 * C), BF),
                    pltpu.VMEM((HP, C), F32),
                    pltpu.VMEM((C, HP), F32),
                ],
            ),
            out_shape=jax.ShapeDtypeStruct((owners, sent_rows, 128), F32),
            compiler_params=params,
            cost_estimate=pl.CostEstimate(
                flops=18 * 10**9, bytes_accessed=10**6, transcendentals=0
            ),
            name="replies",
        )(
            turn_card,
            river_at_turn,
            first,
            strat,
            signed,
            player_range,
            pot,
            holds,
            out_of,
            cols,
        )

    with jax.named_scope("exchange"):
        replies, below, above, turn_parts = lax.optimization_barrier(
            (replies, below, above, turn_parts)
        )
        turn_sums = sum(turn_parts[1:], turn_parts[0])
        column = kept + jnp.concatenate([below + from_above[half:], above + from_below[half:]])
        sent = replies.at[:, turn_row:river_row].set(turn_sums.reshape(owners, -1, 128))
        sent = sent.at[:, river_row:].set(column.reshape(owners, -1, 128))
        came = lax.all_to_all(sent, ("z", "y"), 0, 0)

    with jax.named_scope("update"):
        new_river, new_turn, br_value = pl.pallas_call(
            functools.partial(update_kernel, 1.0 / river_total, each),
            out_shape=[
                jax.ShapeDtypeStruct(river_regret.shape, F32),
                jax.ShapeDtypeStruct(turn_regret.shape, F32),
                jax.ShapeDtypeStruct((turns, each, H), F32),
            ],
            compiler_params=params,
            name="update",
        )(came, river_regret, turn_regret, rperm, tperm)
    return new_river, new_turn, br_value


def solution(mesh):
    mesh = Mesh(mesh.devices.reshape(4, 2, 4, 4), AXES)
    turn, river = AXES[:2], AXES[2:]
    placed = (
        P(AXES, None),
        P(AXES, None),
        P(turn, river, None),
        P(turn, None),
        P(turn, river, None),
        P(turn),
        P(turn, river),
        P(),
        P(),
        P(turn, river, None, None),
        P(),
    )
    return jax.shard_map(
        per_device,
        mesh=mesh,
        in_specs=placed,
        out_specs=(P(AXES, None), P(AXES, None), P(turn, river, None)),
        check_vma=False,
    )
```

time: 588 us -> 156 us (0.27)
  waiting for transfers between devices: 460 us -> 11 us
  starting transfers between devices: 0.16 us -> 29.3 us
  blocking collectives: 0 us -> 26.4 us
  Pallas kernels: 101 us -> 77 us
  between operations: 14.4 us -> 0.82 us
    unnamed x7 -> x0, waiting for transfers between devices: 441 us -> none
    ppermute x0 -> x22, starting transfers between devices: none -> 29.3 us  [the longest x16 28 us: shifted(): return lax.ppermute(x, axis, [(i, (i + shift) % 4) for i in range(4)])]
    all_to_all x0 -> x1, blocking collectives: none -> 26.4 us  [per_device(): came = lax.all_to_all(sent, ('z', 'y'), 0, 0)]
    pallas_call x1, Pallas kernels: 44.7 us -> 19.1 us  [per_device(): pl.pallas_call(functools.partial(payoff_kernel, rivers), grid_spec=pltpu....]
    all_gather x1 -> x0, waiting for transfers between devices: 18.3 us -> none  [per_device(): table = lax.all_gather(strategies, ('turn', 'river'), axis=0, tiled=True)]
    ppermute x0 -> x22, waiting for transfers between devices: none -> 11 us  [the longest x1 6.08 us: per_device(): got = lax.ppermute(theirs, 'core', [(0, 1), (1, 0)])]
    unnamed x11 -> x9, local copies, waits for them, and re-layouts: 11.3 us -> 5.2 us
    pallas_call x3 -> x5, Pallas kernels: 56.2 us -> 57.9 us  [the longest x1 22.1 us: per_device(): pl.pallas_call(functools.partial(node_kernel, rivers, len(pieces)), grid_...]
  transfers between devices with their start and end apart: 4 -> 22, of which waited for: 4 -> 4; matrix products, arithmetic and copies ran while one was open for 2% -> 4% of each run, Pallas kernels for 8% -> 47%
where the time goes in v2:
time: 156 us
  Pallas kernels  77 us (49%)
  starting transfers between devices  29.3 us (19%)
  blocking collectives  26.4 us (17%)
  waiting for transfers between devices  11 us (7%)
  local copies, waits for them, and re-layouts  7.48 us (5%)
  other arithmetic  3.58 us (2%)
    ppermute x16, starting transfers between devices, shifted(): return lax.ppermute(x, axis, [(i, (i + shift) % 4) for i in range(4)])  28 us
    all_to_all x1, blocking collectives, per_device(): came = lax.all_to_all(sent, ('z', 'y'), 0, 0)  26.4 us
    pallas_call x1, Pallas kernels, per_device(): pl.pallas_call(functools.partial(node_kernel, rivers, len(pieces)), grid_...  22.1 us
    pallas_call x1, Pallas kernels, per_device(): pl.pallas_call(functools.partial(payoff_kernel, rivers), grid_spec=pltpu....  19.1 us
    pallas_call x1, Pallas kernels, per_device(): pl.pallas_call(sum_kernel, grid_spec=pltpu.PrefetchScalarGridSpec(num_sca...  15.6 us
    pallas_call x1, Pallas kernels, per_device(): pl.pallas_call(functools.partial(reply_kernel, turns, rivers, river_total...  15.6 us
    ppermute x1, waiting for transfers between devices, per_device(): got = lax.ppermute(theirs, 'core', [(0, 1), (1, 0)])  6.08 us
    unnamed x9, local copies, waits for them, and re-layouts  5.2 us
  transfers between devices with their start and end apart: 22, of which 4 were waited for; matrix products, arithmetic and copies ran while one was open for 4% of the time, Pallas kernels for 47%

profile of v2, /device:TPU:0, one launch (start us, length us, event | category | flops | bytes accessed | tf_op | source)
XLA Modules:
  0.0 155.6 jit_solution(2383795798429811912)
XLA Ops:
  0.6 0.7 pad_add_fusion.place_ref
  1.3 1.9 %strategies.1 = (f32[80,128]{1,0:T(8,128)}, s32[6,16,128]{2,1,0:T(8,128)}, s32[6,16,128]{2,1,0:T(8,128)}, s32[3,16,128]{2,1,0:T(8,128)}) custom-call(s32[4]{0:T(128)} %pad_add_fusion.place_ref, f32[72,256]{1,0:T(8,128)} %river_ref.3, f32[8,128]{1,0:T(8,128)} %turn_ref.3, bf16[256,256]{1,0:T(8,128)(2,1)} %constant.128.clone.rperm_ref, ...), custom_call_target="tpu_custom_call" | custom-call | tf_op jit(solution)/shard_map/strategies/strategies/pallas_call | solution.py:472
  3.2 1.7 %collective-permute-start = (f32[80,128]{1,0:T(8,128)}, f32[80,128]{1,0:T(8,128)S(1)}, u32[]{:S(2)}, u32[]{:S(2)}) collective-permute-start(f32[80,128]{1,0:T(8,128)} %get-tuple-element.59), channel_id=1, source_target_pairs={{0,1},{1,2},{2,3},{3,0},{4,5},{5,6},{6,7},{7,4},{8,9},{9,10},{10,1... | collective-permute-start | bytes 122888 | tf_op jit(solution)/shard_map/strategies/ppermute | solution.py:427
  4.8 2.9 %collective-permute-start.1 = (f32[80,128]{1,0:T(8,128)}, f32[80,128]{1,0:T(8,128)S(1)}, u32[]{:S(2)}, u32[]{:S(2)}) collective-permute-start(f32[80,128]{1,0:T(8,128)} %get-tuple-element.59), channel_id=1, source_target_pairs={{0,2},{1,3},{2,0},{3,1},{4,6},{5,7},{6,4},{7,5},{8,10},{9,11},{10,... | collective-permute-start | bytes 122888 | tf_op jit(solution)/shard_map/strategies/ppermute | solution.py:427
  7.8 1.3 collective-permute-start.2
  9.1 1.4 constant_dynamic-update-slice_fusion.3
  10.5 0.6 constant_dynamic-update-slice_fusion.2
  12.6 1.9 %collective-permute-start.3 = (f32[320,128]{1,0:T(8,128)S(1)}, f32[320,128]{1,0:T(8,128)S(1)}, u32[]{:S(2)}, u32[]{:S(2)}) collective-permute-start(f32[320,128]{1,0:T(8,128)S(1)} %get-tuple-element.95), channel_id=1, source_target_pairs={{0,4},{4,8},{8,12},{12,0},{1,5},{5,9},{9,13},{13,1},{2,6},{6,10},{... | collective-permute-start | bytes 491528 | tf_op jit(solution)/shard_map/strategies/ppermute | solution.py:427
  14.5 3.6 %collective-permute-start.4 = (f32[320,128]{1,0:T(8,128)S(1)}, f32[320,128]{1,0:T(8,128)S(1)}, u32[]{:S(2)}, u32[]{:S(2)}) collective-permute-start(f32[320,128]{1,0:T(8,128)S(1)} %get-tuple-element.95), channel_id=1, source_target_pairs={{0,8},{4,12},{8,0},{12,4},{1,9},{5,13},{9,1},{13,5},{2,10},{6,14},... | collective-permute-start | bytes 491528 | tf_op jit(solution)/shard_map/strategies/ppermute | solution.py:427
  18.1 1.0 collective-permute-start.5
  19.1 2.0 %collective-permute-done.3 = f32[320,128]{1,0:T(8,128)S(1)} collective-permute-done((f32[320,128]{1,0:T(8,128)S(1)}, f32[320,128]{1,0:T(8,128)S(1)}, u32[]{:S(2)}, u32[]{:S(2)}) %collective-permute-start.3) | collective-permute-done | bytes 163872 | tf_op jit(solution)/shard_map/strategies/ppermute | solution.py:427
  21.1 0.7 constant_dynamic-update-slice_fusion.6
  21.8 2.7 %collective-permute-done.4 = f32[320,128]{1,0:T(8,128)S(1)} collective-permute-done((f32[320,128]{1,0:T(8,128)S(1)}, f32[320,128]{1,0:T(8,128)S(1)}, u32[]{:S(2)}, u32[]{:S(2)}) %collective-permute-start.4) | collective-permute-done | bytes 163872 | tf_op jit(solution)/shard_map/strategies/ppermute | solution.py:427
  24.5 0.7 constant_dynamic-update-slice_fusion.5
  25.1 0.7 constant_dynamic-update-slice_fusion.4.refs_0_
  25.8 1.5 collective-permute-start.6
  27.3 2.7 %collective-permute-start.7 = (f32[1280,128]{1,0:T(8,128)}, f32[1280,128]{1,0:T(8,128)}, u32[]{:S(2)}, u32[]{:S(2)}) collective-permute-start(f32[1280,128]{1,0:T(8,128)} %constant_dynamic-update-slice_fusion.4.refs_0_), channel_id=1, source_target_pairs={{0,64},{32,96},{64,0},{96,32},{1,65},{33,97},{65,1},{97,33},{2,66}... | collective-permute-start | bytes 1966088 | tf_op jit(solution)/shard_map/strategies/ppermute | solution.py:427
  30.0 1.4 collective-permute-start.8
  31.5 19.1 %payoffs.1 = (bf16[6,1152,1152]{2,1,0:T(8,128)(2,1)}, f32[6,1152,128]{2,1,0:T(8,128)}, f32[6,1152,128]{2,1,0:T(8,128)}) custom-call(s32[3]{0:T(128)} %tcard_ref.3, s32[2,3]{1,0:T(2,128)} %bitcast.41, s32[3,2,1081]{2,1,0:T(2,128)} %rank_ref.1, bf16[3,1081,2,128]{3,2,1,0:T(2,128)(2,1)} %bitcast.37, f32[64,1081]{1,0:T(8,128)} %opp_ref.1, f32[1,64]{1,0:T(1,128)} %bitcast.43, ...), custom_call_target="tpu_custom_call" | custom-call | flops 22000001024 | bytes 1000000 | tf_op jit(solution)/shard_map/payoffs/payoffs/pallas_call | solution.py:499
  50.5 15.6 %sums.1 = (f32[4,1152,128]{2,1,0:T(8,128)}, f32[4,1152,128]{2,1,0:T(8,128)}) custom-call(s32[12288]{0:T(1024)} %bitcast.39, s32[4]{0:T(128)} %pad_add_fusion.place_ref, f32[6,1152,128]{2,1,0:T(8,128)} %get-tuple-element.65.delta_ref), custom_call_target="tpu_custom_call" | custom-call | flops 22000001024 | bytes 1000000 | tf_op jit(solution)/shard_map/river_sums/sums/pallas_call | solution.py:553
  67.4 6.1 %collective-permute-done.9 = f32[4,1152,128]{2,1,0:T(8,128)S(1)} collective-permute-done((f32[4,1152,128]{2,1,0:T(8,128)}, f32[4,1152,128]{2,1,0:T(8,128)S(1)}, u32[]{:S(2)}, u32[]{:S(2)}) %collective-permute-start.9) | collective-permute-done | bytes 2359328 | tf_op jit(solution)/shard_map/river_sums/ppermute | solution.py:572
  73.4 2.7 %slice_add_fusion = (f32[1,1152,128]{2,1,0:T(8,128)S(1)}, f32[1152,128]{1,0:T(8,128)S(1)}, f32[1152,128]{1,0:T(8,128)}, f32[1152,128]{1,0:T(8,128)S(1)}) fusion(f32[4,1152,128]{2,1,0:T(8,128)S(1)} %collective-permute-done.9, f32[4,1152,128]{2,1,0:T(8,128)} %get-tuple-element.62), kind=kLoop, calls=%fused_computation | loop fusion | flops 589824 | bytes 7077888 | tf_op jit(solution)/shard_map/river_sums/add | solution.py:573
  76.7 2.6 %collective-permute-start.15 = (f32[1152,128]{1,0:T(8,128)S(1)}, f32[1152,128]{1,0:T(8,128)S(1)}, u32[]{:S(2)}, u32[]{:S(2)}) collective-permute-start(f32[1152,128]{1,0:T(8,128)S(1)} %get-tuple-element.86), channel_id=1, source_target_pairs={{0,96},{32,0},{64,32},{96,64},{1,97},{33,1},{65,33},{97,65},{2,98}... | collective-permute-start | bytes 1769480 | tf_op jit(solution)/shard_map/river_sums/ppermute | solution.py:427
  79.4 22.1 %nodes.1 = (f32[6,1152,128]{2,1,0:T(8,128)}, f32[3,1152,128]{2,1,0:T(8,128)}, f32[512,128]{1,0:T(8,128)}) custom-call(s32[12288]{0:T(1024)} %bitcast.38, s32[6144]{0:T(1024)} %bitcast.40, s32[3,1081]{1,0:T(4,128)} %trow_ref.1, f32[6,1152,128]{2,1,0:T(8,128)} %get-tuple-element.65.delta_ref, f32[6,1152,128]{2,1,0:T(8,128)} %get-tuple-element.66.bet_ref, ...), custom_call_target="tpu_custom_call" | custom-call | flops 22000001024 | bytes 1000000 | tf_op jit(solution)/shard_map/nodes/nodes/pallas_call | solution.py:578
  101.5 1.0 dynamic-slice_bitcast_fusion
  102.7 3.2 %collective-permute-start.17 = (f32[576,128]{1,0:T(8,128)S(1)}, f32[576,128]{1,0:T(8,128)S(1)}, u32[]{:S(2)}, u32[]{:S(2)}) collective-permute-start(f32[576,128]{1,0:T(8,128)S(1)} %get-tuple-element.89), channel_id=1, source_target_pairs={{0,96},{32,0},{64,32},{96,64},{1,97},{33,1},{65,33},{97,65},{2,98}... | collective-permute-start | bytes 884744 | tf_op jit(solution)/shard_map/river_sums/ppermute | solution.py:427
  106.1 0.9 collective-permute-start.20
  107.0 2.4 %collective-permute-start.21 = (f32[64,128]{1,0:T(8,128)S(1)}, f32[64,128]{1,0:T(8,128)S(1)}, u32[]{:S(2)}, u32[]{:S(2)}) collective-permute-start(f32[64,128]{1,0:T(8,128)S(1)} %get-tuple-element.91), channel_id=1, source_target_pairs={{0,96},{32,0},{64,32},{96,64},{1,97},{33,1},{65,33},{97,65},{2,98}... | collective-permute-start | bytes 98312 | tf_op jit(solution)/shard_map/turn_sums/ppermute | solution.py:427
  109.4 15.6 %replies.1 = f32[16,184,128]{2,1,0:T(8,128)} custom-call(s32[3]{0:T(128)} %tcard_ref.3, s32[2,3]{1,0:T(2,128)} %bitcast.42, f32[6,1152,128]{2,1,0:T(8,128)} %get-tuple-element.70.first_ref, f32[3,1152,128]{2,1,0:T(8,128)} %get-tuple-element.71.strat_ref, bf16[6,1152,1152]{2,1,0:T(8,128)(2,1)} %get-tuple-element.72.signed_ref, f32[64,1081]{1,0:T(8,128)} %mine_ref.1, ...), custom_call_target="tpu_custom_call" | custom-call | flops 17999998976 | bytes 1000000 | tf_op jit(solution)/shard_map/replies/replies/pallas_call | solution.py:629
  125.2 1.2 copy-done
  126.5 26.4 %all_to_all.5.came_ref = f32[16,184,128]{2,1,0:T(8,128)} all-to-all(f32[16,184,128]{2,1,0:T(8,128)S(1)} %add_dynamic-update-slice_fusion), channel_id=1, replica_groups=mesh['x'=4,'core'=2,'z'=4,'y'=4] {'z','y'}, dimensions={0} | all-to-all | bytes 3014656 | tf_op jit(solution)/shard_map/exchange/all_to_all | solution.py:679
  152.9 2.7 %update.1 = (f32[72,256]{1,0:T(8,128)}, f32[8,128]{1,0:T(8,128)}, f32[3,4,1081]{2,1,0:T(4,128)}) custom-call(f32[16,184,128]{2,1,0:T(8,128)} %all_to_all.5.came_ref, f32[72,256]{1,0:T(8,128)} %river_ref.3, f32[8,128]{1,0:T(8,128)} %turn_ref.3, bf16[256,256]{1,0:T(8,128)(2,1)} %constant.128.clone.rperm_ref, bf16[128,128]{1,0:T(8,128)(2,1)} %constant.129.clone.tperm_ref), custom_call_target="tpu_custom_call" | custom-call | tf_op jit(solution)/shard_map/update/update/pallas_call | solution.py:682
  (41 shorter events, 3.8 us)
Async XLA Ops:
  3.2 7.3 %collective-permute-start = (f32[80,128]{1,0:T(8,128)}, f32[80,128]{1,0:T(8,128)S(1)}, u32[]{:S(2)}, u32[]{:S(2)}) collective-permute-start(f32[80,128]{1,0:T(8,128)} %get-tuple-element.59), channel_id=1, source_target_pairs={{0,1},{1,2},{2,3},{3,0},{4,5},{5,6},{6,7},{7,4},{8,9},{9,10},{10,1... | collective-permute-start | bytes 122888 | tf_op jit(solution)/shard_map/strategies/ppermute | solution.py:427
  4.8 6.3 %collective-permute-start.1 = (f32[80,128]{1,0:T(8,128)}, f32[80,128]{1,0:T(8,128)S(1)}, u32[]{:S(2)}, u32[]{:S(2)}) collective-permute-start(f32[80,128]{1,0:T(8,128)} %get-tuple-element.59), channel_id=1, source_target_pairs={{0,2},{1,3},{2,0},{3,1},{4,6},{5,7},{6,4},{7,5},{8,10},{9,11},{10,... | collective-permute-start | bytes 122888 | tf_op jit(solution)/shard_map/strategies/ppermute | solution.py:427
  7.8 4.2 %collective-permute-start.2 = (f32[80,128]{1,0:T(8,128)}, f32[80,128]{1,0:T(8,128)S(1)}, u32[]{:S(2)}, u32[]{:S(2)}) collective-permute-start(f32[80,128]{1,0:T(8,128)} %get-tuple-element.59), channel_id=1, source_target_pairs={{0,3},{1,0},{2,1},{3,2},{4,7},{5,4},{6,5},{7,6},{8,11},{9,8},{10,9... | collective-permute-start | bytes 122888 | tf_op jit(solution)/shard_map/strategies/ppermute | solution.py:427
  12.6 8.5 %collective-permute-start.3 = (f32[320,128]{1,0:T(8,128)S(1)}, f32[320,128]{1,0:T(8,128)S(1)}, u32[]{:S(2)}, u32[]{:S(2)}) collective-permute-start(f32[320,128]{1,0:T(8,128)S(1)} %get-tuple-element.95), channel_id=1, source_target_pairs={{0,4},{4,8},{8,12},{12,0},{1,5},{5,9},{9,13},{13,1},{2,6},{6,10},{... | collective-permute-start | bytes 491528 | tf_op jit(solution)/shard_map/strategies/ppermute | solution.py:427
  14.5 10.0 %collective-permute-start.4 = (f32[320,128]{1,0:T(8,128)S(1)}, f32[320,128]{1,0:T(8,128)S(1)}, u32[]{:S(2)}, u32[]{:S(2)}) collective-permute-start(f32[320,128]{1,0:T(8,128)S(1)} %get-tuple-element.95), channel_id=1, source_target_pairs={{0,8},{4,12},{8,0},{12,4},{1,9},{5,13},{9,1},{13,5},{2,10},{6,14},... | collective-permute-start | bytes 491528 | tf_op jit(solution)/shard_map/strategies/ppermute | solution.py:427
  18.1 7.1 %collective-permute-start.5 = (f32[320,128]{1,0:T(8,128)S(1)}, f32[320,128]{1,0:T(8,128)S(1)}, u32[]{:S(2)}, u32[]{:S(2)}) collective-permute-start(f32[320,128]{1,0:T(8,128)S(1)} %get-tuple-element.95), channel_id=1, source_target_pairs={{0,12},{4,0},{8,4},{12,8},{1,13},{5,1},{9,5},{13,9},{2,14},{6,2},{... | collective-permute-start | bytes 491528 | tf_op jit(solution)/shard_map/strategies/ppermute | solution.py:427
  25.8 40.4 %collective-permute-start.6 = (f32[1280,128]{1,0:T(8,128)}, f32[1280,128]{1,0:T(8,128)}, u32[]{:S(2)}, u32[]{:S(2)}) collective-permute-start(f32[1280,128]{1,0:T(8,128)} %constant_dynamic-update-slice_fusion.4.refs_0_), channel_id=1, source_target_pairs={{0,32},{32,64},{64,96},{96,0},{1,33},{33,65},{65,97},{97,1},{2,34}... | collective-permute-start | bytes 1966088 | tf_op jit(solution)/shard_map/strategies/ppermute | solution.py:427
  27.3 38.9 %collective-permute-start.7 = (f32[1280,128]{1,0:T(8,128)}, f32[1280,128]{1,0:T(8,128)}, u32[]{:S(2)}, u32[]{:S(2)}) collective-permute-start(f32[1280,128]{1,0:T(8,128)} %constant_dynamic-update-slice_fusion.4.refs_0_), channel_id=1, source_target_pairs={{0,64},{32,96},{64,0},{96,32},{1,65},{33,97},{65,1},{97,33},{2,66}... | collective-permute-start | bytes 1966088 | tf_op jit(solution)/shard_map/strategies/ppermute | solution.py:427
  30.0 36.1 %collective-permute-start.8 = (f32[1280,128]{1,0:T(8,128)}, f32[1280,128]{1,0:T(8,128)}, u32[]{:S(2)}, u32[]{:S(2)}) collective-permute-start(f32[1280,128]{1,0:T(8,128)} %constant_dynamic-update-slice_fusion.4.refs_0_), channel_id=1, source_target_pairs={{0,96},{32,0},{64,32},{96,64},{1,97},{33,1},{65,33},{97,65},{2,98}... | collective-permute-start | bytes 1966088 | tf_op jit(solution)/shard_map/strategies/ppermute | solution.py:427
  66.2 7.3 %collective-permute-start.9 = (f32[4,1152,128]{2,1,0:T(8,128)}, f32[4,1152,128]{2,1,0:T(8,128)S(1)}, u32[]{:S(2)}, u32[]{:S(2)}) collective-permute-start(f32[4,1152,128]{2,1,0:T(8,128)} %get-tuple-element.64), channel_id=1, source_target_pairs={{0,16},{16,0},{1,17},{17,1},{2,18},{18,2},{3,19},{19,3},{4,20},{20... | collective-permute-start | bytes 7077896 | tf_op jit(solution)/shard_map/river_sums/ppermute | solution.py:572
  66.3 10.4 %collective-permute-start.10 = (f32[1280,128]{1,0:T(8,128)}, f32[1280,128]{1,0:T(8,128)}, u32[]{:S(2)}, u32[]{:S(2)}) collective-permute-start(f32[1280,128]{1,0:T(8,128)} %constant_dynamic-update-slice_fusion.4.refs_0_), channel_id=1, source_target_pairs={{0,16},{16,0},{1,17},{17,1},{2,18},{18,2},{3,19},{19,3},{4,20},{20... | collective-permute-start | bytes 1966088 | tf_op jit(solution)/shard_map/river_sums/ppermute | solution.py:571
  66.8 12.6 %collective-permute-start.11 = (f32[1280,128]{1,0:T(8,128)}, f32[1280,128]{1,0:T(8,128)}, u32[]{:S(2)}, u32[]{:S(2)}) collective-permute-start(f32[1280,128]{1,0:T(8,128)} %collective-permute-done.6.refs_1_), channel_id=1, source_target_pairs={{0,16},{16,0},{1,17},{17,1},{2,18},{18,2},{3,19},{19,3},{4,20},{20... | collective-permute-start | bytes 1966088 | tf_op jit(solution)/shard_map/river_sums/ppermute | solution.py:571
  66.9 12.5 %collective-permute-start.12 = (f32[1280,128]{1,0:T(8,128)}, f32[1280,128]{1,0:T(8,128)}, u32[]{:S(2)}, u32[]{:S(2)}) collective-permute-start(f32[1280,128]{1,0:T(8,128)} %collective-permute-done.7.refs_2_), channel_id=1, source_target_pairs={{0,16},{16,0},{1,17},{17,1},{2,18},{18,2},{3,19},{19,3},{4,20},{20... | collective-permute-start | bytes 1966088 | tf_op jit(solution)/shard_map/river_sums/ppermute | solution.py:571
  67.3 12.1 %collective-permute-start.13 = (f32[1280,128]{1,0:T(8,128)}, f32[1280,128]{1,0:T(8,128)}, u32[]{:S(2)}, u32[]{:S(2)}) collective-permute-start(f32[1280,128]{1,0:T(8,128)} %collective-permute-done.8.refs_3_), channel_id=1, source_target_pairs={{0,16},{16,0},{1,17},{17,1},{2,18},{18,2},{3,19},{19,3},{4,20},{20... | collective-permute-start | bytes 1966088 | tf_op jit(solution)/shard_map/river_sums/ppermute | solution.py:571
  76.1 25.4 %collective-permute-start.14 = (f32[1152,128]{1,0:T(8,128)}, f32[1152,128]{1,0:T(8,128)S(1)}, u32[]{:S(2)}, u32[]{:S(2)}) collective-permute-start(f32[1152,128]{1,0:T(8,128)} %get-tuple-element.87), channel_id=1, source_target_pairs={{0,32},{32,64},{64,96},{96,0},{1,33},{33,65},{65,97},{97,1},{2,34}... | collective-permute-start | bytes 1769480 | tf_op jit(solution)/shard_map/river_sums/ppermute | solution.py:427
  76.7 24.8 %collective-permute-start.15 = (f32[1152,128]{1,0:T(8,128)S(1)}, f32[1152,128]{1,0:T(8,128)S(1)}, u32[]{:S(2)}, u32[]{:S(2)}) collective-permute-start(f32[1152,128]{1,0:T(8,128)S(1)} %get-tuple-element.86), channel_id=1, source_target_pairs={{0,96},{32,0},{64,32},{96,64},{1,97},{33,1},{65,33},{97,65},{2,98}... | collective-permute-start | bytes 1769480 | tf_op jit(solution)/shard_map/river_sums/ppermute | solution.py:427
  101.5 4.5 %copy-start.1 = (f32[512,128]{1,0:T(8,128)S(1)}, f32[512,128]{1,0:T(8,128)}, u32[]{:S(2)}) copy-start(f32[512,128]{1,0:T(8,128)} %get-tuple-element.77) | copy-start | bytes 786436
  102.5 3.5 %collective-permute-start.18 = (f32[4,64,128]{2,1,0:T(8,128)S(1)}, f32[4,64,128]{2,1,0:T(8,128)S(1)}, u32[]{:S(2)}, u32[]{:S(2)}) collective-permute-start(f32[4,64,128]{2,1,0:T(8,128)S(1)} %dynamic-slice_bitcast_fusion), channel_id=1, source_target_pairs={{0,16},{16,0},{1,17},{17,1},{2,18},{18,2},{3,19},{19,3},{4,20},{20... | collective-permute-start | bytes 393224 | tf_op jit(solution)/shard_map/turn_sums/ppermute | solution.py:624
  102.7 22.4 %collective-permute-start.16 = (f32[576,128]{1,0:T(8,128)S(1)}, f32[576,128]{1,0:T(8,128)S(1)}, u32[]{:S(2)}, u32[]{:S(2)}) collective-permute-start(f32[576,128]{1,0:T(8,128)S(1)} %get-tuple-element.90), channel_id=1, source_target_pairs={{0,32},{32,64},{64,96},{96,0},{1,33},{33,65},{65,97},{97,1},{2,34}... | collective-permute-start | bytes 884744 | tf_op jit(solution)/shard_map/river_sums/ppermute | solution.py:427
  102.7 22.3 %collective-permute-start.17 = (f32[576,128]{1,0:T(8,128)S(1)}, f32[576,128]{1,0:T(8,128)S(1)}, u32[]{:S(2)}, u32[]{:S(2)}) collective-permute-start(f32[576,128]{1,0:T(8,128)S(1)} %get-tuple-element.89), channel_id=1, source_target_pairs={{0,96},{32,0},{64,32},{96,64},{1,97},{33,1},{65,33},{97,65},{2,98}... | collective-permute-start | bytes 884744 | tf_op jit(solution)/shard_map/river_sums/ppermute | solution.py:427
  106.0 19.0 %collective-permute-start.19 = (f32[64,128]{1,0:T(8,128)S(1)}, f32[64,128]{1,0:T(8,128)S(1)}, u32[]{:S(2)}, u32[]{:S(2)}) collective-permute-start(f32[64,128]{1,0:T(8,128)S(1)} %get-tuple-element.93), channel_id=1, source_target_pairs={{0,64},{32,96},{64,0},{96,32},{1,65},{33,97},{65,1},{97,33},{2,66}... | collective-permute-start | bytes 98312 | tf_op jit(solution)/shard_map/turn_sums/ppermute | solution.py:427
  106.1 18.9 %collective-permute-start.20 = (f32[64,128]{1,0:T(8,128)S(1)}, f32[64,128]{1,0:T(8,128)S(1)}, u32[]{:S(2)}, u32[]{:S(2)}) collective-permute-start(f32[64,128]{1,0:T(8,128)S(1)} %get-tuple-element.92), channel_id=1, source_target_pairs={{0,32},{32,64},{64,96},{96,0},{1,33},{33,65},{65,97},{97,1},{2,34}... | collective-permute-start | bytes 98312 | tf_op jit(solution)/shard_map/turn_sums/ppermute | solution.py:427
  107.0 18.1 %collective-permute-start.21 = (f32[64,128]{1,0:T(8,128)S(1)}, f32[64,128]{1,0:T(8,128)S(1)}, u32[]{:S(2)}, u32[]{:S(2)}) collective-permute-start(f32[64,128]{1,0:T(8,128)S(1)} %get-tuple-element.91), channel_id=1, source_target_pairs={{0,96},{32,0},{64,32},{96,64},{1,97},{33,1},{65,33},{97,65},{2,98}... | collective-permute-start | bytes 98312 | tf_op jit(solution)/shard_map/turn_sums/ppermute | solution.py:427
  125.0 1.4 copy-start

commit v3 on v2

v3 whole, which is shorter than its diff:
```python
import functools

import jax
import jax.numpy as jnp
import ml_dtypes
import numpy as np
from jax import lax
from jax.experimental import pallas as pl
from jax.experimental.pallas import tpu as pltpu
from jax.sharding import Mesh
from jax.sharding import PartitionSpec as P

CARDS = 47
H = CARDS * (CARDS - 1) // 2
HP = 1152
G = 64
C = 2 * G
BF = jnp.bfloat16
F32 = jnp.float32
NT = (((1,), (1,)), ((), ()))
NN = (((1,), (0,)), ((), ()))
TABLES = 6
UNROLL = 47
CHUNKS = 3
INDEX_ROW = 2048
RANKS = 16384.0
AXES = ("x", "core", "z", "y")
VMEM_LIMIT = 60 * 1024 * 1024


def constants():
    first, second = np.triu_indices(CARDS, 1)
    share = (
        (first[:, None] == first[None, :])
        | (first[:, None] == second[None, :])
        | (second[:, None] == first[None, :])
        | (second[:, None] == second[None, :])
    )
    disjoint = np.zeros((HP, HP), np.float32)
    disjoint[:H, :H] = ~share
    cards = np.full((8, HP), -1, np.int32)
    cards[0, :H] = first
    cards[1, :H] = second
    holds = np.zeros((64, HP), np.float32)
    holds[first, np.arange(H)] = 1
    holds[second, np.arange(H)] = 1
    holds[CARDS, :H] = 1
    spread_out = np.zeros((HP, 64), np.float32)
    spread_out[:H, :CARDS] = -holds[:CARDS, :H].T
    spread_out[:H, CARDS] = 1
    spread_out = np.concatenate([spread_out] * 3 + [np.zeros_like(spread_out)], axis=1)
    river_perm = np.zeros((4 * G, 4 * G), np.float32)
    turn_perm = np.zeros((2 * G, 2 * G), np.float32)
    for g in range(G):
        for a in range(2):
            turn_perm[g * 2 + a, a * G + g] = 1
            for b in range(2):
                river_perm[g * 4 + a * 2 + b, b * C + a * G + g] = 1
    halves = [m.astype(ml_dtypes.bfloat16) for m in (disjoint, holds, spread_out, river_perm, turn_perm)]
    return halves + [cards]


def others(x, holds_ref, out_of_ref):
    sums = lax.dot_general(holds_ref[...], x, NN, preferred_element_type=F32)
    pieces = parts(sums, 3)
    pieces = jnp.concatenate(pieces + [jnp.zeros_like(pieces[0])], axis=0)
    return x.astype(F32) + lax.dot_general(
        out_of_ref[...], pieces, NN, preferred_element_type=F32
    )


def parts(x, count):
    out = []
    for _ in range(count):
        piece = x.astype(BF)
        out.append(piece)
        x = x - piece.astype(F32)
    return out


def permuted(x, perm, dims):
    hi, mid, lo = [
        lax.dot_general(piece, perm, dims, preferred_element_type=F32) for piece in parts(x, 3)
    ]
    return (hi + mid) + lo


def first_share(pos0, pos1):
    total = pos0 + pos1
    some = total > 0.0
    safe = jnp.where(some, total, 1.0)
    return jnp.where(some, pos0 / safe, 0.5), jnp.where(some, pos1 / safe, 0.5)


def river_shares(permuted_regret):
    pos = jnp.maximum(permuted_regret, 0.0)
    return first_share(pos[:, :C], pos[:, C:])


def turn_shares(permuted_regret):
    pos = jnp.maximum(permuted_regret, 0.0)
    return first_share(pos, pltpu.roll(pos, G, 1))


def strategy_kernel(
    place_ref,
    river_ref,
    turn_ref,
    rperm_ref,
    tperm_ref,
    bucket_ref,
    tbucket_ref,
    out_ref,
    index_ref,
    at_ref,
    tat_ref,
):
    owned, towned = river_ref.shape[0], turn_ref.shape[0]
    rest = owned + towned
    share, _ = river_shares(permuted(river_ref[...], rperm_ref[...], NN))
    tshare, _ = turn_shares(permuted(turn_ref[...], tperm_ref[...], NN))
    for i in range(out_ref.shape[0]):
        out_ref[i, :owned, :] = share
        out_ref[i, owned:, :] = tshare

    turns, rivers, _ = bucket_ref.shape
    index_ref[...] = jnp.zeros_like(index_ref)
    tat_ref[...] = jnp.zeros_like(tat_ref)
    for j in range(HP // 128):
        width = min(128, H - j * 128)
        lanes = slice(j * 128, j * 128 + width)
        for t in range(turns):
            tat_ref[t, j : j + 1, :width] = tbucket_ref[t : t + 1, lanes]
            for r in range(rivers):
                index_ref[t * rivers + r, j : j + 1, :width] = bucket_ref[t, r : r + 1, lanes]

    x, core = place_ref[0], place_ref[1]

    def placed(bucket, count, offset):
        owner = ((bucket.astype(F32) + 0.5) * (1.0 / count)).astype(jnp.int32)
        row = bucket - owner * count
        other = (core - (owner >> 4)) & 1
        slot = (other * 4 + ((x - (owner >> 5)) & 3)) * 16 + (owner & 15)
        return slot * rest + offset + row

    at_ref[...] = placed(index_ref[...], owned, 0)
    tat_ref[...] = placed(tat_ref[...], towned, owned)


def update_kernel(
    scale, each, came_ref, river_ref, turn_ref, rperm_ref, tperm_ref, river_out, turn_out, br_out
):
    turns = br_out.shape[0]
    blocks = HP // 128
    came = came_ref[0]
    for source in range(1, came_ref.shape[0]):
        came = came + came_ref[source]
    for t in range(turns):
        for j in range(blocks):
            row = (t * blocks + j) * each
            width = min(128, H - j * 128)
            br_out[t, :, j * 128 : j * 128 + width] = came[row : row + each, :width]
    at = turns * blocks * each
    rsum = came[at + 4 : at + 4 + river_ref.shape[0]]
    tsum = came[at : at + 4]
    rp = permuted(river_ref[...], rperm_ref[...], NN)
    s0, s1 = river_shares(rp)
    gain = rsum * scale
    new = jnp.maximum(rp + jnp.concatenate([s1 * gain, -(s0 * gain)], axis=1), 0.0)
    river_out[...] = permuted(new, rperm_ref[...], NT)
    tp = permuted(turn_ref[...], tperm_ref[...], NN)
    _, other = turn_shares(tp)
    lane = lax.broadcasted_iota(jnp.int32, tsum.shape, 1)
    swapped = pltpu.roll(tsum, G, 1)
    low = jnp.where(lane < G, tsum, -swapped)
    high = jnp.where(lane < G, swapped, -tsum)
    gain = jnp.concatenate([low, high], axis=0) * scale
    turn_out[...] = permuted(jnp.maximum(tp + other * gain, 0.0), tperm_ref[...], NT)


def stake_rows(pot_ref):
    pot = pot_ref[...]
    lane = lax.broadcasted_iota(jnp.int32, (1, C), 1)
    bet = 0.5 * jnp.concatenate([pot, pot], axis=1) + jnp.where(lane >= G, 2.0, 0.0)
    return bet * (1.0 / H), (bet + 2.0) * (1.0 / H)


def playable(first, second, turn_value, river_value):
    return (
        (first != turn_value)
        & (second != turn_value)
        & (first != river_value)
        & (second != river_value)
    )


def for_each_hand(index_ref, board, body):
    base = board * INDEX_ROW

    def some(i, _):
        for j in range(UNROLL):
            h = i * UNROLL + j
            body(h, index_ref[base + h], j)
        return 0

    lax.fori_loop(0, H // UNROLL, some, 0)


def widen(wide_s, narrow_ref, out_s):
    wide_s[...] = jnp.zeros_like(wide_s)
    wide_s[:G, :H] = narrow_ref[...]
    wide_s[G:, :H] = narrow_ref[...]
    out_s[...] = jnp.transpose(wide_s[...])


def sign_matrix(rank_ref, r, turn_value, river_value, cards_ref, disjoint_ref, rank_s, signed_s):
    out = jnp.logical_not(
        playable(cards_ref[0:1, :], cards_ref[1:2, :], turn_value, river_value)
    )
    rank_s[r : r + 1, :H] = rank_ref[0, r : r + 1, :]
    rank_row = rank_s[r : r + 1, :].astype(F32) + jnp.where(out, RANKS, 0.0)
    rank_col = jnp.transpose(jnp.broadcast_to(rank_row, (128, HP)))
    for j in range(HP // 128):
        lanes = slice(j * 128, (j + 1) * 128)
        more = (rank_col - rank_row[:, lanes]).astype(BF)
        bound = disjoint_ref[:, lanes]
        signed_s[r, :, lanes] = jnp.maximum(jnp.minimum(more, bound), -bound)
    return rank_col < RANKS


def payoff_kernel(
    rivers,
    start,
    tcard_ref,
    rcard_ref,
    rank_ref,
    call_ref,
    opp_ref,
    pot_ref,
    disjoint_ref,
    holds_ref,
    out_of_ref,
    tperm_ref,
    cards_ref,
    *refs,
):
    (
        delta_ref,
        bet_ref,
        rank_s,
        call_s,
        wide_s,
        opp_s,
        show_s,
        signed_s,
    ) = refs[-8:]
    t = pl.program_id(0) + start

    @pl.when(t == start)
    def _():
        rank_s[...] = jnp.zeros_like(rank_s)
        call_s[rivers * H :, :] = jnp.zeros((rivers * (HP - H), C), F32)
        widen(wide_s, opp_ref, opp_s)

    call_s[: rivers * H, :] = lax.dot_general(
        call_ref[0].reshape(rivers * H, C), tperm_ref[...], NN, preferred_element_type=F32
    )
    low, high = stake_rows(pot_ref)
    bets = 0.0
    for r in range(rivers):
        col_ok = sign_matrix(
            rank_ref, r, tcard_ref[t], rcard_ref[r, t], cards_ref, disjoint_ref, rank_s, signed_s
        )
        called = call_s[pl.ds(r, HP, stride=rivers), :]
        theirs = jnp.where(col_ok, opp_s[...], 0.0)
        show_s[r, :, :C] = theirs.astype(BF)
        show_s[r, :, C:] = (theirs * called).astype(BF)
        show = lax.dot_general(signed_s[r], show_s[r], NN, preferred_element_type=F32)
        fold = others((theirs * (1.0 - called)).astype(BF), holds_ref, out_of_ref)
        bet = jnp.where(col_ok, high * show[:, C:] + low * fold, 0.0)
        delta_ref[r] = jnp.where(col_ok, low * show[:, :C], 0.0) - bet
        bets = bets + bet
    bet_ref[0] = bets


def sum_kernel(index_ref, place_ref, delta_ref, mine_ref, theirs_ref, *tables):
    board = pl.program_id(0)

    @pl.when(board == 0)
    def _():
        for table in tables:
            table[...] = jnp.zeros_like(table)

    def add_row(h, k, j):
        table = tables[j % TABLES]
        table[pl.ds(k, 1), :] += delta_ref[0, pl.ds(h, 1), :]

    for_each_hand(index_ref, board, add_row)

    @pl.when(board == pl.num_programs(0) - 1)
    def _():
        core = place_ref[1]
        rows = mine_ref.shape[1]
        for s in range(mine_ref.shape[0]):
            for out_ref, c in ((mine_ref, core), (theirs_ref, 1 - core)):
                at = pl.multiple_of((s * 2 + c) * rows, 8)
                total = tables[0][pl.ds(at, rows), :]
                for table in tables[1:]:
                    total = total + table[pl.ds(at, rows), :]
                out_ref[s] = total


def reply_kernel(
    turns,
    rivers,
    river_total,
    pieces,
    bucket_ref,
    tbucket_ref,
    tcard_ref,
    rcard_ref,
    rank_ref,
    trow_ref,
    delta_ref,
    bet_ref,
    mine_ref,
    pot_ref,
    disjoint_ref,
    holds_ref,
    out_of_ref,
    cards_ref,
    *refs,
):
    piece_refs = refs[:pieces]
    (
        out_ref,
        gain_ref,
        table_s,
        rows_s,
        mine_s,
        wide_s,
        rank_s,
        trow_s,
        col_s,
        reach_s,
        sums_s,
        reply_s,
        sem,
    ) = refs[pieces:]
    t = pl.program_id(0)
    now, later = t % 2, (t + 1) % 2
    kinds = rivers + 1

    def take_rows(first, count, turn, slot):
        for j in range(count):
            h = first + j
            k = tbucket_ref[turn * INDEX_ROW + h]
            rows_s[slot, 0, pl.ds(h, 1), :] = table_s[pl.ds(k, 1), :]
            for r in range(rivers):
                k = bucket_ref[(turn * rivers + r) * INDEX_ROW + h]
                rows_s[slot, r + 1, pl.ds(h, 1), :] = table_s[pl.ds(k, 1), :]

    @pl.when(t == 0)
    def _():
        at, copies = 0, []
        for i, piece in enumerate(piece_refs):
            rows = piece.shape[0]
            copies.append(pltpu.make_async_copy(piece, table_s.at[pl.ds(at, rows)], sem.at[i]))
            copies[-1].start()
            at += rows
        rank_s[...] = jnp.zeros_like(rank_s)
        trow_s[...] = jnp.full_like(trow_s, -1)
        gain_ref[...] = jnp.zeros_like(gain_ref)
        widen(wide_s, mine_ref, mine_s)
        for slot in range(2):
            for kind in range(kinds):
                rows_s[slot, kind, H:, :] = jnp.zeros((HP - H, C), F32)
        for copy in copies:
            copy.wait()

        def some(i, _):
            take_rows(i * UNROLL, UNROLL, 0, 0)
            return 0

        lax.fori_loop(0, H // UNROLL, some, 0)

    low, high = stake_rows(pot_ref)
    reach = mine_s[...] * rows_s[now, 0]
    nodes = bet_ref[0]
    for r in range(rivers):
        first = rows_s[now, r + 1]
        out = jnp.logical_not(
            playable(cards_ref[0:1, :], cards_ref[1:2, :], tcard_ref[t], rcard_ref[r, t])
        )
        rank_s[r : r + 1, :H] = rank_ref[0, r : r + 1, :]
        rank_row = rank_s[r : r + 1, :].astype(F32) + jnp.where(out, RANKS, 0.0)
        col_s[r] = jnp.transpose(jnp.broadcast_to(rank_row, (128, HP)))
        col_ok = col_s[r] < RANKS
        reach_s[r, :, :C] = jnp.where(col_ok, reach * first, 0.0).astype(BF)
        reach_s[r, :, C:] = jnp.where(col_ok, reach * (1.0 - first), 0.0).astype(BF)
        sums = lax.dot_general(
            holds_ref[...], reach_s[r, :, C:], NN, preferred_element_type=F32
        )
        split = parts(sums, 3)
        sums_s[r] = jnp.concatenate(split + [jnp.zeros_like(split[0])], axis=0)
        nodes = nodes + first * delta_ref[r]
    rank_rows = [
        rank_s[r : r + 1, :].astype(F32)
        + jnp.where(
            playable(cards_ref[0:1, :], cards_ref[1:2, :], tcard_ref[t], rcard_ref[r, t]),
            0.0,
            RANKS,
        )
        for r in range(rivers)
    ]

    def some_replies(at, count):
        rows = pl.ds(at, count)
        total = 0.0
        for r in range(rivers):
            col = col_s[r, rows, :]
            signed = []
            for j in range(HP // 128):
                lanes = slice(j * 128, (j + 1) * 128)
                more = (col - rank_rows[r][:, lanes]).astype(BF)
                bound = disjoint_ref[rows, lanes]
                signed.append(jnp.maximum(jnp.minimum(more, bound), -bound))
            against = lax.dot_general(
                jnp.concatenate(signed, axis=1), reach_s[r], NN, preferred_element_type=F32
            )
            against_bet = reach_s[r, rows, C:].astype(F32) + lax.dot_general(
                out_of_ref[rows, :], sums_s[r], NN, preferred_element_type=F32
            )
            reply = low * against[:, :C] + jnp.maximum(
                high * against[:, C:], -(low * against_bet)
            )
            total = total + jnp.where(col < RANKS, reply, 0.0)
        reply_s[rows, :] = total

    chunk = HP // CHUNKS
    taken = -(-H // CHUNKS)

    def with_rows(i, _):
        take_rows(i * taken, taken, t + 1, later)
        some_replies(pl.multiple_of(i * chunk, 128), chunk)
        return 0

    def without_rows(i, _):
        some_replies(pl.multiple_of(i * chunk, 128), chunk)
        return 0

    @pl.when(t < turns - 1)
    def _():
        lax.fori_loop(0, CHUNKS, with_rows, 0)

    @pl.when(t == turns - 1)
    def _():
        lax.fori_loop(0, CHUNKS, without_rows, 0)

    hi, lo = parts(nodes - pltpu.roll(nodes, G, 1), 2)
    both = jnp.concatenate([hi[:, :G], lo[:, :G]], axis=1)
    trow_s[0:1, :H] = trow_ref[pl.ds(t, 1), :]
    trow = trow_s[0:1, :]
    row = lax.broadcasted_iota(jnp.int32, (gain_ref.shape[0], HP), 0)
    bucket = row // 4 * 8 + row % 4

    def sums_of(ids):
        hot = jnp.where(ids == trow, 1.0, 0.0).astype(BF)
        out = lax.dot_general(hot, both, NN, preferred_element_type=F32)
        return out + pltpu.roll(out, G, 1)

    lane = lax.broadcasted_iota(jnp.int32, gain_ref.shape, 1)
    gain_ref[...] += jnp.where(lane < G, sums_of(bucket), sums_of(bucket + 4))

    flat = jnp.transpose(reply_s[...])
    flat = (flat[:G] + flat[G:]) * (1.0 / river_total)
    owners = out_ref.shape[0]
    each = G // owners
    blocks = HP // 128
    for turn in range(turns):

        @pl.when(t == turn)
        def _():
            for j in range(blocks):
                piece = flat[:, j * 128 : (j + 1) * 128].reshape(owners, each, 128)
                row = (turn * blocks + j) * each
                out_ref[:, row : row + each, :] = piece


def shifted(x, axis, shift):
    return lax.ppermute(x, axis, [(i, (i + shift) % 4) for i in range(4)])


def block(x, at):
    return lax.dynamic_index_in_dim(x, at, 0, keepdims=False)


def per_device(
    river_regret,
    turn_regret,
    river_bucket,
    turn_bucket,
    ranks,
    turn_card,
    river_card,
    player_range,
    opp_range,
    call_prob,
    base_pot,
):
    turns, rivers, _ = river_bucket.shape
    boards = turns * rivers
    devices = 128
    owners = 16
    each = G // owners
    river_total = rivers * owners
    owned, towned = river_regret.shape[0], turn_regret.shape[0]
    buckets, tbuckets = owned * devices, towned * devices
    disjoint, holds, out_of, rperm, tperm, cards = constants()
    params = pltpu.CompilerParams(vmem_limit_bytes=VMEM_LIMIT)
    pot = base_pot.reshape(1, G)
    calls = jnp.transpose(call_prob, (0, 3, 1, 2))
    river_at_turn = river_card.T
    place = jnp.stack([lax.axis_index(a) for a in AXES]).astype(jnp.int32)
    rest = owned + towned
    turn_row = turns * (HP // 128) * each
    river_row = turn_row + towned // 2
    sent_rows = river_row + owned
    vmem, smem = (pl.BlockSpec(memory_space=space) for space in (pltpu.VMEM, pltpu.SMEM))

    with jax.named_scope("strategies"):
        strategies, *indices = pl.pallas_call(
            strategy_kernel,
            in_specs=[smem] + [vmem] * 6,
            out_shape=[
                jax.ShapeDtypeStruct((owners, rest, C), F32),
                jax.ShapeDtypeStruct((boards, INDEX_ROW // 128, 128), jnp.int32),
                jax.ShapeDtypeStruct((boards, INDEX_ROW // 128, 128), jnp.int32),
                jax.ShapeDtypeStruct((turns, INDEX_ROW // 128, 128), jnp.int32),
            ],
            compiler_params=params,
            name="strategies",
        )(place, river_regret, turn_regret, rperm, tperm, river_bucket, turn_bucket)
        index, river_at, turn_at = (a.reshape(-1) for a in indices)
        plane = lax.all_to_all(strategies, ("z", "y"), 0, 0).reshape(-1, C)

    def whole(shape):
        return pl.BlockSpec(shape, lambda i, *_: (0,) * len(shape))

    def per_turn(shape, count=1):
        return pl.BlockSpec((count,) + shape, lambda i, *_: (i,) + (0,) * len(shape))

    def per_board(shape):
        return per_turn(shape, rivers)

    def payoffs(start, count, known=()):
        def of_turn(shape, each_turn=1):
            return pl.BlockSpec(
                (each_turn,) + shape, lambda i, *_: (i + start,) + (0,) * len(shape)
            )

        return pl.pallas_call(
            functools.partial(payoff_kernel, rivers, start),
            grid_spec=pltpu.PrefetchScalarGridSpec(
                num_scalar_prefetch=2,
                grid=(count,),
                in_specs=[
                    of_turn((rivers, H)),
                    of_turn((H, rivers, C)),
                    whole((G, H)),
                    whole((1, G)),
                    whole((HP, HP)),
                    whole((64, HP)),
                    whole((HP, 256)),
                    whole((C, C)),
                    whole((8, HP)),
                ]
                + [pl.BlockSpec(memory_space=pl.ANY)] * len(known),
                out_specs=[of_turn((HP, C), rivers), of_turn((HP, C))],
                scratch_shapes=[
                    pltpu.VMEM((8, HP), jnp.int32),
                    pltpu.VMEM((rivers * HP, C), F32),
                    pltpu.VMEM((C, HP), F32),
                    pltpu.VMEM((HP, C), F32),
                    pltpu.VMEM((rivers, HP, 2 * C), BF),
                    pltpu.VMEM((rivers, HP, HP), BF),
                ],
            ),
            out_shape=[
                jax.ShapeDtypeStruct((boards, HP, C), F32),
                jax.ShapeDtypeStruct((turns, HP, C), F32),
            ],
            input_output_aliases={11 + i: i for i in range(len(known))},
            compiler_params=params,
            cost_estimate=pl.CostEstimate(
                flops=count * 8 * 10**9, bytes_accessed=10**6, transcendentals=0
            ),
            name="payoffs",
        )(
            turn_card,
            river_at_turn,
            ranks,
            calls,
            opp_range,
            pot,
            disjoint,
            holds,
            out_of,
            tperm,
            cards,
            *known,
        )

    with jax.named_scope("payoffs"):
        delta, bet = payoffs(0, 1)
    with jax.named_scope("strategies"):
        plane, delta = lax.optimization_barrier((plane, delta))
        up, down = shifted(plane, "x", 1), shifted(plane, "x", 3)
    with jax.named_scope("payoffs"):
        delta, bet = payoffs(1, turns - 1, (delta, bet))
    with jax.named_scope("strategies"):
        up, down, delta = lax.optimization_barrier((up, down, delta))
        far = shifted(up, "x", 1)

    with jax.named_scope("river_sums"):
        mine, theirs = pl.pallas_call(
            sum_kernel,
            grid_spec=pltpu.PrefetchScalarGridSpec(
                num_scalar_prefetch=2,
                grid=(boards,),
                in_specs=[per_turn((HP, C))],
                out_specs=[whole((4, owners * owned, C))] * 2,
                scratch_shapes=[pltpu.VMEM((buckets, C), F32)] * TABLES,
            ),
            out_shape=[jax.ShapeDtypeStruct((4, owners * owned, C), F32)] * 2,
            compiler_params=params,
            cost_estimate=pl.CostEstimate(
                flops=22 * 10**9, bytes_accessed=10**6, transcendentals=0
            ),
            name="sums",
        )(index, place, delta)
        near = [lax.ppermute(piece, "core", [(0, 1), (1, 0)]) for piece in (plane, up, down)]
        far, theirs, *near = lax.optimization_barrier((far, theirs, *near))
        pieces = [plane, up, far, down, near[0], near[1]]
        pieces += [lax.ppermute(far, "core", [(0, 1), (1, 0)]), near[2]]
        got = lax.ppermute(theirs, "core", [(0, 1), (1, 0)])

    with jax.named_scope("river_sums"):
        chip = mine + got
        columns = lax.all_to_all(chip, "x", 0, 0)
        chip, delta = lax.optimization_barrier((chip, delta))

    with jax.named_scope("replies"):
        replies, gains = pl.pallas_call(
            functools.partial(reply_kernel, turns, rivers, river_total, len(pieces)),
            grid_spec=pltpu.PrefetchScalarGridSpec(
                num_scalar_prefetch=4,
                grid=(turns,),
                in_specs=[
                    per_turn((rivers, H)),
                    whole((turns, H)),
                    per_board((HP, C)),
                    per_turn((HP, C)),
                    whole((G, H)),
                    whole((1, G)),
                    whole((HP, HP)),
                    whole((64, HP)),
                    whole((HP, 256)),
                    whole((8, HP)),
                ]
                + [pl.BlockSpec(memory_space=pl.ANY)] * len(pieces),
                out_specs=[
                    whole((owners, sent_rows, 128)),
                    whole((tbuckets // 2, C)),
                ],
                scratch_shapes=[
                    pltpu.VMEM((rest * devices, C), F32),
                    pltpu.VMEM((2, rivers + 1, HP, C), F32),
                    pltpu.VMEM((HP, C), F32),
                    pltpu.VMEM((C, HP), F32),
                    pltpu.VMEM((8, HP), jnp.int32),
                    pltpu.VMEM((8, HP), jnp.int32),
                    pltpu.VMEM((rivers, HP, C), F32),
                    pltpu.VMEM((rivers, HP, 2 * C), BF),
                    pltpu.VMEM((rivers, 256, C), BF),
                    pltpu.VMEM((HP, C), F32),
                    pltpu.SemaphoreType.DMA((len(pieces),)),
                ],
            ),
            out_shape=[
                jax.ShapeDtypeStruct((owners, sent_rows, 128), F32),
                jax.ShapeDtypeStruct((tbuckets // 2, C), F32),
            ],
            compiler_params=params,
            cost_estimate=pl.CostEstimate(
                flops=30 * 10**9, bytes_accessed=10**6, transcendentals=0
            ),
            name="replies",
        )(
            river_at,
            turn_at,
            turn_card,
            river_at_turn,
            ranks,
            turn_bucket,
            delta,
            bet,
            player_range,
            pot,
            disjoint,
            holds,
            out_of,
            cards,
            *pieces,
        )
    with jax.named_scope("turn_sums"):
        x, core = place[0], place[1]
        pairs = gains.reshape(4, 2, -1, C)
        held = lax.dynamic_index_in_dim(pairs, core, 1, keepdims=False)
        lent = lax.dynamic_index_in_dim(pairs, 1 - core, 1, keepdims=False)
        held = held + lax.ppermute(lent, "core", [(0, 1), (1, 0)])
        turn_parts = [block(held, x)]
        turn_parts += [shifted(block(held, (x + s) % 4), "x", s) for s in (2, 1, 3)]

    with jax.named_scope("exchange"):
        replies, columns, turn_parts = lax.optimization_barrier((replies, columns, turn_parts))
        turn_sums, column = sum(turn_parts[1:], turn_parts[0]), columns.sum(0)
        sent = replies.at[:, turn_row:river_row].set(turn_sums.reshape(owners, -1, 128))
        sent = sent.at[:, river_row:].set(column.reshape(owners, -1, 128))
        came = lax.all_to_all(sent, ("z", "y"), 0, 0)

    with jax.named_scope("update"):
        new_river, new_turn, br_value = pl.pallas_call(
            functools.partial(update_kernel, 1.0 / river_total, each),
            out_shape=[
                jax.ShapeDtypeStruct(river_regret.shape, F32),
                jax.ShapeDtypeStruct(turn_regret.shape, F32),
                jax.ShapeDtypeStruct((turns, each, H), F32),
            ],
            compiler_params=params,
            name="update",
        )(came, river_regret, turn_regret, rperm, tperm)
    return new_river, new_turn, br_value


def solution(mesh):
    mesh = Mesh(mesh.devices.reshape(4, 2, 4, 4), AXES)
    turn, river = AXES[:2], AXES[2:]
    placed = (
        P(AXES, None),
        P(AXES, None),
        P(turn, river, None),
        P(turn, None),
        P(turn, river, None),
        P(turn),
        P(turn, river),
        P(),
        P(),
        P(turn, river, None, None),
        P(),
    )
    return jax.shard_map(
        per_device,
        mesh=mesh,
        in_specs=placed,
        out_specs=(P(AXES, None), P(AXES, None), P(turn, river, None)),
        check_vma=False,
    )
```

time: 156 us -> 146 us (0.936)
  Pallas kernels: 77 us -> 71.6 us
  starting transfers between devices: 29.3 us -> 25 us
  local copies, waits for them, and re-layouts: 7.48 us -> 3.76 us
  waiting for transfers between devices: 11 us -> 12.6 us
    pallas_call x2, Pallas kernels: 41.2 us -> 21.1 us  [payoffs(): pl.pallas_call(functools.partial(payoff_kernel, rivers, start), grid_spec...]
    ppermute x16 -> x6, starting transfers between devices: 28 us -> 11.6 us  [shifted(): return lax.ppermute(x, axis, [(i, (i + shift) % 4) for i in range(4)])]
    pallas_call x1, Pallas kernels: 15.6 us -> 30.2 us  [per_device(): pl.pallas_call(functools.partial(reply_kernel, turns, rivers, river_total...]
    all_to_all x0 -> x2, starting transfers between devices: none -> 12.3 us  [the longest x1 8.13 us: per_device(): plane = lax.all_to_all(strategies, ('z', 'y'), 0, 0).reshape(-1, C)]
    all_to_all x0 -> x2, waiting for transfers between devices: none -> 4.18 us  [the longest x1 4.18 us: per_device(): plane = lax.all_to_all(strategies, ('z', 'y'), 0, 0).reshape(-1, C)]
    unnamed x9 -> x10, local copies, waits for them, and re-layouts: 5.2 us -> 1.32 us
    ppermute x16 -> x6, waiting for transfers between devices: 4.94 us -> 2.9 us  [shifted(): return lax.ppermute(x, axis, [(i, (i + shift) % 4) for i in range(4)])]
    ppermute x1, waiting for transfers between devices: 6.08 us -> 4.23 us  [per_device(): got = lax.ppermute(theirs, 'core', [(0, 1), (1, 0)])]
  transfers between devices with their start and end apart: 22 -> 14, of which waited for: 4 -> 6; matrix products, arithmetic and copies ran while one was open for 4% -> 4% of each run, Pallas kernels for 47% -> 46%
where the time goes in v3:
time: 146 us; the launch traced here: 145 us
  Pallas kernels  71.6 us (49%)
  blocking collectives  25.9 us (18%)
  starting transfers between devices  25 us (17%)
  waiting for transfers between devices  12.6 us (9%)
  other arithmetic  5.02 us (3%)
  local copies, waits for them, and re-layouts  3.76 us (3%)
    pallas_call x1, Pallas kernels, per_device(): pl.pallas_call(functools.partial(reply_kernel, turns, rivers, river_total...  30.2 us
    all_to_all x1, blocking collectives, per_device(): came = lax.all_to_all(sent, ('z', 'y'), 0, 0)  25.9 us
    pallas_call x2, Pallas kernels, payoffs(): pl.pallas_call(functools.partial(payoff_kernel, rivers, start), grid_spec...  21.1 us
    pallas_call x1, Pallas kernels, per_device(): pl.pallas_call(sum_kernel, grid_spec=pltpu.PrefetchScalarGridSpec(num_sca...  15.5 us
    ppermute x6, starting transfers between devices, shifted(): return lax.ppermute(x, axis, [(i, (i + shift) % 4) for i in range(4)])  11.6 us
    all_to_all x1, starting transfers between devices, per_device(): plane = lax.all_to_all(strategies, ('z', 'y'), 0, 0).reshape(-1, C)  8.13 us
    ppermute x1, waiting for transfers between devices, per_device(): got = lax.ppermute(theirs, 'core', [(0, 1), (1, 0)])  4.23 us
    all_to_all x1, starting transfers between devices, per_device(): columns = lax.all_to_all(chip, 'x', 0, 0)  4.2 us
  transfers between devices with their start and end apart: 14, of which 6 were waited for; matrix products, arithmetic and copies ran while one was open for 4% of the time, Pallas kernels for 46%

profile of v3, /device:TPU:0, one launch (start us, length us, event | category | flops | bytes accessed | tf_op | source)
XLA Modules:
  0.0 144.7 jit_solution(14463998110130690270)
XLA Ops:
  0.6 0.6 pad_add_fusion.place_ref
  1.3 2.1 %strategies.1 = (f32[16,80,128]{2,1,0:T(8,128)}, s32[6,16,128]{2,1,0:T(8,128)}, s32[6,16,128]{2,1,0:T(8,128)}, s32[3,16,128]{2,1,0:T(8,128)}) custom-call(s32[4]{0:T(128)} %pad_add_fusion.place_ref, f32[72,256]{1,0:T(8,128)} %river_ref.3, f32[8,128]{1,0:T(8,128)} %turn_ref.3, bf16[256,256]{1,0:T(8,128)(2,1)} %constant.130.clone.rperm_ref, ...), custom_call_target="tpu_custom_call" | custom-call | tf_op jit(solution)/shard_map/strategies/strategies/pallas_call | solution.py:532
  3.4 8.1 %all-to-all-start = ((f32[16,80,128]{2,1,0:T(8,128)}), f32[16,80,128]{2,1,0:T(8,128)S(1)}, u32[]{:S(2)}, u32[]{:S(2)}) async-start(f32[16,80,128]{2,1,0:T(8,128)} %get-tuple-element.59), calls=%async_computation | async-start | bytes 1310720 | tf_op jit(solution)/shard_map/strategies/all_to_all | solution.py:545
  11.5 8.8 %payoffs.2 = (f32[6,1152,128]{2,1,0:T(8,128)}, f32[3,1152,128]{2,1,0:T(8,128)}) custom-call(s32[3]{0:T(128)} %tcard_ref.5, s32[2,3]{1,0:T(2,128)} %bitcast.39, s32[3,2,1081]{2,1,0:T(2,128)} %rank_ref.5, bf16[3,1081,2,128]{3,2,1,0:T(2,128)(2,1)} %bitcast.34, f32[64,1081]{1,0:T(8,128)} %opp_ref.3, f32[1,64]{1,0:T(1,128)} %bitcast.42, ...), custom_call_target="tpu_custom_call" | custom-call | flops 8000000000 | bytes 1000000 | tf_op jit(solution)/shard_map/payoffs/payoffs/pallas_call | solution.py:562
  20.3 4.2 %all-to-all-done = f32[16,80,128]{2,1,0:T(8,128)S(1)} async-done(((f32[16,80,128]{2,1,0:T(8,128)}), f32[16,80,128]{2,1,0:T(8,128)S(1)}, u32[]{:S(2)}, u32[]{:S(2)}) %all-to-all-start) | async-done | bytes 655392 | tf_op jit(solution)/shard_map/strategies/all_to_all | solution.py:545
  24.5 1.5 %collective-permute-start = (f32[1280,128]{1,0:T(8,128)S(1)}, f32[1280,128]{1,0:T(8,128)S(1)}, u32[]{:S(2)}, u32[]{:S(2)}) collective-permute-start(f32[1280,128]{1,0:T(8,128)S(1)} %bitcast.27), channel_id=1, source_target_pairs={{0,32},{32,64},{64,96},{96,0},{1,33},{33,65},{65,97},{97,1},{2,34}... | collective-permute-start | bytes 1966088 | tf_op jit(solution)/shard_map/strategies/ppermute | solution.py:491
  26.0 1.7 %collective-permute-start.1 = (f32[1280,128]{1,0:T(8,128)S(1)}, f32[1280,128]{1,0:T(8,128)S(1)}, u32[]{:S(2)}, u32[]{:S(2)}) collective-permute-start(f32[1280,128]{1,0:T(8,128)S(1)} %bitcast.28), channel_id=1, source_target_pairs={{0,96},{32,0},{64,32},{96,64},{1,97},{33,1},{65,33},{97,65},{2,98}... | collective-permute-start | bytes 1966088 | tf_op jit(solution)/shard_map/strategies/ppermute | solution.py:491
  27.7 12.4 %payoffs.3 = (f32[6,1152,128]{2,1,0:T(8,128)}, f32[3,1152,128]{2,1,0:T(8,128)}) custom-call(s32[3]{0:T(128)} %tcard_ref.5, s32[2,3]{1,0:T(2,128)} %bitcast.40, s32[3,2,1081]{2,1,0:T(2,128)} %rank_ref.5, bf16[3,1081,2,128]{3,2,1,0:T(2,128)(2,1)} %bitcast.35, f32[64,1081]{1,0:T(8,128)} %opp_ref.3, ...), custom_call_target="tpu_custom_call", output_to_operand_aliasing={{0}: (11, {}), {1}: (12, {})} | custom-call | flops 16000000000 | bytes 1000000 | tf_op jit(solution)/shard_map/payoffs/payoffs/pallas_call | solution.py:562
  40.1 0.6 collective-permute-done.refs_1_
  40.7 1.5 %collective-permute-start.2 = (f32[1280,128]{1,0:T(8,128)S(1)}, f32[1280,128]{1,0:T(8,128)}, u32[]{:S(2)}, u32[]{:S(2)}) collective-permute-start(f32[1280,128]{1,0:T(8,128)S(1)} %collective-permute-done.refs_1_), channel_id=1, source_target_pairs={{0,32},{32,64},{64,96},{96,0},{1,33},{33,65},{65,97},{97,1},{2,34}... | collective-permute-start | bytes 1966088 | tf_op jit(solution)/shard_map/strategies/ppermute | solution.py:491
  42.2 0.5 collective-permute-start.5
  42.7 15.5 %sums.1 = (f32[4,1152,128]{2,1,0:T(8,128)}, f32[4,1152,128]{2,1,0:T(8,128)}) custom-call(s32[12288]{0:T(1024)} %bitcast.37, s32[4]{0:T(128)} %pad_add_fusion.place_ref, f32[6,1152,128]{2,1,0:T(8,128)} %get-tuple-element.71.delta_ref), custom_call_target="tpu_custom_call" | custom-call | flops 22000001024 | bytes 1000000 | tf_op jit(solution)/shard_map/river_sums/sums/pallas_call | solution.py:626
  58.3 0.4 collective-permute-done.2.refs_2_
  58.7 0.4 copy-done.3
  59.1 0.5 collective-permute-start.7
  59.6 4.2 %collective-permute-done.6 = f32[4,1152,128]{2,1,0:T(8,128)S(1)} collective-permute-done((f32[4,1152,128]{2,1,0:T(8,128)}, f32[4,1152,128]{2,1,0:T(8,128)S(1)}, u32[]{:S(2)}, u32[]{:S(2)}) %collective-permute-start.6) | collective-permute-done | bytes 2359328 | tf_op jit(solution)/shard_map/river_sums/ppermute | solution.py:646
  63.9 3.3 %add.59 = f32[4,1152,128]{2,1,0:T(8,128)} add(f32[4,1152,128]{2,1,0:T(8,128)} %get-tuple-element.66, f32[4,1152,128]{2,1,0:T(8,128)S(1)} %collective-permute-done.6) | non-fusion elementwise | flops 589824 | bytes 7077888 | tf_op jit(solution)/shard_map/river_sums/add | solution.py:649
  67.2 4.2 %all-to-all-start.1 = ((f32[4,1152,128]{2,1,0:T(8,128)}), f32[4,1152,128]{2,1,0:T(8,128)S(1)}, u32[]{:S(2)}, u32[]{:S(2)}) async-start(f32[4,1152,128]{2,1,0:T(8,128)} %add.59), calls=%async_computation.1 | async-start | bytes 4718592 | tf_op jit(solution)/shard_map/river_sums/all_to_all | solution.py:650
  71.4 0.9 copy-done.4
  72.2 30.2 %replies.1 = (f32[16,184,128]{2,1,0:T(8,128)}, f32[512,128]{1,0:T(8,128)}) custom-call(s32[12288]{0:T(1024)} %bitcast.36, s32[6144]{0:T(1024)} %bitcast.38, s32[3]{0:T(128)} %tcard_ref.5, s32[2,3]{1,0:T(2,128)} %bitcast.41, s32[3,2,1081]{2,1,0:T(2,128)} %rank_ref.5, s32[3,1081]{1,0:T(4,128)} %trow_ref.1, f32[6,1152,128]{2,1,0:T(8,128)} %get-tuple-element.71.delta_ref, ...), custom_call_target="tpu_custom_call" | custom-call | flops 30000001024 | bytes 1000000 | tf_op jit(solution)/shard_map/replies/replies/pallas_call | solution.py:654
  102.4 0.9 dynamic-slice_bitcast_fusion
  103.5 1.3 collective-permute-done.8
  104.8 0.9 bitcast_add_fusion
  105.7 3.6 %collective-permute-start.9 = (f32[64,128]{1,0:T(8,128)S(1)}, f32[64,128]{1,0:T(8,128)S(1)}, u32[]{:S(2)}, u32[]{:S(2)}) collective-permute-start(f32[64,128]{1,0:T(8,128)S(1)} %get-tuple-element.87), channel_id=1, source_target_pairs={{0,64},{32,96},{64,0},{96,32},{1,65},{33,97},{65,1},{97,33},{2,66}... | collective-permute-start | bytes 98312 | tf_op jit(solution)/shard_map/turn_sums/ppermute | solution.py:491
  109.3 0.6 collective-permute-start.10
  109.9 2.7 %collective-permute-start.11 = (f32[64,128]{1,0:T(8,128)S(1)}, f32[64,128]{1,0:T(8,128)S(1)}, u32[]{:S(2)}, u32[]{:S(2)}) collective-permute-start(f32[64,128]{1,0:T(8,128)S(1)} %get-tuple-element.85), channel_id=1, source_target_pairs={{0,96},{32,0},{64,32},{96,64},{1,97},{33,1},{65,33},{97,65},{2,98}... | collective-permute-start | bytes 98312 | tf_op jit(solution)/shard_map/turn_sums/ppermute | solution.py:491
  112.6 1.9 %collective-permute-done.10 = f32[64,128]{1,0:T(8,128)S(1)} collective-permute-done((f32[64,128]{1,0:T(8,128)S(1)}, f32[64,128]{1,0:T(8,128)S(1)}, u32[]{:S(2)}, u32[]{:S(2)}) %collective-permute-start.10) | collective-permute-done | bytes 32800 | tf_op jit(solution)/shard_map/turn_sums/ppermute | solution.py:491
  114.5 0.6 constant_dynamic-update-slice_fusion.1
  115.1 0.2 reduce_sum.9
  115.3 0.9 constant_dynamic-update-slice_fusion
  116.1 25.9 %all_to_all.15.came_ref = f32[16,184,128]{2,1,0:T(8,128)} all-to-all(f32[16,184,128]{2,1,0:T(8,128)} %constant_dynamic-update-slice_fusion), channel_id=1, replica_groups=mesh['x'=4,'core'=2,'z'=4,'y'=4] {'z','y'}, dimensions={0} | all-to-all | bytes 3014656 | tf_op jit(solution)/shard_map/exchange/all_to_all | solution.py:730
  142.0 2.7 %update.1 = (f32[72,256]{1,0:T(8,128)}, f32[8,128]{1,0:T(8,128)}, f32[3,4,1081]{2,1,0:T(4,128)}) custom-call(f32[16,184,128]{2,1,0:T(8,128)} %all_to_all.15.came_ref, f32[72,256]{1,0:T(8,128)} %river_ref.3, f32[8,128]{1,0:T(8,128)} %turn_ref.3, bf16[256,256]{1,0:T(8,128)(2,1)} %constant.130.clone.rperm_ref, bf16[128,128]{1,0:T(8,128)(2,1)} %constant.131.clone.tperm_ref), custom_call_target="tpu_custom_call" | custom-call | tf_op jit(solution)/shard_map/update/update/pallas_call | solution.py:733
  (22 shorter events, 0.2 us)
Async XLA Ops:
  3.4 21.1 %all-to-all-start = ((f32[16,80,128]{2,1,0:T(8,128)}), f32[16,80,128]{2,1,0:T(8,128)S(1)}, u32[]{:S(2)}, u32[]{:S(2)}) async-start(f32[16,80,128]{2,1,0:T(8,128)} %get-tuple-element.59), calls=%async_computation | async-start | bytes 1310720 | tf_op jit(solution)/shard_map/strategies/all_to_all | solution.py:545
  24.5 15.6 %copy-start = (f32[16,80,128]{2,1,0:T(8,128)}, f32[16,80,128]{2,1,0:T(8,128)S(1)}, u32[]{:S(2)}) copy-start(f32[16,80,128]{2,1,0:T(8,128)S(1)} %all-to-all-done) | copy-start | bytes 1966084
  24.5 16.2 %collective-permute-start = (f32[1280,128]{1,0:T(8,128)S(1)}, f32[1280,128]{1,0:T(8,128)S(1)}, u32[]{:S(2)}, u32[]{:S(2)}) collective-permute-start(f32[1280,128]{1,0:T(8,128)S(1)} %bitcast.27), channel_id=1, source_target_pairs={{0,32},{32,64},{64,96},{96,0},{1,33},{33,65},{65,97},{97,1},{2,34}... | collective-permute-start | bytes 1966088 | tf_op jit(solution)/shard_map/strategies/ppermute | solution.py:491
  26.0 14.8 %collective-permute-start.1 = (f32[1280,128]{1,0:T(8,128)S(1)}, f32[1280,128]{1,0:T(8,128)S(1)}, u32[]{:S(2)}, u32[]{:S(2)}) collective-permute-start(f32[1280,128]{1,0:T(8,128)S(1)} %bitcast.28), channel_id=1, source_target_pairs={{0,96},{32,0},{64,32},{96,64},{1,97},{33,1},{65,33},{97,65},{2,98}... | collective-permute-start | bytes 1966088 | tf_op jit(solution)/shard_map/strategies/ppermute | solution.py:491
  27.7 30.5 %collective-permute-start.3 = (f32[1280,128]{1,0:T(8,128)S(1)}, f32[1280,128]{1,0:T(8,128)S(1)}, u32[]{:S(2)}, u32[]{:S(2)}) collective-permute-start(f32[1280,128]{1,0:T(8,128)S(1)} %bitcast.29), channel_id=1, source_target_pairs={{0,16},{16,0},{1,17},{17,1},{2,18},{18,2},{3,19},{19,3},{4,20},{20... | collective-permute-start | bytes 1966088 | tf_op jit(solution)/shard_map/river_sums/ppermute | solution.py:642
  40.7 17.5 %copy-start.1 = (f32[1280,128]{1,0:T(8,128)}, f32[1280,128]{1,0:T(8,128)S(1)}, u32[]{:S(2)}) copy-start(f32[1280,128]{1,0:T(8,128)S(1)} %collective-permute-done.refs_1_) | copy-start | bytes 1966084
  40.7 17.5 %copy-start.2 = (f32[1280,128]{1,0:T(8,128)}, f32[1280,128]{1,0:T(8,128)S(1)}, u32[]{:S(2)}) copy-start(f32[1280,128]{1,0:T(8,128)S(1)} %collective-permute-done.1.refs_3_) | copy-start | bytes 1966084
  40.7 18.0 %collective-permute-start.2 = (f32[1280,128]{1,0:T(8,128)S(1)}, f32[1280,128]{1,0:T(8,128)}, u32[]{:S(2)}, u32[]{:S(2)}) collective-permute-start(f32[1280,128]{1,0:T(8,128)S(1)} %collective-permute-done.refs_1_), channel_id=1, source_target_pairs={{0,32},{32,64},{64,96},{96,0},{1,33},{33,65},{65,97},{97,1},{2,34}... | collective-permute-start | bytes 1966088 | tf_op jit(solution)/shard_map/strategies/ppermute | solution.py:491
  42.2 16.5 %collective-permute-start.4 = (f32[1280,128]{1,0:T(8,128)S(1)}, f32[1280,128]{1,0:T(8,128)}, u32[]{:S(2)}, u32[]{:S(2)}) collective-permute-start(f32[1280,128]{1,0:T(8,128)S(1)} %collective-permute-done.refs_1_), channel_id=1, source_target_pairs={{0,16},{16,0},{1,17},{17,1},{2,18},{18,2},{3,19},{19,3},{4,20},{20... | collective-permute-start | bytes 1966088 | tf_op jit(solution)/shard_map/river_sums/ppermute | solution.py:642
  42.2 16.5 %collective-permute-start.5 = (f32[1280,128]{1,0:T(8,128)S(1)}, f32[1280,128]{1,0:T(8,128)}, u32[]{:S(2)}, u32[]{:S(2)}) collective-permute-start(f32[1280,128]{1,0:T(8,128)S(1)} %collective-permute-done.1.refs_3_), channel_id=1, source_target_pairs={{0,16},{16,0},{1,17},{17,1},{2,18},{18,2},{3,19},{19,3},{4,20},{20... | collective-permute-start | bytes 1966088 | tf_op jit(solution)/shard_map/river_sums/ppermute | solution.py:642
  58.3 0.9 copy-start.3
  59.1 4.7 %collective-permute-start.6 = (f32[4,1152,128]{2,1,0:T(8,128)}, f32[4,1152,128]{2,1,0:T(8,128)S(1)}, u32[]{:S(2)}, u32[]{:S(2)}) collective-permute-start(f32[4,1152,128]{2,1,0:T(8,128)} %get-tuple-element.70), channel_id=1, source_target_pairs={{0,16},{16,0},{1,17},{17,1},{2,18},{18,2},{3,19},{19,3},{4,20},{20... | collective-permute-start | bytes 7077896 | tf_op jit(solution)/shard_map/river_sums/ppermute | solution.py:646
  59.1 12.2 %collective-permute-start.7 = (f32[1280,128]{1,0:T(8,128)}, f32[1280,128]{1,0:T(8,128)S(1)}, u32[]{:S(2)}, u32[]{:S(2)}) collective-permute-start(f32[1280,128]{1,0:T(8,128)} %collective-permute-done.2.refs_2_), channel_id=1, source_target_pairs={{0,16},{16,0},{1,17},{17,1},{2,18},{18,2},{3,19},{19,3},{4,20},{20... | collective-permute-start | bytes 1966088 | tf_op jit(solution)/shard_map/river_sums/ppermute | solution.py:645
  67.2 47.3 %all-to-all-start.1 = ((f32[4,1152,128]{2,1,0:T(8,128)}), f32[4,1152,128]{2,1,0:T(8,128)S(1)}, u32[]{:S(2)}, u32[]{:S(2)}) async-start(f32[4,1152,128]{2,1,0:T(8,128)} %add.59), calls=%async_computation.1 | async-start | bytes 4718592 | tf_op jit(solution)/shard_map/river_sums/all_to_all | solution.py:650
  71.4 0.9 copy-start.4
  103.3 1.4 collective-permute-start.8
  105.7 6.9 %collective-permute-start.9 = (f32[64,128]{1,0:T(8,128)S(1)}, f32[64,128]{1,0:T(8,128)S(1)}, u32[]{:S(2)}, u32[]{:S(2)}) collective-permute-start(f32[64,128]{1,0:T(8,128)S(1)} %get-tuple-element.87), channel_id=1, source_target_pairs={{0,64},{32,96},{64,0},{96,32},{1,65},{33,97},{65,1},{97,33},{2,66}... | collective-permute-start | bytes 98312 | tf_op jit(solution)/shard_map/turn_sums/ppermute | solution.py:491
  109.3 5.1 %collective-permute-start.10 = (f32[64,128]{1,0:T(8,128)S(1)}, f32[64,128]{1,0:T(8,128)S(1)}, u32[]{:S(2)}, u32[]{:S(2)}) collective-permute-start(f32[64,128]{1,0:T(8,128)S(1)} %get-tuple-element.86), channel_id=1, source_target_pairs={{0,32},{32,64},{64,96},{96,0},{1,33},{33,65},{65,97},{97,1},{2,34}... | collective-permute-start | bytes 98312 | tf_op jit(solution)/shard_map/turn_sums/ppermute | solution.py:491
  109.9 4.6 %collective-permute-start.11 = (f32[64,128]{1,0:T(8,128)S(1)}, f32[64,128]{1,0:T(8,128)S(1)}, u32[]{:S(2)}, u32[]{:S(2)}) collective-permute-start(f32[64,128]{1,0:T(8,128)S(1)} %get-tuple-element.85), channel_id=1, source_target_pairs={{0,96},{32,0},{64,32},{96,64},{1,97},{33,1},{65,33},{97,65},{2,98}... | collective-permute-start | bytes 98312 | tf_op jit(solution)/shard_map/turn_sums/ppermute | solution.py:491

commit v4 on v3

--- a/solution.py
+++ b/solution.py
@@ -103,7 +103,6 @@
 
 
 def strategy_kernel(
-    place_ref,
     river_ref,
     turn_ref,
     rperm_ref,
@@ -134,7 +133,7 @@
             for r in range(rivers):
                 index_ref[t * rivers + r, j : j + 1, :width] = bucket_ref[t, r : r + 1, lanes]
 
-    x, core = place_ref[0], place_ref[1]
+    x, core = lax.axis_index("x"), lax.axis_index("core")
 
     def placed(bucket, count, offset):
         owner = ((bucket.astype(F32) + 0.5) * (1.0 / count)).astype(jnp.int32)
@@ -283,7 +282,7 @@
     bet_ref[0] = bets
 
 
-def sum_kernel(index_ref, place_ref, delta_ref, mine_ref, theirs_ref, *tables):
+def sum_kernel(index_ref, delta_ref, mine_ref, theirs_ref, *tables):
     board = pl.program_id(0)
 
     @pl.when(board == 0)
@@ -299,7 +298,7 @@
 
     @pl.when(board == pl.num_programs(0) - 1)
     def _():
-        core = place_ref[1]
+        core = lax.axis_index("core")
         rows = mine_ref.shape[1]
         for s in range(mine_ref.shape[0]):
             for out_ref, c in ((mine_ref, core), (theirs_ref, 1 - core)):
@@ -334,6 +333,8 @@
     piece_refs = refs[:pieces]
     (
         out_ref,
+        held_ref,
+        lent_ref,
         gain_ref,
         table_s,
         rows_s,
@@ -472,6 +473,15 @@
     lane = lax.broadcasted_iota(jnp.int32, gain_ref.shape, 1)
     gain_ref[...] += jnp.where(lane < G, sums_of(bucket), sums_of(bucket + 4))
 
+    @pl.when(t == turns - 1)
+    def _():
+        x, core = lax.axis_index("x"), lax.axis_index("core")
+        ring, count, _ = held_ref.shape
+        for s in range(ring):
+            for part_ref, c in ((held_ref, core), (lent_ref, 1 - core)):
+                at = pl.multiple_of((((x + s) & 3) * 2 + c) * count, 8)
+                part_ref[s] = gain_ref[pl.ds(at, count), :]
+
     flat = jnp.transpose(reply_s[...])
     flat = (flat[:G] + flat[G:]) * (1.0 / river_total)
     owners = out_ref.shape[0]
@@ -489,10 +499,6 @@
 
 def shifted(x, axis, shift):
     return lax.ppermute(x, axis, [(i, (i + shift) % 4) for i in range(4)])
-
-
-def block(x, at):
-    return lax.dynamic_index_in_dim(x, at, 0, keepdims=False)
 
 
 def per_device(
@@ -521,17 +527,15 @@
     pot = base_pot.reshape(1, G)
     calls = jnp.transpose(call_prob, (0, 3, 1, 2))
     river_at_turn = river_card.T
-    place = jnp.stack([lax.axis_index(a) for a in AXES]).astype(jnp.int32)
     rest = owned + towned
+    swap = [(0, 1), (1, 0)]
     turn_row = turns * (HP // 128) * each
     river_row = turn_row + towned // 2
     sent_rows = river_row + owned
-    vmem, smem = (pl.BlockSpec(memory_space=space) for space in (pltpu.VMEM, pltpu.SMEM))
 
     with jax.named_scope("strategies"):
         strategies, *indices = pl.pallas_call(
             strategy_kernel,
-            in_specs=[smem] + [vmem] * 6,
             out_shape=[
                 jax.ShapeDtypeStruct((owners, rest, C), F32),
                 jax.ShapeDtypeStruct((boards, INDEX_ROW // 128, 128), jnp.int32),
@@ -540,7 +544,7 @@
             ],
             compiler_params=params,
             name="strategies",
-        )(place, river_regret, turn_regret, rperm, tperm, river_bucket, turn_bucket)
+        )(river_regret, turn_regret, rperm, tperm, river_bucket, turn_bucket)
         index, river_at, turn_at = (a.reshape(-1) for a in indices)
         plane = lax.all_to_all(strategies, ("z", "y"), 0, 0).reshape(-1, C)
 
@@ -612,21 +616,16 @@
         )
 
     with jax.named_scope("payoffs"):
-        delta, bet = payoffs(0, 1)
+        delta, bet = payoffs(0, turns)
     with jax.named_scope("strategies"):
         plane, delta = lax.optimization_barrier((plane, delta))
         up, down = shifted(plane, "x", 1), shifted(plane, "x", 3)
-    with jax.named_scope("payoffs"):
-        delta, bet = payoffs(1, turns - 1, (delta, bet))
-    with jax.named_scope("strategies"):
-        up, down, delta = lax.optimization_barrier((up, down, delta))
-        far = shifted(up, "x", 1)
 
     with jax.named_scope("river_sums"):
         mine, theirs = pl.pallas_call(
             sum_kernel,
             grid_spec=pltpu.PrefetchScalarGridSpec(
-                num_scalar_prefetch=2,
+                num_scalar_prefetch=1,
                 grid=(boards,),
                 in_specs=[per_turn((HP, C))],
                 out_specs=[whole((4, owners * owned, C))] * 2,
@@ -638,20 +637,20 @@
                 flops=22 * 10**9, bytes_accessed=10**6, transcendentals=0
             ),
             name="sums",
-        )(index, place, delta)
-        near = [lax.ppermute(piece, "core", [(0, 1), (1, 0)]) for piece in (plane, up, down)]
-        far, theirs, *near = lax.optimization_barrier((far, theirs, *near))
-        pieces = [plane, up, far, down, near[0], near[1]]
-        pieces += [lax.ppermute(far, "core", [(0, 1), (1, 0)]), near[2]]
-        got = lax.ppermute(theirs, "core", [(0, 1), (1, 0)])
-
-    with jax.named_scope("river_sums"):
+        )(index, delta)
+        up, down, theirs = lax.optimization_barrier((up, down, theirs))
+        got = lax.ppermute(theirs, "core", swap)
+        half = up.shape[0] // 2
+        far = [shifted(up[:half], "x", 1), shifted(down[half:], "x", 3)]
         chip = mine + got
+        chip, *far = lax.optimization_barrier((chip, *far))
         columns = lax.all_to_all(chip, "x", 0, 0)
-        chip, delta = lax.optimization_barrier((chip, delta))
+        own = [plane, up, *far, down]
+        pieces = own + [lax.ppermute(piece, "core", swap) for piece in own]
+        delta, chip, *pieces = lax.optimization_barrier((delta, chip, *pieces))
 
     with jax.named_scope("replies"):
-        replies, gains = pl.pallas_call(
+        replies, held, lent = pl.pallas_call(
             functools.partial(reply_kernel, turns, rivers, river_total, len(pieces)),
             grid_spec=pltpu.PrefetchScalarGridSpec(
                 num_scalar_prefetch=4,
@@ -671,9 +670,11 @@
                 + [pl.BlockSpec(memory_space=pl.ANY)] * len(pieces),
                 out_specs=[
                     whole((owners, sent_rows, 128)),
-                    whole((tbuckets // 2, C)),
+                    whole((4, owners * towned // 2, C)),
+                    whole((4, owners * towned // 2, C)),
                 ],
                 scratch_shapes=[
+                    pltpu.VMEM((tbuckets // 2, C), F32),
                     pltpu.VMEM((rest * devices, C), F32),
                     pltpu.VMEM((2, rivers + 1, HP, C), F32),
                     pltpu.VMEM((HP, C), F32),
@@ -689,7 +690,8 @@
             ),
             out_shape=[
                 jax.ShapeDtypeStruct((owners, sent_rows, 128), F32),
-                jax.ShapeDtypeStruct((tbuckets // 2, C), F32),
+                jax.ShapeDtypeStruct((4, owners * towned // 2, C), F32),
+                jax.ShapeDtypeStruct((4, owners * towned // 2, C), F32),
             ],
             compiler_params=params,
             cost_estimate=pl.CostEstimate(
@@ -714,13 +716,8 @@
             *pieces,
         )
     with jax.named_scope("turn_sums"):
-        x, core = place[0], place[1]
-        pairs = gains.reshape(4, 2, -1, C)
-        held = lax.dynamic_index_in_dim(pairs, core, 1, keepdims=False)
-        lent = lax.dynamic_index_in_dim(pairs, 1 - core, 1, keepdims=False)
-        held = held + lax.ppermute(lent, "core", [(0, 1), (1, 0)])
-        turn_parts = [block(held, x)]
-        turn_parts += [shifted(block(held, (x + s) % 4), "x", s) for s in (2, 1, 3)]
+        held = held + lax.ppermute(lent, "core", swap)
+        turn_parts = [held[0]] + [shifted(held[s], "x", s) for s in (2, 1, 3)]
 
     with jax.named_scope("exchange"):
         replies, columns, turn_parts = lax.optimization_barrier((replies, columns, turn_parts))

time: 146 us -> 141 us (0.966)
  waiting for transfers between devices: 12.6 us -> 6.84 us
  Pallas kernels: 71.6 us -> 67.5 us
  blocking collectives: 25.9 us -> 28.8 us
  starting transfers between devices: 25 us -> 27.9 us
    pallas_call x2 -> x1, Pallas kernels: 21.1 us -> 16.4 us  [payoffs(): pl.pallas_call(functools.partial(payoff_kernel, rivers, start), grid_spec...]
    all_to_all x1, waiting for transfers between devices: 4.18 us -> 0.01 us  [per_device(): plane = lax.all_to_all(strategies, ('z', 'y'), 0, 0).reshape(-1, C)]
    ppermute x6 -> x7, waiting for transfers between devices: 5.53 us -> 1.56 us  [the longest x1 1.55 us: per_device(): held = held + lax.ppermute(lent, 'core', swap)]
    all_to_all x1, blocking collectives: 25.9 us -> 28.8 us  [per_device(): came = lax.all_to_all(sent, ('z', 'y'), 0, 0)]
    ppermute x6 -> x7, waiting for transfers between devices: 2.9 us -> 5.28 us  [shifted(): return lax.ppermute(x, axis, [(i, (i + shift) % 4) for i in range(4)])]
    slice x0 -> x2, local copies, waits for them, and re-layouts: none -> 1.99 us  [per_device(): far = [shifted(up[:half], 'x', 1), shifted(down[half:], 'x', 3)]]
    ppermute x6 -> x7, starting transfers between devices: 11.6 us -> 13.5 us  [shifted(): return lax.ppermute(x, axis, [(i, (i + shift) % 4) for i in range(4)])]
  transfers between devices with their start and end apart: 14 -> 16, of which waited for: 6 -> 4; matrix products, arithmetic and copies ran while one was open for 4% -> 5% of each run, Pallas kernels for 46% -> 45%
where the time goes in v4:
time: 141 us; the launch traced here: 140 us
  Pallas kernels  67.5 us (48%)
  blocking collectives  28.8 us (20%)
  starting transfers between devices  27.9 us (20%)
  waiting for transfers between devices  6.84 us (5%)
  other arithmetic  4.55 us (3%)
  local copies, waits for them, and re-layouts  3.51 us (2%)
    pallas_call x1, Pallas kernels, per_device(): pl.pallas_call(functools.partial(reply_kernel, turns, rivers, river_total...  30.8 us
    all_to_all x1, blocking collectives, per_device(): came = lax.all_to_all(sent, ('z', 'y'), 0, 0)  28.8 us
    pallas_call x1, Pallas kernels, payoffs(): pl.pallas_call(functools.partial(payoff_kernel, rivers, start), grid_spec...  16.4 us
    pallas_call x1, Pallas kernels, per_device(): pl.pallas_call(sum_kernel, grid_spec=pltpu.PrefetchScalarGridSpec(num_sca...  15.5 us
    ppermute x7, starting transfers between devices, shifted(): return lax.ppermute(x, axis, [(i, (i + shift) % 4) for i in range(4)])  13.5 us
    all_to_all x1, starting transfers between devices, per_device(): plane = lax.all_to_all(strategies, ('z', 'y'), 0, 0).reshape(-1, C)  8.13 us
    ppermute x7, waiting for transfers between devices, shifted(): return lax.ppermute(x, axis, [(i, (i + shift) % 4) for i in range(4)])  5.28 us
    all_to_all x1, starting transfers between devices, per_device(): columns = lax.all_to_all(chip, 'x', 0, 0)  5.07 us
  transfers between devices with their start and end apart: 16, of which 4 were waited for; matrix products, arithmetic and copies ran while one was open for 5% of the time, Pallas kernels for 45%

profile of v4, /device:TPU:0, one launch (start us, length us, event | category | flops | bytes accessed | tf_op | source)
XLA Modules:
  0.0 139.9 jit_solution(10285158242338091490)
XLA Ops:
  0.6 2.1 %strategies.1 = (f32[16,80,128]{2,1,0:T(8,128)}, s32[6,16,128]{2,1,0:T(8,128)}, s32[6,16,128]{2,1,0:T(8,128)}, s32[3,16,128]{2,1,0:T(8,128)}) custom-call(f32[72,256]{1,0:T(8,128)} %river_ref.3, f32[8,128]{1,0:T(8,128)} %turn_ref.3, bf16[256,256]{1,0:T(8,128)(2,1)} %constant.71.clone.rperm_ref, bf16[128,128]{1,0:T(8,128)(2,1)} %constant.72.clone.tperm_ref, ...), custom_call_target="tpu_custom_call" | custom-call | tf_op jit(solution)/shard_map/strategies/strategies/pallas_call | solution.py:537
  2.8 8.1 %all-to-all-start = ((f32[16,80,128]{2,1,0:T(8,128)}), f32[16,80,128]{2,1,0:T(8,128)S(1)}, u32[]{:S(2)}, u32[]{:S(2)}) async-start(f32[16,80,128]{2,1,0:T(8,128)} %get-tuple-element.65), calls=%async_computation | async-start | bytes 1310720 | tf_op jit(solution)/shard_map/strategies/all_to_all | solution.py:549
  10.9 16.4 %payoffs.1 = (f32[6,1152,128]{2,1,0:T(8,128)}, f32[3,1152,128]{2,1,0:T(8,128)}) custom-call(s32[3]{0:T(128)} %tcard_ref.3, s32[2,3]{1,0:T(2,128)} %bitcast.27, s32[3,2,1081]{2,1,0:T(2,128)} %rank_ref.3, bf16[3,1081,2,128]{3,2,1,0:T(2,128)(2,1)} %bitcast.23, f32[64,1081]{1,0:T(8,128)} %opp_ref.1, f32[1,64]{1,0:T(1,128)} %bitcast.29, ...), custom_call_target="tpu_custom_call" | custom-call | flops 24000000000 | bytes 1000000 | tf_op jit(solution)/shard_map/payoffs/payoffs/pallas_call | solution.py:566
  27.3 0.0 all-to-all-done
  27.3 1.6 %collective-permute-start = (f32[1280,128]{1,0:T(8,128)S(1)}, f32[1280,128]{1,0:T(8,128)}, u32[]{:S(2)}, u32[]{:S(2)}) collective-permute-start(f32[1280,128]{1,0:T(8,128)S(1)} %bitcast.18), channel_id=1, source_target_pairs={{0,32},{32,64},{64,96},{96,0},{1,33},{33,65},{65,97},{97,1},{2,34}... | collective-permute-start | bytes 1966088 | tf_op jit(solution)/shard_map/strategies/ppermute | solution.py:501
  28.9 1.7 %collective-permute-start.1 = (f32[1280,128]{1,0:T(8,128)S(1)}, f32[1280,128]{1,0:T(8,128)}, u32[]{:S(2)}, u32[]{:S(2)}) collective-permute-start(f32[1280,128]{1,0:T(8,128)S(1)} %bitcast.19), channel_id=1, source_target_pairs={{0,96},{32,0},{64,32},{96,64},{1,97},{33,1},{65,33},{97,65},{2,98}... | collective-permute-start | bytes 1966088 | tf_op jit(solution)/shard_map/strategies/ppermute | solution.py:501
  30.7 15.5 %sums.1 = (f32[4,1152,128]{2,1,0:T(8,128)}, f32[4,1152,128]{2,1,0:T(8,128)}) custom-call(s32[12288]{0:T(1024)} %bitcast.25, f32[6,1152,128]{2,1,0:T(8,128)} %get-tuple-element.78.delta_ref), custom_call_target="tpu_custom_call" | custom-call | flops 22000001024 | bytes 1000000 | tf_op jit(solution)/shard_map/river_sums/sums/pallas_call | solution.py:625
  46.2 0.1 collective-permute-start.2
  46.3 1.0 slice.62
  47.3 0.4 collective-permute-start.3
  47.6 1.0 slice.63
  48.6 3.0 %collective-permute-start.4 = (f32[640,128]{1,0:T(8,128)S(1)}, f32[640,128]{1,0:T(8,128)}, u32[]{:S(2)}, u32[]{:S(2)}) collective-permute-start(f32[640,128]{1,0:T(8,128)S(1)} %slice.63), channel_id=1, source_target_pairs={{0,96},{32,0},{64,32},{96,64},{1,97},{33,1},{65,33},{97,65},{2,98}... | collective-permute-start | bytes 983048 | tf_op jit(solution)/shard_map/river_sums/ppermute | solution.py:501
  51.6 0.5 collective-permute-start.6
  52.1 0.0 collective-permute-start.9
  52.1 3.4 %add.19 = f32[4,1152,128]{2,1,0:T(8,128)} add(f32[4,1152,128]{2,1,0:T(8,128)} %get-tuple-element.69, f32[4,1152,128]{2,1,0:T(8,128)S(1)} %collective-permute-done.2) | non-fusion elementwise | flops 589824 | bytes 7077888 | tf_op jit(solution)/shard_map/river_sums/add | solution.py:645
  55.6 3.1 %collective-permute-done.3.refs_2_ = f32[640,128]{1,0:T(8,128)S(1)} collective-permute-done((f32[640,128]{1,0:T(8,128)S(1)}, f32[640,128]{1,0:T(8,128)S(1)}, u32[]{:S(2)}, u32[]{:S(2)}) %collective-permute-start.3) | collective-permute-done | bytes 327712 | tf_op jit(solution)/shard_map/river_sums/ppermute | solution.py:501
  58.7 0.3 collective-permute-done.4.refs_3_
  59.0 0.5 collective-permute-start.8
  59.5 5.1 %all-to-all-start.1 = ((f32[4,1152,128]{2,1,0:T(8,128)}), f32[4,1152,128]{2,1,0:T(8,128)S(1)}, u32[]{:S(2)}, u32[]{:S(2)}) async-start(f32[4,1152,128]{2,1,0:T(8,128)} %add.19), calls=%async_computation.1 | async-start | bytes 4718592 | tf_op jit(solution)/shard_map/river_sums/all_to_all | solution.py:647
  64.6 30.8 %replies.1 = (f32[16,184,128]{2,1,0:T(8,128)}, f32[4,64,128]{2,1,0:T(8,128)}, f32[4,64,128]{2,1,0:T(8,128)}) custom-call(s32[12288]{0:T(1024)} %bitcast.24, s32[6144]{0:T(1024)} %bitcast.26, s32[3]{0:T(128)} %tcard_ref.3, s32[2,3]{1,0:T(2,128)} %bitcast.28, s32[3,2,1081]{2,1,0:T(2,128)} %rank_ref.3, s32[3,1081]{1,0:T(4,128)} %trow_ref.1, ...), custom_call_target="tpu_custom_call" | custom-call | flops 30000001024 | bytes 1000000 | tf_op jit(solution)/shard_map/replies/replies/pallas_call | solution.py:653
  95.4 0.1 collective-permute-start.10
  95.5 1.5 %collective-permute-done.10 = f32[4,64,128]{2,1,0:T(8,128)S(1)} collective-permute-done((f32[4,64,128]{2,1,0:T(8,128)}, f32[4,64,128]{2,1,0:T(8,128)S(1)}, u32[]{:S(2)}, u32[]{:S(2)}) %collective-permute-start.10) | collective-permute-done | bytes 131104 | tf_op jit(solution)/shard_map/turn_sums/ppermute | solution.py:719
  97.0 0.9 add.20
  97.9 3.6 %collective-permute-start.11 = (f32[64,128]{1,0:T(8,128)S(1)}, f32[64,128]{1,0:T(8,128)S(1)}, u32[]{:S(2)}, u32[]{:S(2)}) collective-permute-start(f32[64,128]{1,0:T(8,128)S(1)} %get-tuple-element.101), channel_id=1, source_target_pairs={{0,64},{32,96},{64,0},{96,32},{1,65},{33,97},{65,1},{97,33},{2,66}... | collective-permute-start | bytes 98312 | tf_op jit(solution)/shard_map/turn_sums/ppermute | solution.py:501
  101.6 0.5 collective-permute-start.12
  102.1 2.7 %collective-permute-start.13 = (f32[64,128]{1,0:T(8,128)S(1)}, f32[64,128]{1,0:T(8,128)S(1)}, u32[]{:S(2)}, u32[]{:S(2)}) collective-permute-start(f32[64,128]{1,0:T(8,128)S(1)} %get-tuple-element.99), channel_id=1, source_target_pairs={{0,96},{32,0},{64,32},{96,64},{1,97},{33,1},{65,33},{97,65},{2,98}... | collective-permute-start | bytes 98312 | tf_op jit(solution)/shard_map/turn_sums/ppermute | solution.py:501
  104.8 1.9 %collective-permute-done.12 = f32[64,128]{1,0:T(8,128)S(1)} collective-permute-done((f32[64,128]{1,0:T(8,128)S(1)}, f32[64,128]{1,0:T(8,128)S(1)}, u32[]{:S(2)}, u32[]{:S(2)}) %collective-permute-start.12) | collective-permute-done | bytes 32800 | tf_op jit(solution)/shard_map/turn_sums/ppermute | solution.py:501
  106.7 0.6 constant_dynamic-update-slice_fusion.1
  107.3 0.2 reduce_sum.9
  107.5 0.9 constant_dynamic-update-slice_fusion
  108.4 28.8 %all_to_all.15.came_ref = f32[16,184,128]{2,1,0:T(8,128)} all-to-all(f32[16,184,128]{2,1,0:T(8,128)} %constant_dynamic-update-slice_fusion), channel_id=1, replica_groups=mesh['x'=4,'core'=2,'z'=4,'y'=4] {'z','y'}, dimensions={0} | all-to-all | bytes 3014656 | tf_op jit(solution)/shard_map/exchange/all_to_all | solution.py:727
  137.2 2.7 %update.1 = (f32[72,256]{1,0:T(8,128)}, f32[8,128]{1,0:T(8,128)}, f32[3,4,1081]{2,1,0:T(4,128)}) custom-call(f32[16,184,128]{2,1,0:T(8,128)} %all_to_all.15.came_ref, f32[72,256]{1,0:T(8,128)} %river_ref.3, f32[8,128]{1,0:T(8,128)} %turn_ref.3, bf16[256,256]{1,0:T(8,128)(2,1)} %constant.71.clone.rperm_ref, bf16[128,128]{1,0:T(8,128)(2,1)} %constant.72.clone.tperm_ref), custom_call_target="tpu_custom_call" | custom-call | tf_op jit(solution)/shard_map/update/update/pallas_call | solution.py:730
  (19 shorter events, 0.1 us)
Async XLA Ops:
  2.8 24.6 %all-to-all-start = ((f32[16,80,128]{2,1,0:T(8,128)}), f32[16,80,128]{2,1,0:T(8,128)S(1)}, u32[]{:S(2)}, u32[]{:S(2)}) async-start(f32[16,80,128]{2,1,0:T(8,128)} %get-tuple-element.65), calls=%async_computation | async-start | bytes 1310720 | tf_op jit(solution)/shard_map/strategies/all_to_all | solution.py:549
  27.3 24.3 %copy-start = (f32[16,80,128]{2,1,0:T(8,128)}, f32[16,80,128]{2,1,0:T(8,128)S(1)}, u32[]{:S(2)}) copy-start(f32[16,80,128]{2,1,0:T(8,128)S(1)} %all-to-all-done) | copy-start | bytes 1966084
  27.3 18.8 %collective-permute-start = (f32[1280,128]{1,0:T(8,128)S(1)}, f32[1280,128]{1,0:T(8,128)}, u32[]{:S(2)}, u32[]{:S(2)}) collective-permute-start(f32[1280,128]{1,0:T(8,128)S(1)} %bitcast.18), channel_id=1, source_target_pairs={{0,32},{32,64},{64,96},{96,0},{1,33},{33,65},{65,97},{97,1},{2,34}... | collective-permute-start | bytes 1966088 | tf_op jit(solution)/shard_map/strategies/ppermute | solution.py:501
  28.9 17.3 %collective-permute-start.1 = (f32[1280,128]{1,0:T(8,128)S(1)}, f32[1280,128]{1,0:T(8,128)}, u32[]{:S(2)}, u32[]{:S(2)}) collective-permute-start(f32[1280,128]{1,0:T(8,128)S(1)} %bitcast.19), channel_id=1, source_target_pairs={{0,96},{32,0},{64,32},{96,64},{1,97},{33,1},{65,33},{97,65},{2,98}... | collective-permute-start | bytes 1966088 | tf_op jit(solution)/shard_map/strategies/ppermute | solution.py:501
  46.2 6.0 %collective-permute-start.2 = (f32[4,1152,128]{2,1,0:T(8,128)}, f32[4,1152,128]{2,1,0:T(8,128)S(1)}, u32[]{:S(2)}, u32[]{:S(2)}) collective-permute-start(f32[4,1152,128]{2,1,0:T(8,128)} %get-tuple-element.72), channel_id=1, source_target_pairs={{0,16},{16,0},{1,17},{17,1},{2,18},{18,2},{3,19},{19,3},{4,20},{20... | collective-permute-start | bytes 7077896 | tf_op jit(solution)/shard_map/river_sums/ppermute | solution.py:642
  47.3 11.4 %collective-permute-start.3 = (f32[640,128]{1,0:T(8,128)S(1)}, f32[640,128]{1,0:T(8,128)S(1)}, u32[]{:S(2)}, u32[]{:S(2)}) collective-permute-start(f32[640,128]{1,0:T(8,128)S(1)} %slice.62), channel_id=1, source_target_pairs={{0,32},{32,64},{64,96},{96,0},{1,33},{33,65},{65,97},{97,1},{2,34}... | collective-permute-start | bytes 983048 | tf_op jit(solution)/shard_map/river_sums/ppermute | solution.py:501
  48.6 10.4 %collective-permute-start.4 = (f32[640,128]{1,0:T(8,128)S(1)}, f32[640,128]{1,0:T(8,128)}, u32[]{:S(2)}, u32[]{:S(2)}) collective-permute-start(f32[640,128]{1,0:T(8,128)S(1)} %slice.63), channel_id=1, source_target_pairs={{0,96},{32,0},{64,32},{96,64},{1,97},{33,1},{65,33},{97,65},{2,98}... | collective-permute-start | bytes 983048 | tf_op jit(solution)/shard_map/river_sums/ppermute | solution.py:501
  51.6 12.9 %collective-permute-start.5 = (f32[1280,128]{1,0:T(8,128)S(1)}, f32[1280,128]{1,0:T(8,128)}, u32[]{:S(2)}, u32[]{:S(2)}) collective-permute-start(f32[1280,128]{1,0:T(8,128)S(1)} %bitcast.20), channel_id=1, source_target_pairs={{0,16},{16,0},{1,17},{17,1},{2,18},{18,2},{3,19},{19,3},{4,20},{20... | collective-permute-start | bytes 1966088 | tf_op jit(solution)/shard_map/river_sums/ppermute | solution.py:649
  51.6 12.9 %collective-permute-start.6 = (f32[1280,128]{1,0:T(8,128)}, f32[1280,128]{1,0:T(8,128)}, u32[]{:S(2)}, u32[]{:S(2)}) collective-permute-start(f32[1280,128]{1,0:T(8,128)} %collective-permute-done.refs_1_), channel_id=1, source_target_pairs={{0,16},{16,0},{1,17},{17,1},{2,18},{18,2},{3,19},{19,3},{4,20},{20... | collective-permute-start | bytes 1966088 | tf_op jit(solution)/shard_map/river_sums/ppermute | solution.py:649
  52.1 12.4 %collective-permute-start.9 = (f32[1280,128]{1,0:T(8,128)}, f32[1280,128]{1,0:T(8,128)}, u32[]{:S(2)}, u32[]{:S(2)}) collective-permute-start(f32[1280,128]{1,0:T(8,128)} %collective-permute-done.1.refs_4_), channel_id=1, source_target_pairs={{0,16},{16,0},{1,17},{17,1},{2,18},{18,2},{3,19},{19,3},{4,20},{20... | collective-permute-start | bytes 1966088 | tf_op jit(solution)/shard_map/river_sums/ppermute | solution.py:649
  58.6 0.8 copy-start.1
  59.0 5.6 %collective-permute-start.7 = (f32[640,128]{1,0:T(8,128)S(1)}, f32[640,128]{1,0:T(8,128)}, u32[]{:S(2)}, u32[]{:S(2)}) collective-permute-start(f32[640,128]{1,0:T(8,128)S(1)} %collective-permute-done.3.refs_2_), channel_id=1, source_target_pairs={{0,16},{16,0},{1,17},{17,1},{2,18},{18,2},{3,19},{19,3},{4,20},{20... | collective-permute-start | bytes 983048 | tf_op jit(solution)/shard_map/river_sums/ppermute | solution.py:649
  59.0 5.6 %collective-permute-start.8 = (f32[640,128]{1,0:T(8,128)}, f32[640,128]{1,0:T(8,128)}, u32[]{:S(2)}, u32[]{:S(2)}) collective-permute-start(f32[640,128]{1,0:T(8,128)} %collective-permute-done.4.refs_3_), channel_id=1, source_target_pairs={{0,16},{16,0},{1,17},{17,1},{2,18},{18,2},{3,19},{19,3},{4,20},{20... | collective-permute-start | bytes 983048 | tf_op jit(solution)/shard_map/river_sums/ppermute | solution.py:649
  59.5 47.2 %all-to-all-start.1 = ((f32[4,1152,128]{2,1,0:T(8,128)}), f32[4,1152,128]{2,1,0:T(8,128)S(1)}, u32[]{:S(2)}, u32[]{:S(2)}) async-start(f32[4,1152,128]{2,1,0:T(8,128)} %add.19), calls=%async_computation.1 | async-start | bytes 4718592 | tf_op jit(solution)/shard_map/river_sums/all_to_all | solution.py:647
  95.4 1.6 %collective-permute-start.10 = (f32[4,64,128]{2,1,0:T(8,128)}, f32[4,64,128]{2,1,0:T(8,128)S(1)}, u32[]{:S(2)}, u32[]{:S(2)}) collective-permute-start(f32[4,64,128]{2,1,0:T(8,128)} %get-tuple-element.92), channel_id=1, source_target_pairs={{0,16},{16,0},{1,17},{17,1},{2,18},{18,2},{3,19},{19,3},{4,20},{20... | collective-permute-start | bytes 393224 | tf_op jit(solution)/shard_map/turn_sums/ppermute | solution.py:719
  97.9 6.9 %collective-permute-start.11 = (f32[64,128]{1,0:T(8,128)S(1)}, f32[64,128]{1,0:T(8,128)S(1)}, u32[]{:S(2)}, u32[]{:S(2)}) collective-permute-start(f32[64,128]{1,0:T(8,128)S(1)} %get-tuple-element.101), channel_id=1, source_target_pairs={{0,64},{32,96},{64,0},{96,32},{1,65},{33,97},{65,1},{97,33},{2,66}... | collective-permute-start | bytes 98312 | tf_op jit(solution)/shard_map/turn_sums/ppermute | solution.py:501
  101.6 5.1 %collective-permute-start.12 = (f32[64,128]{1,0:T(8,128)S(1)}, f32[64,128]{1,0:T(8,128)S(1)}, u32[]{:S(2)}, u32[]{:S(2)}) collective-permute-start(f32[64,128]{1,0:T(8,128)S(1)} %get-tuple-element.100), channel_id=1, source_target_pairs={{0,32},{32,64},{64,96},{96,0},{1,33},{33,65},{65,97},{97,1},{2,34}... | collective-permute-start | bytes 98312 | tf_op jit(solution)/shard_map/turn_sums/ppermute | solution.py:501
  102.1 4.6 %collective-permute-start.13 = (f32[64,128]{1,0:T(8,128)S(1)}, f32[64,128]{1,0:T(8,128)S(1)}, u32[]{:S(2)}, u32[]{:S(2)}) collective-permute-start(f32[64,128]{1,0:T(8,128)S(1)} %get-tuple-element.99), channel_id=1, source_target_pairs={{0,96},{32,0},{64,32},{96,64},{1,97},{33,1},{65,33},{97,65},{2,98}... | collective-permute-start | bytes 98312 | tf_op jit(solution)/shard_map/turn_sums/ppermute | solution.py:501

commit v5 on v4

--- a/solution.py
+++ b/solution.py
@@ -21,7 +21,6 @@
 NN = (((1,), (0,)), ((), ()))
 TABLES = 6
 UNROLL = 47
-CHUNKS = 3
 INDEX_ROW = 2048
 RANKS = 16384.0
 AXES = ("x", "core", "z", "y")
@@ -212,19 +211,20 @@
     out_s[...] = jnp.transpose(wide_s[...])
 
 
-def sign_matrix(rank_ref, r, turn_value, river_value, cards_ref, disjoint_ref, rank_s, signed_s):
+def sign_matrix(rank_ref, r, turn_value, river_value, cards_ref, disjoint_ref, rank_s):
     out = jnp.logical_not(
         playable(cards_ref[0:1, :], cards_ref[1:2, :], turn_value, river_value)
     )
     rank_s[r : r + 1, :H] = rank_ref[0, r : r + 1, :]
     rank_row = rank_s[r : r + 1, :].astype(F32) + jnp.where(out, RANKS, 0.0)
     rank_col = jnp.transpose(jnp.broadcast_to(rank_row, (128, HP)))
+    signed = []
     for j in range(HP // 128):
         lanes = slice(j * 128, (j + 1) * 128)
         more = (rank_col - rank_row[:, lanes]).astype(BF)
         bound = disjoint_ref[:, lanes]
-        signed_s[r, :, lanes] = jnp.maximum(jnp.minimum(more, bound), -bound)
-    return rank_col < RANKS
+        signed.append(jnp.maximum(jnp.minimum(more, bound), -bound))
+    return rank_col < RANKS, jnp.concatenate(signed, axis=1)
 
 
 def payoff_kernel(
@@ -251,8 +251,7 @@
         wide_s,
         opp_s,
         show_s,
-        signed_s,
-    ) = refs[-8:]
+    ) = refs[-7:]
     t = pl.program_id(0) + start
 
     @pl.when(t == start)
@@ -267,14 +266,14 @@
     low, high = stake_rows(pot_ref)
     bets = 0.0
     for r in range(rivers):
-        col_ok = sign_matrix(
-            rank_ref, r, tcard_ref[t], rcard_ref[r, t], cards_ref, disjoint_ref, rank_s, signed_s
+        col_ok, signed = sign_matrix(
+            rank_ref, r, tcard_ref[t], rcard_ref[r, t], cards_ref, disjoint_ref, rank_s
         )
         called = call_s[pl.ds(r, HP, stride=rivers), :]
         theirs = jnp.where(col_ok, opp_s[...], 0.0)
         show_s[r, :, :C] = theirs.astype(BF)
         show_s[r, :, C:] = (theirs * called).astype(BF)
-        show = lax.dot_general(signed_s[r], show_s[r], NN, preferred_element_type=F32)
+        show = lax.dot_general(signed, show_s[r], NN, preferred_element_type=F32)
         fold = others((theirs * (1.0 - called)).astype(BF), holds_ref, out_of_ref)
         bet = jnp.where(col_ok, high * show[:, C:] + low * fold, 0.0)
         delta_ref[r] = jnp.where(col_ok, low * show[:, :C], 0.0) - bet
@@ -438,25 +437,8 @@
             total = total + jnp.where(col < RANKS, reply, 0.0)
         reply_s[rows, :] = total
 
-    chunk = HP // CHUNKS
-    taken = -(-H // CHUNKS)
-
-    def with_rows(i, _):
-        take_rows(i * taken, taken, t + 1, later)
-        some_replies(pl.multiple_of(i * chunk, 128), chunk)
-        return 0
-
-    def without_rows(i, _):
-        some_replies(pl.multiple_of(i * chunk, 128), chunk)
-        return 0
-
-    @pl.when(t < turns - 1)
-    def _():
-        lax.fori_loop(0, CHUNKS, with_rows, 0)
-
-    @pl.when(t == turns - 1)
-    def _():
-        lax.fori_loop(0, CHUNKS, without_rows, 0)
+
+    some_replies(0, HP)
 
     hi, lo = parts(nodes - pltpu.roll(nodes, G, 1), 2)
     both = jnp.concatenate([hi[:, :G], lo[:, :G]], axis=1)
@@ -481,6 +463,14 @@
             for part_ref, c in ((held_ref, core), (lent_ref, 1 - core)):
                 at = pl.multiple_of((((x + s) & 3) * 2 + c) * count, 8)
                 part_ref[s] = gain_ref[pl.ds(at, count), :]
+
+    @pl.when(t < turns - 1)
+    def _():
+        def some(i, _):
+            take_rows(i * UNROLL, UNROLL, t + 1, later)
+            return 0
+
+        lax.fori_loop(0, H // UNROLL, some, 0)
 
     flat = jnp.transpose(reply_s[...])
     flat = (flat[:G] + flat[G:]) * (1.0 / river_total)
@@ -587,7 +577,6 @@
                     pltpu.VMEM((C, HP), F32),
                     pltpu.VMEM((HP, C), F32),
                     pltpu.VMEM((rivers, HP, 2 * C), BF),
-                    pltpu.VMEM((rivers, HP, HP), BF),
                 ],
             ),
             out_shape=[
@@ -640,12 +629,14 @@
         )(index, delta)
         up, down, theirs = lax.optimization_barrier((up, down, theirs))
         got = lax.ppermute(theirs, "core", swap)
-        half = up.shape[0] // 2
-        far = [shifted(up[:half], "x", 1), shifted(down[half:], "x", 3)]
+        onward = [(2 * i, (2 * i + 2) % 8) for i in range(4)]
+        onward += [(2 * i + 1, (2 * i + 7) % 8) for i in range(4)]
+        passed = jnp.where(lax.axis_index("core") == 0, up, down)
+        far = lax.ppermute(passed, ("x", "core"), onward)
         chip = mine + got
-        chip, *far = lax.optimization_barrier((chip, *far))
+        chip, far = lax.optimization_barrier((chip, far))
         columns = lax.all_to_all(chip, "x", 0, 0)
-        own = [plane, up, *far, down]
+        own = [plane, up, far, down]
         pieces = own + [lax.ppermute(piece, "core", swap) for piece in own]
         delta, chip, *pieces = lax.optimization_barrier((delta, chip, *pieces))
 

time: 141 us -> 134 us (0.950)
  Pallas kernels: 67.5 us -> 62.2 us
  starting transfers between devices: 27.9 us -> 24.8 us
  waiting for transfers between devices: 6.84 us -> 9.35 us
  local copies, waits for them, and re-layouts: 3.51 us -> 1.54 us
    ppermute x0 -> x1, waiting for transfers between devices: none -> 5.1 us  [per_device(): far = lax.ppermute(passed, ('x', 'core'), onward)]
    ppermute x7 -> x5, starting transfers between devices: 13.5 us -> 9.78 us  [shifted(): return lax.ppermute(x, axis, [(i, (i + shift) % 4) for i in range(4)])]
    ppermute x7 -> x5, waiting for transfers between devices: 5.28 us -> 1.9 us  [shifted(): return lax.ppermute(x, axis, [(i, (i + shift) % 4) for i in range(4)])]
    pallas_call x1, Pallas kernels: 16.4 us -> 13.6 us  [payoffs(): pl.pallas_call(functools.partial(payoff_kernel, rivers, start), grid_spec...]
    pallas_call x1, Pallas kernels: 30.8 us -> 28.3 us  [per_device(): pl.pallas_call(functools.partial(reply_kernel, turns, rivers, river_total...]
    slice x2 -> x0, local copies, waits for them, and re-layouts: 1.99 us -> none  [per_device(): far = [shifted(up[:half], 'x', 1), shifted(down[half:], 'x', 3)]]
  transfers between devices with their start and end apart: 16 -> 14, of which waited for: 4 -> 4; matrix products, arithmetic and copies ran while one was open for 5% -> 4% of each run, Pallas kernels for 45% -> 43%
where the time goes in v5:
time: 134 us; the launch traced here: 133 us
  Pallas kernels  62.2 us (46%)
  blocking collectives  28.8 us (21%)
  starting transfers between devices  24.8 us (19%)
  waiting for transfers between devices  9.35 us (7%)
  other arithmetic  5.58 us (4%)
  local copies, waits for them, and re-layouts  1.54 us (1%)
    all_to_all x1, blocking collectives, per_device(): came = lax.all_to_all(sent, ('z', 'y'), 0, 0)  28.8 us
    pallas_call x1, Pallas kernels, per_device(): pl.pallas_call(functools.partial(reply_kernel, turns, rivers, river_total...  28.3 us
    pallas_call x1, Pallas kernels, per_device(): pl.pallas_call(sum_kernel, grid_spec=pltpu.PrefetchScalarGridSpec(num_sca...  15.5 us
    pallas_call x1, Pallas kernels, payoffs(): pl.pallas_call(functools.partial(payoff_kernel, rivers, start), grid_spec...  13.6 us
    ppermute x5, starting transfers between devices, shifted(): return lax.ppermute(x, axis, [(i, (i + shift) % 4) for i in range(4)])  9.78 us
    all_to_all x1, starting transfers between devices, per_device(): plane = lax.all_to_all(strategies, ('z', 'y'), 0, 0).reshape(-1, C)  8.13 us
    ppermute x1, waiting for transfers between devices, per_device(): far = lax.ppermute(passed, ('x', 'core'), onward)  5.1 us
    all_to_all x1, starting transfers between devices, per_device(): columns = lax.all_to_all(chip, 'x', 0, 0)  3.81 us
  transfers between devices with their start and end apart: 14, of which 4 were waited for; matrix products, arithmetic and copies ran while one was open for 4% of the time, Pallas kernels for 43%

profile of v5, /device:TPU:0, one launch (start us, length us, event | category | flops | bytes accessed | tf_op | source)
XLA Modules:
  0.0 133.0 jit_solution(3676406470186275722)
XLA Ops:
  0.6 2.1 %strategies.1 = (f32[16,80,128]{2,1,0:T(8,128)}, s32[6,16,128]{2,1,0:T(8,128)}, s32[6,16,128]{2,1,0:T(8,128)}, s32[3,16,128]{2,1,0:T(8,128)}) custom-call(f32[72,256]{1,0:T(8,128)} %river_ref.3, f32[8,128]{1,0:T(8,128)} %turn_ref.3, bf16[256,256]{1,0:T(8,128)(2,1)} %constant.78.clone.rperm_ref, bf16[128,128]{1,0:T(8,128)(2,1)} %constant.79.clone.tperm_ref, ...), custom_call_target="tpu_custom_call" | custom-call | tf_op jit(solution)/shard_map/strategies/strategies/pallas_call | solution.py:527
  2.8 8.1 %all-to-all-start = ((f32[16,80,128]{2,1,0:T(8,128)}), f32[16,80,128]{2,1,0:T(8,128)S(1)}, u32[]{:S(2)}, u32[]{:S(2)}) async-start(f32[16,80,128]{2,1,0:T(8,128)} %get-tuple-element.62), calls=%async_computation | async-start | bytes 1310720 | tf_op jit(solution)/shard_map/strategies/all_to_all | solution.py:539
  10.9 13.6 %payoffs.1 = (f32[6,1152,128]{2,1,0:T(8,128)}, f32[3,1152,128]{2,1,0:T(8,128)}) custom-call(s32[3]{0:T(128)} %tcard_ref.3, s32[2,3]{1,0:T(2,128)} %bitcast.27, s32[3,2,1081]{2,1,0:T(2,128)} %rank_ref.3, bf16[3,1081,2,128]{3,2,1,0:T(2,128)(2,1)} %bitcast.23, f32[64,1081]{1,0:T(8,128)} %opp_ref.1, f32[1,64]{1,0:T(1,128)} %bitcast.29, ...), custom_call_target="tpu_custom_call" | custom-call | flops 24000000000 | bytes 1000000 | tf_op jit(solution)/shard_map/payoffs/payoffs/pallas_call | solution.py:556
  24.5 0.0 all-to-all-done
  24.5 1.6 %collective-permute-start = (f32[1280,128]{1,0:T(8,128)S(1)}, f32[1280,128]{1,0:T(8,128)}, u32[]{:S(2)}, u32[]{:S(2)}) collective-permute-start(f32[1280,128]{1,0:T(8,128)S(1)} %bitcast.18), channel_id=1, source_target_pairs={{0,32},{32,64},{64,96},{96,0},{1,33},{33,65},{65,97},{97,1},{2,34}... | collective-permute-start | bytes 1966088 | tf_op jit(solution)/shard_map/strategies/ppermute | solution.py:491
  26.1 1.7 %collective-permute-start.1 = (f32[1280,128]{1,0:T(8,128)S(1)}, f32[1280,128]{1,0:T(8,128)}, u32[]{:S(2)}, u32[]{:S(2)}) collective-permute-start(f32[1280,128]{1,0:T(8,128)S(1)} %bitcast.19), channel_id=1, source_target_pairs={{0,96},{32,0},{64,32},{96,64},{1,97},{33,1},{65,33},{97,65},{2,98}... | collective-permute-start | bytes 1966088 | tf_op jit(solution)/shard_map/strategies/ppermute | solution.py:491
  27.8 15.5 %sums.1 = (f32[4,1152,128]{2,1,0:T(8,128)}, f32[4,1152,128]{2,1,0:T(8,128)}) custom-call(s32[12288]{0:T(1024)} %bitcast.25, f32[6,1152,128]{2,1,0:T(8,128)} %get-tuple-element.74.delta_ref), custom_call_target="tpu_custom_call" | custom-call | flops 22000001024 | bytes 1000000 | tf_op jit(solution)/shard_map/river_sums/sums/pallas_call | solution.py:614
  43.3 0.0 collective-permute-done.1.refs_3_
  43.3 0.1 collective-permute-start.2
  43.4 1.2 broadcast_select_fusion
  44.6 0.4 collective-permute-start.3
  44.9 1.6 %collective-permute-start.4 = (f32[1280,128]{1,0:T(8,128)S(1)}, f32[1280,128]{1,0:T(8,128)}, u32[]{:S(2)}, u32[]{:S(2)}) collective-permute-start(f32[1280,128]{1,0:T(8,128)S(1)} %bitcast.20), channel_id=1, source_target_pairs={{0,16},{16,0},{1,17},{17,1},{2,18},{18,2},{3,19},{19,3},{4,20},{20... | collective-permute-start | bytes 1966088 | tf_op jit(solution)/shard_map/river_sums/ppermute | solution.py:640
  46.5 0.0 collective-permute-start.5
  46.5 0.5 collective-permute-start.7
  47.0 1.1 collective-permute-done.2
  48.1 3.3 %add.19 = f32[4,1152,128]{2,1,0:T(8,128)} add(f32[4,1152,128]{2,1,0:T(8,128)} %get-tuple-element.66, f32[4,1152,128]{2,1,0:T(8,128)S(1)} %collective-permute-done.2) | non-fusion elementwise | flops 589824 | bytes 7077888 | tf_op jit(solution)/shard_map/river_sums/add | solution.py:636
  51.5 5.1 %collective-permute-done.3.refs_2_ = f32[1280,128]{1,0:T(8,128)} collective-permute-done((f32[1280,128]{1,0:T(8,128)S(1)}, f32[1280,128]{1,0:T(8,128)}, u32[]{:S(2)}, u32[]{:S(2)}) %collective-permute-start.3) | collective-permute-done | bytes 655392 | tf_op jit(solution)/shard_map/river_sums/ppermute | solution.py:635
  56.6 3.8 %all-to-all-start.1 = ((f32[4,1152,128]{2,1,0:T(8,128)}), f32[4,1152,128]{2,1,0:T(8,128)S(1)}, u32[]{:S(2)}, u32[]{:S(2)}) async-start(f32[4,1152,128]{2,1,0:T(8,128)} %add.19), calls=%async_computation.1 | async-start | bytes 4718592 | tf_op jit(solution)/shard_map/river_sums/all_to_all | solution.py:638
  60.4 0.0 collective-permute-done.4.refs_4_
  60.4 28.3 %replies.1 = (f32[16,184,128]{2,1,0:T(8,128)}, f32[4,64,128]{2,1,0:T(8,128)}, f32[4,64,128]{2,1,0:T(8,128)}) custom-call(s32[12288]{0:T(1024)} %bitcast.24, s32[6144]{0:T(1024)} %bitcast.26, s32[3]{0:T(128)} %tcard_ref.3, s32[2,3]{1,0:T(2,128)} %bitcast.28, s32[3,2,1081]{2,1,0:T(2,128)} %rank_ref.3, s32[3,1081]{1,0:T(4,128)} %trow_ref.1, ...), custom_call_target="tpu_custom_call" | custom-call | flops 30000001024 | bytes 1000000 | tf_op jit(solution)/shard_map/replies/replies/pallas_call | solution.py:644
  88.7 0.6 collective-permute-start.8
  89.3 1.2 collective-permute-done.8
  90.5 0.9 add.20
  91.4 3.2 %collective-permute-start.9 = (f32[64,128]{1,0:T(8,128)S(1)}, f32[64,128]{1,0:T(8,128)S(1)}, u32[]{:S(2)}, u32[]{:S(2)}) collective-permute-start(f32[64,128]{1,0:T(8,128)S(1)} %get-tuple-element.95), channel_id=1, source_target_pairs={{0,64},{32,96},{64,0},{96,32},{1,65},{33,97},{65,1},{97,33},{2,66}... | collective-permute-start | bytes 98312 | tf_op jit(solution)/shard_map/turn_sums/ppermute | solution.py:491
  94.7 0.6 collective-permute-start.10
  95.2 2.7 %collective-permute-start.11 = (f32[64,128]{1,0:T(8,128)S(1)}, f32[64,128]{1,0:T(8,128)S(1)}, u32[]{:S(2)}, u32[]{:S(2)}) collective-permute-start(f32[64,128]{1,0:T(8,128)S(1)} %get-tuple-element.93), channel_id=1, source_target_pairs={{0,96},{32,0},{64,32},{96,64},{1,97},{33,1},{65,33},{97,65},{2,98}... | collective-permute-start | bytes 98312 | tf_op jit(solution)/shard_map/turn_sums/ppermute | solution.py:491
  97.9 1.9 %collective-permute-done.10 = f32[64,128]{1,0:T(8,128)S(1)} collective-permute-done((f32[64,128]{1,0:T(8,128)S(1)}, f32[64,128]{1,0:T(8,128)S(1)}, u32[]{:S(2)}, u32[]{:S(2)}) %collective-permute-start.10) | collective-permute-done | bytes 32800 | tf_op jit(solution)/shard_map/turn_sums/ppermute | solution.py:491
  99.8 0.6 constant_dynamic-update-slice_fusion.1
  100.5 0.2 reduce_sum.9
  100.6 0.9 constant_dynamic-update-slice_fusion
  101.5 28.8 %all_to_all.15.came_ref = f32[16,184,128]{2,1,0:T(8,128)} all-to-all(f32[16,184,128]{2,1,0:T(8,128)} %constant_dynamic-update-slice_fusion), channel_id=1, replica_groups=mesh['x'=4,'core'=2,'z'=4,'y'=4] {'z','y'}, dimensions={0} | all-to-all | bytes 3014656 | tf_op jit(solution)/shard_map/exchange/all_to_all | solution.py:718
  130.3 2.7 %update.1 = (f32[72,256]{1,0:T(8,128)}, f32[8,128]{1,0:T(8,128)}, f32[3,4,1081]{2,1,0:T(4,128)}) custom-call(f32[16,184,128]{2,1,0:T(8,128)} %all_to_all.15.came_ref, f32[72,256]{1,0:T(8,128)} %river_ref.3, f32[8,128]{1,0:T(8,128)} %turn_ref.3, bf16[256,256]{1,0:T(8,128)(2,1)} %constant.78.clone.rperm_ref, bf16[128,128]{1,0:T(8,128)(2,1)} %constant.79.clone.tperm_ref), custom_call_target="tpu_custom_call" | custom-call | tf_op jit(solution)/shard_map/update/update/pallas_call | solution.py:721
  (12 shorter events, 0.0 us)
Async XLA Ops:
  2.8 21.7 %all-to-all-start = ((f32[16,80,128]{2,1,0:T(8,128)}), f32[16,80,128]{2,1,0:T(8,128)S(1)}, u32[]{:S(2)}, u32[]{:S(2)}) async-start(f32[16,80,128]{2,1,0:T(8,128)} %get-tuple-element.62), calls=%async_computation | async-start | bytes 1310720 | tf_op jit(solution)/shard_map/strategies/all_to_all | solution.py:539
  24.5 20.5 %copy-start = (f32[16,80,128]{2,1,0:T(8,128)}, f32[16,80,128]{2,1,0:T(8,128)S(1)}, u32[]{:S(2)}) copy-start(f32[16,80,128]{2,1,0:T(8,128)S(1)} %all-to-all-done) | copy-start | bytes 1966084
  24.5 18.8 %collective-permute-start = (f32[1280,128]{1,0:T(8,128)S(1)}, f32[1280,128]{1,0:T(8,128)}, u32[]{:S(2)}, u32[]{:S(2)}) collective-permute-start(f32[1280,128]{1,0:T(8,128)S(1)} %bitcast.18), channel_id=1, source_target_pairs={{0,32},{32,64},{64,96},{96,0},{1,33},{33,65},{65,97},{97,1},{2,34}... | collective-permute-start | bytes 1966088 | tf_op jit(solution)/shard_map/strategies/ppermute | solution.py:491
  26.1 17.3 %collective-permute-start.1 = (f32[1280,128]{1,0:T(8,128)S(1)}, f32[1280,128]{1,0:T(8,128)}, u32[]{:S(2)}, u32[]{:S(2)}) collective-permute-start(f32[1280,128]{1,0:T(8,128)S(1)} %bitcast.19), channel_id=1, source_target_pairs={{0,96},{32,0},{64,32},{96,64},{1,97},{33,1},{65,33},{97,65},{2,98}... | collective-permute-start | bytes 1966088 | tf_op jit(solution)/shard_map/strategies/ppermute | solution.py:491
  43.3 4.8 %collective-permute-start.2 = (f32[4,1152,128]{2,1,0:T(8,128)}, f32[4,1152,128]{2,1,0:T(8,128)S(1)}, u32[]{:S(2)}, u32[]{:S(2)}) collective-permute-start(f32[4,1152,128]{2,1,0:T(8,128)} %get-tuple-element.69), channel_id=1, source_target_pairs={{0,16},{16,0},{1,17},{17,1},{2,18},{18,2},{3,19},{19,3},{4,20},{20... | collective-permute-start | bytes 7077896 | tf_op jit(solution)/shard_map/river_sums/ppermute | solution.py:631
  44.6 12.0 %collective-permute-start.3 = (f32[1280,128]{1,0:T(8,128)S(1)}, f32[1280,128]{1,0:T(8,128)}, u32[]{:S(2)}, u32[]{:S(2)}) collective-permute-start(f32[1280,128]{1,0:T(8,128)S(1)} %broadcast_select_fusion), channel_id=1, source_target_pairs={{0,32},{32,64},{64,96},{96,0},{16,112},{48,16},{80,48},{112,80},{1... | collective-permute-start | bytes 1966088 | tf_op jit(solution)/shard_map/river_sums/ppermute | solution.py:635
  44.9 15.4 %collective-permute-start.4 = (f32[1280,128]{1,0:T(8,128)S(1)}, f32[1280,128]{1,0:T(8,128)}, u32[]{:S(2)}, u32[]{:S(2)}) collective-permute-start(f32[1280,128]{1,0:T(8,128)S(1)} %bitcast.20), channel_id=1, source_target_pairs={{0,16},{16,0},{1,17},{17,1},{2,18},{18,2},{3,19},{19,3},{4,20},{20... | collective-permute-start | bytes 1966088 | tf_op jit(solution)/shard_map/river_sums/ppermute | solution.py:640
  46.5 13.9 %collective-permute-start.5 = (f32[1280,128]{1,0:T(8,128)}, f32[1280,128]{1,0:T(8,128)}, u32[]{:S(2)}, u32[]{:S(2)}) collective-permute-start(f32[1280,128]{1,0:T(8,128)} %collective-permute-done.refs_1_), channel_id=1, source_target_pairs={{0,16},{16,0},{1,17},{17,1},{2,18},{18,2},{3,19},{19,3},{4,20},{20... | collective-permute-start | bytes 1966088 | tf_op jit(solution)/shard_map/river_sums/ppermute | solution.py:640
  46.5 13.9 %collective-permute-start.7 = (f32[1280,128]{1,0:T(8,128)}, f32[1280,128]{1,0:T(8,128)}, u32[]{:S(2)}, u32[]{:S(2)}) collective-permute-start(f32[1280,128]{1,0:T(8,128)} %collective-permute-done.1.refs_3_), channel_id=1, source_target_pairs={{0,16},{16,0},{1,17},{17,1},{2,18},{18,2},{3,19},{19,3},{4,20},{20... | collective-permute-start | bytes 1966088 | tf_op jit(solution)/shard_map/river_sums/ppermute | solution.py:640
  56.6 3.9 %collective-permute-start.6 = (f32[1280,128]{1,0:T(8,128)}, f32[1280,128]{1,0:T(8,128)}, u32[]{:S(2)}, u32[]{:S(2)}) collective-permute-start(f32[1280,128]{1,0:T(8,128)} %collective-permute-done.3.refs_2_), channel_id=1, source_target_pairs={{0,16},{16,0},{1,17},{17,1},{2,18},{18,2},{3,19},{19,3},{4,20},{20... | collective-permute-start | bytes 1966088 | tf_op jit(solution)/shard_map/river_sums/ppermute | solution.py:640
  56.6 43.2 %all-to-all-start.1 = ((f32[4,1152,128]{2,1,0:T(8,128)}), f32[4,1152,128]{2,1,0:T(8,128)S(1)}, u32[]{:S(2)}, u32[]{:S(2)}) async-start(f32[4,1152,128]{2,1,0:T(8,128)} %add.19), calls=%async_computation.1 | async-start | bytes 4718592 | tf_op jit(solution)/shard_map/river_sums/all_to_all | solution.py:638
  88.7 1.8 %collective-permute-start.8 = (f32[4,64,128]{2,1,0:T(8,128)}, f32[4,64,128]{2,1,0:T(8,128)S(1)}, u32[]{:S(2)}, u32[]{:S(2)}) collective-permute-start(f32[4,64,128]{2,1,0:T(8,128)} %get-tuple-element.86), channel_id=1, source_target_pairs={{0,16},{16,0},{1,17},{17,1},{2,18},{18,2},{3,19},{19,3},{4,20},{20... | collective-permute-start | bytes 393224 | tf_op jit(solution)/shard_map/turn_sums/ppermute | solution.py:710
  91.4 6.5 %collective-permute-start.9 = (f32[64,128]{1,0:T(8,128)S(1)}, f32[64,128]{1,0:T(8,128)S(1)}, u32[]{:S(2)}, u32[]{:S(2)}) collective-permute-start(f32[64,128]{1,0:T(8,128)S(1)} %get-tuple-element.95), channel_id=1, source_target_pairs={{0,64},{32,96},{64,0},{96,32},{1,65},{33,97},{65,1},{97,33},{2,66}... | collective-permute-start | bytes 98312 | tf_op jit(solution)/shard_map/turn_sums/ppermute | solution.py:491
  94.7 5.1 %collective-permute-start.10 = (f32[64,128]{1,0:T(8,128)S(1)}, f32[64,128]{1,0:T(8,128)S(1)}, u32[]{:S(2)}, u32[]{:S(2)}) collective-permute-start(f32[64,128]{1,0:T(8,128)S(1)} %get-tuple-element.94), channel_id=1, source_target_pairs={{0,32},{32,64},{64,96},{96,0},{1,33},{33,65},{65,97},{97,1},{2,34}... | collective-permute-start | bytes 98312 | tf_op jit(solution)/shard_map/turn_sums/ppermute | solution.py:491
  95.2 4.6 %collective-permute-start.11 = (f32[64,128]{1,0:T(8,128)S(1)}, f32[64,128]{1,0:T(8,128)S(1)}, u32[]{:S(2)}, u32[]{:S(2)}) collective-permute-start(f32[64,128]{1,0:T(8,128)S(1)} %get-tuple-element.93), channel_id=1, source_target_pairs={{0,96},{32,0},{64,32},{96,64},{1,97},{33,1},{65,33},{97,65},{2,98}... | collective-permute-start | bytes 98312 | tf_op jit(solution)/shard_map/turn_sums/ppermute | solution.py:491

commit v6 on v5

--- a/solution.py
+++ b/solution.py
@@ -137,8 +137,10 @@
     def placed(bucket, count, offset):
         owner = ((bucket.astype(F32) + 0.5) * (1.0 / count)).astype(jnp.int32)
         row = bucket - owner * count
-        other = (core - (owner >> 4)) & 1
-        slot = (other * 4 + ((x - (owner >> 5)) & 3)) * 16 + (owner & 15)
+        owner_core = (owner >> 4) & 1
+        other = (core - owner_core) & 1
+        steps = (x - (owner >> 5)) * (1 - 2 * owner_core)
+        slot = (other * 4 + (steps & 3)) * 16 + (owner & 15)
         return slot * rest + offset + row
 
     at_ref[...] = placed(index_ref[...], owned, 0)
@@ -608,7 +610,11 @@
         delta, bet = payoffs(0, turns)
     with jax.named_scope("strategies"):
         plane, delta = lax.optimization_barrier((plane, delta))
-        up, down = shifted(plane, "x", 1), shifted(plane, "x", 3)
+        onward = [(2 * i, (2 * i + 2) % 8) for i in range(4)]
+        onward += [(2 * i + 1, (2 * i + 7) % 8) for i in range(4)]
+        back = [(j, i) for i, j in onward]
+        near = lax.ppermute(plane, ("x", "core"), onward)
+        last = lax.ppermute(plane, ("x", "core"), back)
 
     with jax.named_scope("river_sums"):
         mine, theirs = pl.pallas_call(
@@ -627,16 +633,13 @@
             ),
             name="sums",
         )(index, delta)
-        up, down, theirs = lax.optimization_barrier((up, down, theirs))
+        near, last, theirs = lax.optimization_barrier((near, last, theirs))
         got = lax.ppermute(theirs, "core", swap)
-        onward = [(2 * i, (2 * i + 2) % 8) for i in range(4)]
-        onward += [(2 * i + 1, (2 * i + 7) % 8) for i in range(4)]
-        passed = jnp.where(lax.axis_index("core") == 0, up, down)
-        far = lax.ppermute(passed, ("x", "core"), onward)
+        far = lax.ppermute(near, ("x", "core"), onward)
         chip = mine + got
         chip, far = lax.optimization_barrier((chip, far))
         columns = lax.all_to_all(chip, "x", 0, 0)
-        own = [plane, up, far, down]
+        own = [plane, near, far, last]
         pieces = own + [lax.ppermute(piece, "core", swap) for piece in own]
         delta, chip, *pieces = lax.optimization_barrier((delta, chip, *pieces))
 

time: 134 us -> 133 us (level)
  waiting for transfers between devices: 9.35 us -> 11.2 us
  starting transfers between devices: 24.8 us -> 23.4 us
    ppermute x5 -> x3, starting transfers between devices: 9.78 us -> 5.24 us  [shifted(): return lax.ppermute(x, axis, [(i, (i + shift) % 4) for i in range(4)])]
    ppermute x1 -> x3, starting transfers between devices: 0.35 us -> 3.65 us  [the longest x1 1.75 us: per_device(): last = lax.ppermute(plane, ('x', 'core'), back)]
    ppermute x5 -> x3, waiting for transfers between devices: 1.9 us -> 3.5 us  [shifted(): return lax.ppermute(x, axis, [(i, (i + shift) % 4) for i in range(4)])]
    ppermute x1 -> x3, waiting for transfers between devices: 5.1 us -> 3.99 us  [the longest x1 3.99 us: per_device(): far = lax.ppermute(near, ('x', 'core'), onward)]
  transfers between devices with their start and end apart: 14 -> 14, of which waited for: 4 -> 5; matrix products, arithmetic and copies ran while one was open for 4% -> 3% of each run, Pallas kernels for 43% -> 43%
where the time goes in v6:
time: 133 us; the launch traced here: 132 us
  Pallas kernels  62.2 us (47%)
  blocking collectives  28.7 us (22%)
  starting transfers between devices  23.4 us (18%)
  waiting for transfers between devices  11.2 us (8%)
  other arithmetic  4.56 us (3%)
  local copies, waits for them, and re-layouts  1.54 us (1%)
    all_to_all x1, blocking collectives, per_device(): came = lax.all_to_all(sent, ('z', 'y'), 0, 0)  28.7 us
    pallas_call x1, Pallas kernels, per_device(): pl.pallas_call(functools.partial(reply_kernel, turns, rivers, river_total...  28.3 us
    pallas_call x1, Pallas kernels, per_device(): pl.pallas_call(sum_kernel, grid_spec=pltpu.PrefetchScalarGridSpec(num_sca...  15.5 us
    pallas_call x1, Pallas kernels, payoffs(): pl.pallas_call(functools.partial(payoff_kernel, rivers, start), grid_spec...  13.6 us
    all_to_all x1, starting transfers between devices, per_device(): plane = lax.all_to_all(strategies, ('z', 'y'), 0, 0).reshape(-1, C)  8.13 us
    ppermute x3, starting transfers between devices, shifted(): return lax.ppermute(x, axis, [(i, (i + shift) % 4) for i in range(4)])  5.24 us
    ppermute x1, waiting for transfers between devices, per_device(): far = lax.ppermute(near, ('x', 'core'), onward)  3.99 us
    all_to_all x1, starting transfers between devices, per_device(): columns = lax.all_to_all(chip, 'x', 0, 0)  3.81 us
  transfers between devices with their start and end apart: 14, of which 5 were waited for; matrix products, arithmetic and copies ran while one was open for 3% of the time, Pallas kernels for 43%

profile of v6, /device:TPU:0, one launch (start us, length us, event | category | flops | bytes accessed | tf_op | source)
XLA Modules:
  0.0 132.3 jit_solution(11103602140239214255)
XLA Ops:
  0.6 2.1 %strategies.1 = (f32[16,80,128]{2,1,0:T(8,128)}, s32[6,16,128]{2,1,0:T(8,128)}, s32[6,16,128]{2,1,0:T(8,128)}, s32[3,16,128]{2,1,0:T(8,128)}) custom-call(f32[72,256]{1,0:T(8,128)} %river_ref.3, f32[8,128]{1,0:T(8,128)} %turn_ref.3, bf16[256,256]{1,0:T(8,128)(2,1)} %constant.71.clone.rperm_ref, bf16[128,128]{1,0:T(8,128)(2,1)} %constant.72.clone.tperm_ref, ...), custom_call_target="tpu_custom_call" | custom-call | tf_op jit(solution)/shard_map/strategies/strategies/pallas_call | solution.py:529
  2.8 8.1 %all-to-all-start = ((f32[16,80,128]{2,1,0:T(8,128)}), f32[16,80,128]{2,1,0:T(8,128)S(1)}, u32[]{:S(2)}, u32[]{:S(2)}) async-start(f32[16,80,128]{2,1,0:T(8,128)} %get-tuple-element.62), calls=%async_computation | async-start | bytes 1310720 | tf_op jit(solution)/shard_map/strategies/all_to_all | solution.py:541
  10.9 13.6 %payoffs.1 = (f32[6,1152,128]{2,1,0:T(8,128)}, f32[3,1152,128]{2,1,0:T(8,128)}) custom-call(s32[3]{0:T(128)} %tcard_ref.3, s32[2,3]{1,0:T(2,128)} %bitcast.27, s32[3,2,1081]{2,1,0:T(2,128)} %rank_ref.3, bf16[3,1081,2,128]{3,2,1,0:T(2,128)(2,1)} %bitcast.23, f32[64,1081]{1,0:T(8,128)} %opp_ref.1, f32[1,64]{1,0:T(1,128)} %bitcast.29, ...), custom_call_target="tpu_custom_call" | custom-call | flops 24000000000 | bytes 1000000 | tf_op jit(solution)/shard_map/payoffs/payoffs/pallas_call | solution.py:558
  24.5 0.0 all-to-all-done
  24.5 1.6 %collective-permute-start = (f32[1280,128]{1,0:T(8,128)S(1)}, f32[1280,128]{1,0:T(8,128)}, u32[]{:S(2)}, u32[]{:S(2)}) collective-permute-start(f32[1280,128]{1,0:T(8,128)S(1)} %bitcast.18), channel_id=1, source_target_pairs={{0,32},{32,64},{64,96},{96,0},{16,112},{48,16},{80,48},{112,80},{1... | collective-permute-start | bytes 1966088 | tf_op jit(solution)/shard_map/strategies/ppermute | solution.py:616
  26.1 1.7 %collective-permute-start.1 = (f32[1280,128]{1,0:T(8,128)S(1)}, f32[1280,128]{1,0:T(8,128)}, u32[]{:S(2)}, u32[]{:S(2)}) collective-permute-start(f32[1280,128]{1,0:T(8,128)S(1)} %bitcast.19), channel_id=1, source_target_pairs={{32,0},{64,32},{96,64},{0,96},{112,16},{16,48},{48,80},{80,112},{3... | collective-permute-start | bytes 1966088 | tf_op jit(solution)/shard_map/strategies/ppermute | solution.py:617
  27.8 15.5 %sums.1 = (f32[4,1152,128]{2,1,0:T(8,128)}, f32[4,1152,128]{2,1,0:T(8,128)}) custom-call(s32[12288]{0:T(1024)} %bitcast.25, f32[6,1152,128]{2,1,0:T(8,128)} %get-tuple-element.74.delta_ref), custom_call_target="tpu_custom_call" | custom-call | flops 22000001024 | bytes 1000000 | tf_op jit(solution)/shard_map/river_sums/sums/pallas_call | solution.py:620
  43.3 0.0 collective-permute-done.refs_1_
  43.3 0.0 collective-permute-done.1.refs_3_
  43.3 0.1 collective-permute-start.2
  43.4 0.3 collective-permute-start.3
  43.8 1.4 %collective-permute-start.4 = (f32[1280,128]{1,0:T(8,128)S(1)}, f32[1280,128]{1,0:T(8,128)}, u32[]{:S(2)}, u32[]{:S(2)}) collective-permute-start(f32[1280,128]{1,0:T(8,128)S(1)} %bitcast.20), channel_id=1, source_target_pairs={{0,16},{16,0},{1,17},{17,1},{2,18},{18,2},{3,19},{19,3},{4,20},{20... | collective-permute-start | bytes 1966088 | tf_op jit(solution)/shard_map/river_sums/ppermute | solution.py:643
  45.2 0.0 collective-permute-start.5
  45.2 0.5 collective-permute-start.7
  45.7 2.5 %collective-permute-done.2 = f32[4,1152,128]{2,1,0:T(8,128)S(1)} collective-permute-done((f32[4,1152,128]{2,1,0:T(8,128)}, f32[4,1152,128]{2,1,0:T(8,128)S(1)}, u32[]{:S(2)}, u32[]{:S(2)}) %collective-permute-start.2) | collective-permute-done | bytes 2359328 | tf_op jit(solution)/shard_map/river_sums/ppermute | solution.py:637
  48.1 3.5 %add.19 = f32[4,1152,128]{2,1,0:T(8,128)} add(f32[4,1152,128]{2,1,0:T(8,128)} %get-tuple-element.66, f32[4,1152,128]{2,1,0:T(8,128)S(1)} %collective-permute-done.2) | non-fusion elementwise | flops 589824 | bytes 7077888 | tf_op jit(solution)/shard_map/river_sums/add | solution.py:639
  51.6 4.0 %collective-permute-done.3.refs_2_ = f32[1280,128]{1,0:T(8,128)} collective-permute-done((f32[1280,128]{1,0:T(8,128)}, f32[1280,128]{1,0:T(8,128)}, u32[]{:S(2)}, u32[]{:S(2)}) %collective-permute-start.3) | collective-permute-done | bytes 655392 | tf_op jit(solution)/shard_map/river_sums/ppermute | solution.py:638
  55.6 3.8 %all-to-all-start.1 = ((f32[4,1152,128]{2,1,0:T(8,128)}), f32[4,1152,128]{2,1,0:T(8,128)S(1)}, u32[]{:S(2)}, u32[]{:S(2)}) async-start(f32[4,1152,128]{2,1,0:T(8,128)} %add.19), calls=%async_computation.1 | async-start | bytes 4718592 | tf_op jit(solution)/shard_map/river_sums/all_to_all | solution.py:641
  59.5 28.3 %replies.1 = (f32[16,184,128]{2,1,0:T(8,128)}, f32[4,64,128]{2,1,0:T(8,128)}, f32[4,64,128]{2,1,0:T(8,128)}) custom-call(s32[12288]{0:T(1024)} %bitcast.24, s32[6144]{0:T(1024)} %bitcast.26, s32[3]{0:T(128)} %tcard_ref.3, s32[2,3]{1,0:T(2,128)} %bitcast.28, s32[3,2,1081]{2,1,0:T(2,128)} %rank_ref.3, s32[3,1081]{1,0:T(4,128)} %trow_ref.1, ...), custom_call_target="tpu_custom_call" | custom-call | flops 30000001024 | bytes 1000000 | tf_op jit(solution)/shard_map/replies/replies/pallas_call | solution.py:647
  87.7 0.6 collective-permute-start.8
  88.3 1.2 collective-permute-done.8
  89.5 0.9 add.20
  90.5 1.7 %collective-permute-start.10 = (f32[64,128]{1,0:T(8,128)S(1)}, f32[64,128]{1,0:T(8,128)S(1)}, u32[]{:S(2)}, u32[]{:S(2)}) collective-permute-start(f32[64,128]{1,0:T(8,128)S(1)} %get-tuple-element.94), channel_id=1, source_target_pairs={{0,32},{32,64},{64,96},{96,0},{1,33},{33,65},{65,97},{97,1},{2,34}... | collective-permute-start | bytes 98312 | tf_op jit(solution)/shard_map/turn_sums/ppermute | solution.py:493
  92.2 1.6 %collective-permute-start.11 = (f32[64,128]{1,0:T(8,128)S(1)}, f32[64,128]{1,0:T(8,128)S(1)}, u32[]{:S(2)}, u32[]{:S(2)}) collective-permute-start(f32[64,128]{1,0:T(8,128)S(1)} %get-tuple-element.93), channel_id=1, source_target_pairs={{0,96},{32,0},{64,32},{96,64},{1,97},{33,1},{65,33},{97,65},{2,98}... | collective-permute-start | bytes 98312 | tf_op jit(solution)/shard_map/turn_sums/ppermute | solution.py:493
  93.8 1.9 %collective-permute-start.9 = (f32[64,128]{1,0:T(8,128)S(1)}, f32[64,128]{1,0:T(8,128)S(1)}, u32[]{:S(2)}, u32[]{:S(2)}) collective-permute-start(f32[64,128]{1,0:T(8,128)S(1)} %get-tuple-element.95), channel_id=1, source_target_pairs={{0,64},{32,96},{64,0},{96,32},{1,65},{33,97},{65,1},{97,33},{2,66}... | collective-permute-start | bytes 98312 | tf_op jit(solution)/shard_map/turn_sums/ppermute | solution.py:493
  95.7 0.4 collective-permute-done.11
  96.1 3.1 %collective-permute-done.9 = f32[64,128]{1,0:T(8,128)S(1)} collective-permute-done((f32[64,128]{1,0:T(8,128)S(1)}, f32[64,128]{1,0:T(8,128)S(1)}, u32[]{:S(2)}, u32[]{:S(2)}) %collective-permute-start.9) | collective-permute-done | bytes 32800 | tf_op jit(solution)/shard_map/turn_sums/ppermute | solution.py:493
  99.2 0.6 constant_dynamic-update-slice_fusion.1
  99.9 0.2 reduce_sum.9
  100.1 0.9 constant_dynamic-update-slice_fusion
  100.9 28.7 %all_to_all.15.came_ref = f32[16,184,128]{2,1,0:T(8,128)} all-to-all(f32[16,184,128]{2,1,0:T(8,128)} %constant_dynamic-update-slice_fusion), channel_id=1, replica_groups=mesh['x'=4,'core'=2,'z'=4,'y'=4] {'z','y'}, dimensions={0} | all-to-all | bytes 3014656 | tf_op jit(solution)/shard_map/exchange/all_to_all | solution.py:721
  129.7 2.7 %update.1 = (f32[72,256]{1,0:T(8,128)}, f32[8,128]{1,0:T(8,128)}, f32[3,4,1081]{2,1,0:T(4,128)}) custom-call(f32[16,184,128]{2,1,0:T(8,128)} %all_to_all.15.came_ref, f32[72,256]{1,0:T(8,128)} %river_ref.3, f32[8,128]{1,0:T(8,128)} %turn_ref.3, bf16[256,256]{1,0:T(8,128)(2,1)} %constant.71.clone.rperm_ref, bf16[128,128]{1,0:T(8,128)(2,1)} %constant.72.clone.tperm_ref), custom_call_target="tpu_custom_call" | custom-call | tf_op jit(solution)/shard_map/update/update/pallas_call | solution.py:724
  (11 shorter events, 0.0 us)
Async XLA Ops:
  2.8 21.7 %all-to-all-start = ((f32[16,80,128]{2,1,0:T(8,128)}), f32[16,80,128]{2,1,0:T(8,128)S(1)}, u32[]{:S(2)}, u32[]{:S(2)}) async-start(f32[16,80,128]{2,1,0:T(8,128)} %get-tuple-element.62), calls=%async_computation | async-start | bytes 1310720 | tf_op jit(solution)/shard_map/strategies/all_to_all | solution.py:541
  24.5 19.3 %copy-start = (f32[16,80,128]{2,1,0:T(8,128)}, f32[16,80,128]{2,1,0:T(8,128)S(1)}, u32[]{:S(2)}) copy-start(f32[16,80,128]{2,1,0:T(8,128)S(1)} %all-to-all-done) | copy-start | bytes 1966084
  24.5 18.8 %collective-permute-start = (f32[1280,128]{1,0:T(8,128)S(1)}, f32[1280,128]{1,0:T(8,128)}, u32[]{:S(2)}, u32[]{:S(2)}) collective-permute-start(f32[1280,128]{1,0:T(8,128)S(1)} %bitcast.18), channel_id=1, source_target_pairs={{0,32},{32,64},{64,96},{96,0},{16,112},{48,16},{80,48},{112,80},{1... | collective-permute-start | bytes 1966088 | tf_op jit(solution)/shard_map/strategies/ppermute | solution.py:616
  26.1 17.3 %collective-permute-start.1 = (f32[1280,128]{1,0:T(8,128)S(1)}, f32[1280,128]{1,0:T(8,128)}, u32[]{:S(2)}, u32[]{:S(2)}) collective-permute-start(f32[1280,128]{1,0:T(8,128)S(1)} %bitcast.19), channel_id=1, source_target_pairs={{32,0},{64,32},{96,64},{0,96},{112,16},{16,48},{48,80},{80,112},{3... | collective-permute-start | bytes 1966088 | tf_op jit(solution)/shard_map/strategies/ppermute | solution.py:617
  43.3 4.8 %collective-permute-start.2 = (f32[4,1152,128]{2,1,0:T(8,128)}, f32[4,1152,128]{2,1,0:T(8,128)S(1)}, u32[]{:S(2)}, u32[]{:S(2)}) collective-permute-start(f32[4,1152,128]{2,1,0:T(8,128)} %get-tuple-element.69), channel_id=1, source_target_pairs={{0,16},{16,0},{1,17},{17,1},{2,18},{18,2},{3,19},{19,3},{4,20},{20... | collective-permute-start | bytes 7077896 | tf_op jit(solution)/shard_map/river_sums/ppermute | solution.py:637
  43.4 12.2 %collective-permute-start.3 = (f32[1280,128]{1,0:T(8,128)}, f32[1280,128]{1,0:T(8,128)}, u32[]{:S(2)}, u32[]{:S(2)}) collective-permute-start(f32[1280,128]{1,0:T(8,128)} %collective-permute-done.refs_1_), channel_id=1, source_target_pairs={{0,32},{32,64},{64,96},{96,0},{16,112},{48,16},{80,48},{112,80},{1... | collective-permute-start | bytes 1966088 | tf_op jit(solution)/shard_map/river_sums/ppermute | solution.py:638
  43.8 15.7 %collective-permute-start.4 = (f32[1280,128]{1,0:T(8,128)S(1)}, f32[1280,128]{1,0:T(8,128)}, u32[]{:S(2)}, u32[]{:S(2)}) collective-permute-start(f32[1280,128]{1,0:T(8,128)S(1)} %bitcast.20), channel_id=1, source_target_pairs={{0,16},{16,0},{1,17},{17,1},{2,18},{18,2},{3,19},{19,3},{4,20},{20... | collective-permute-start | bytes 1966088 | tf_op jit(solution)/shard_map/river_sums/ppermute | solution.py:643
  45.2 14.2 %collective-permute-start.5 = (f32[1280,128]{1,0:T(8,128)}, f32[1280,128]{1,0:T(8,128)}, u32[]{:S(2)}, u32[]{:S(2)}) collective-permute-start(f32[1280,128]{1,0:T(8,128)} %collective-permute-done.refs_1_), channel_id=1, source_target_pairs={{0,16},{16,0},{1,17},{17,1},{2,18},{18,2},{3,19},{19,3},{4,20},{20... | collective-permute-start | bytes 1966088 | tf_op jit(solution)/shard_map/river_sums/ppermute | solution.py:643
  45.2 14.3 %collective-permute-start.7 = (f32[1280,128]{1,0:T(8,128)}, f32[1280,128]{1,0:T(8,128)}, u32[]{:S(2)}, u32[]{:S(2)}) collective-permute-start(f32[1280,128]{1,0:T(8,128)} %collective-permute-done.1.refs_3_), channel_id=1, source_target_pairs={{0,16},{16,0},{1,17},{17,1},{2,18},{18,2},{3,19},{19,3},{4,20},{20... | collective-permute-start | bytes 1966088 | tf_op jit(solution)/shard_map/river_sums/ppermute | solution.py:643
  55.6 3.9 %collective-permute-start.6 = (f32[1280,128]{1,0:T(8,128)}, f32[1280,128]{1,0:T(8,128)}, u32[]{:S(2)}, u32[]{:S(2)}) collective-permute-start(f32[1280,128]{1,0:T(8,128)} %collective-permute-done.3.refs_2_), channel_id=1, source_target_pairs={{0,16},{16,0},{1,17},{17,1},{2,18},{18,2},{3,19},{19,3},{4,20},{20... | collective-permute-start | bytes 1966088 | tf_op jit(solution)/shard_map/river_sums/ppermute | solution.py:643
  55.6 43.6 %all-to-all-start.1 = ((f32[4,1152,128]{2,1,0:T(8,128)}), f32[4,1152,128]{2,1,0:T(8,128)S(1)}, u32[]{:S(2)}, u32[]{:S(2)}) async-start(f32[4,1152,128]{2,1,0:T(8,128)} %add.19), calls=%async_computation.1 | async-start | bytes 4718592 | tf_op jit(solution)/shard_map/river_sums/all_to_all | solution.py:641
  87.7 1.8 %collective-permute-start.8 = (f32[4,64,128]{2,1,0:T(8,128)}, f32[4,64,128]{2,1,0:T(8,128)S(1)}, u32[]{:S(2)}, u32[]{:S(2)}) collective-permute-start(f32[4,64,128]{2,1,0:T(8,128)} %get-tuple-element.86), channel_id=1, source_target_pairs={{0,16},{16,0},{1,17},{17,1},{2,18},{18,2},{3,19},{19,3},{4,20},{20... | collective-permute-start | bytes 393224 | tf_op jit(solution)/shard_map/turn_sums/ppermute | solution.py:713
  90.5 5.2 %collective-permute-start.10 = (f32[64,128]{1,0:T(8,128)S(1)}, f32[64,128]{1,0:T(8,128)S(1)}, u32[]{:S(2)}, u32[]{:S(2)}) collective-permute-start(f32[64,128]{1,0:T(8,128)S(1)} %get-tuple-element.94), channel_id=1, source_target_pairs={{0,32},{32,64},{64,96},{96,0},{1,33},{33,65},{65,97},{97,1},{2,34}... | collective-permute-start | bytes 98312 | tf_op jit(solution)/shard_map/turn_sums/ppermute | solution.py:493
  92.2 3.9 %collective-permute-start.11 = (f32[64,128]{1,0:T(8,128)S(1)}, f32[64,128]{1,0:T(8,128)S(1)}, u32[]{:S(2)}, u32[]{:S(2)}) collective-permute-start(f32[64,128]{1,0:T(8,128)S(1)} %get-tuple-element.93), channel_id=1, source_target_pairs={{0,96},{32,0},{64,32},{96,64},{1,97},{33,1},{65,33},{97,65},{2,98}... | collective-permute-start | bytes 98312 | tf_op jit(solution)/shard_map/turn_sums/ppermute | solution.py:493
  93.8 5.4 %collective-permute-start.9 = (f32[64,128]{1,0:T(8,128)S(1)}, f32[64,128]{1,0:T(8,128)S(1)}, u32[]{:S(2)}, u32[]{:S(2)}) collective-permute-start(f32[64,128]{1,0:T(8,128)S(1)} %get-tuple-element.95), channel_id=1, source_target_pairs={{0,64},{32,96},{64,0},{96,32},{1,65},{33,97},{65,1},{97,33},{2,66}... | collective-permute-start | bytes 98312 | tf_op jit(solution)/shard_map/turn_sums/ppermute | solution.py:493

commit v7 on v6

--- a/solution.py
+++ b/solution.py
@@ -24,7 +24,7 @@
 INDEX_ROW = 2048
 RANKS = 16384.0
 AXES = ("x", "core", "z", "y")
-VMEM_LIMIT = 60 * 1024 * 1024
+VMEM_LIMIT = 44 * 1024 * 1024
 
 
 def constants():

time: 133 us -> 153 us (1.15)
  local copies, waits for them, and re-layouts: 1.54 us -> 28.9 us
  Pallas kernels: 62.2 us -> 51.9 us
  waiting for transfers between devices: 11.2 us -> 12.9 us
    unnamed x2 -> x78, local copies, waits for them, and re-layouts: 0.01 us -> 28.9 us
    pallas_call x1, Pallas kernels: 15.5 us -> 12.1 us  [per_device(): pl.pallas_call(sum_kernel, grid_spec=pltpu.PrefetchScalarGridSpec(num_sca...]
    pallas_call x1, Pallas kernels: 13.6 us -> 11.2 us  [payoffs(): pl.pallas_call(functools.partial(payoff_kernel, rivers, start), grid_spec...]
    pallas_call x1, Pallas kernels: 28.3 us -> 26.3 us  [per_device(): pl.pallas_call(functools.partial(reply_kernel, turns, rivers, river_total...]
    ppermute x1, waiting for transfers between devices: 3.99 us -> 5.93 us  [per_device(): far = lax.ppermute(near, ('x', 'core'), onward)]
    add x1, other arithmetic: 3.46 us -> 1.69 us  [per_device(): chip = mine + got]
    reduce_sum x1, other arithmetic: 0.17 us -> 1.86 us  [per_device(): turn_sums, column = (sum(turn_parts[1:], turn_parts[0]), columns.sum(0))]
  transfers between devices with their start and end apart: 14 -> 14, of which waited for: 5 -> 6; matrix products, arithmetic and copies ran while one was open for 3% -> 1% of each run, Pallas kernels for 43% -> 33%
where the time goes in v7:
time: 153 us; the launch traced here: 151 us
  Pallas kernels  51.9 us (34%)
  local copies, waits for them, and re-layouts  28.9 us (19%)
  blocking collectives  28.5 us (19%)
  starting transfers between devices  24.7 us (16%)
  waiting for transfers between devices  12.9 us (8%)
  other arithmetic  3.57 us (2%)
    unnamed x78, local copies, waits for them, and re-layouts  28.9 us
    all_to_all x1, blocking collectives, per_device(): came = lax.all_to_all(sent, ('z', 'y'), 0, 0)  28.5 us
    pallas_call x1, Pallas kernels, per_device(): pl.pallas_call(functools.partial(reply_kernel, turns, rivers, river_total...  26.3 us
    pallas_call x1, Pallas kernels, per_device(): pl.pallas_call(sum_kernel, grid_spec=pltpu.PrefetchScalarGridSpec(num_sca...  12.1 us
    pallas_call x1, Pallas kernels, payoffs(): pl.pallas_call(functools.partial(payoff_kernel, rivers, start), grid_spec...  11.2 us
    all_to_all x1, starting transfers between devices, per_device(): plane = lax.all_to_all(strategies, ('z', 'y'), 0, 0).reshape(-1, C)  8.13 us
    ppermute x1, waiting for transfers between devices, per_device(): far = lax.ppermute(near, ('x', 'core'), onward)  5.93 us
    ppermute x3, starting transfers between devices, shifted(): return lax.ppermute(x, axis, [(i, (i + shift) % 4) for i in range(4)])  5.39 us
  transfers between devices with their start and end apart: 14, of which 6 were waited for; matrix products, arithmetic and copies ran while one was open for 1% of the time, Pallas kernels for 33%

profile of v7, /device:TPU:0, one launch (start us, length us, event | category | flops | bytes accessed | tf_op | source)
XLA Modules:
  0.0 151.4 jit_solution(14814938021938409541)
XLA Ops:
  5.3 1.2 strategies.1
  6.5 8.1 %all-to-all-start = ((f32[16,80,128]{2,1,0:T(8,128)}), f32[16,80,128]{2,1,0:T(8,128)S(1)}, u32[]{:S(2)}, u32[]{:S(2)}) async-start(f32[16,80,128]{2,1,0:T(8,128)} %get-tuple-element.62), calls=%async_computation | async-start | bytes 1310720 | tf_op jit(solution)/shard_map/strategies/all_to_all | solution.py:541
  15.4 1.4 copy-done.12
  16.9 1.0 copy-done.17
  20.6 1.7 %copy-done.29 = bf16[1152,1152]{1,0:T(8,128)(2,1)S(1)} copy-done((bf16[1152,1152]{1,0:T(8,128)(2,1)S(1)}, bf16[1152,1152]{1,0:T(8,128)(2,1)}, u32[]{:S(2)}) %copy-start.29) | copy-done | bytes 2654232
  22.3 1.1 copy-done.30
  23.4 0.9 copy-done.32
  25.0 11.2 %payoffs.1 = (f32[6,1152,128]{2,1,0:T(8,128)}, f32[3,1152,128]{2,1,0:T(8,128)S(1)}) custom-call(s32[3]{0:T(128)S(1)} %copy-done.25, s32[2,3]{1,0:T(2,128)S(1)} %bitcast.25, s32[3,2,1081]{2,1,0:T(2,128)S(1)} %copy-done.19, bf16[3,1081,2,128]{3,2,1,0:T(2,128)(2,1)S(1)} %bitcast.21, f32[64,1081]{1,0:T(8,128)S(1)} %copy-done.17, f32[1,64]{1,0:T(1,128)S(1)} %bitcast.27, ...), custom_call_target="tpu_custom_call" | custom-call | flops 24000000000 | bytes 1000000 | tf_op jit(solution)/shard_map/payoffs/payoffs/pallas_call | solution.py:558
  36.2 1.2 copy-done.37
  37.5 1.5 collective-permute-start
  38.9 1.7 %collective-permute-start.1 = (f32[1280,128]{1,0:T(8,128)S(1)}, f32[1280,128]{1,0:T(8,128)S(1)}, u32[]{:S(2)}, u32[]{:S(2)}) collective-permute-start(f32[1280,128]{1,0:T(8,128)S(1)} %bitcast.18), channel_id=1, source_target_pairs={{32,0},{64,32},{96,64},{0,96},{112,16},{16,48},{48,80},{80,112},{3... | collective-permute-start | bytes 1966088 | tf_op jit(solution)/shard_map/strategies/ppermute | solution.py:617
  40.7 2.0 %copy-done.36 = f32[6,1152,128]{2,1,0:T(8,128)S(1)} copy-done((f32[6,1152,128]{2,1,0:T(8,128)S(1)}, f32[6,1152,128]{2,1,0:T(8,128)}, u32[]{:S(2)}) %copy-start.36) | copy-done | bytes 3538968
  42.7 12.1 %sums.1 = (f32[4,1152,128]{2,1,0:T(8,128)S(1)}, f32[4,1152,128]{2,1,0:T(8,128)S(1)}) custom-call(s32[12288]{0:T(1024)S(1)} %bitcast.23, f32[6,1152,128]{2,1,0:T(8,128)S(1)} %copy-done.36), custom_call_target="tpu_custom_call" | custom-call | flops 22000001024 | bytes 1000000 | tf_op jit(solution)/shard_map/river_sums/sums/pallas_call | solution.py:620
  56.4 1.4 collective-permute-start.4
  58.4 1.9 %collective-permute-done.2 = f32[4,1152,128]{2,1,0:T(8,128)S(1)} collective-permute-done((f32[4,1152,128]{2,1,0:T(8,128)S(1)}, f32[4,1152,128]{2,1,0:T(8,128)S(1)}, u32[]{:S(2)}, u32[]{:S(2)}) %collective-permute-start.2) | collective-permute-done | bytes 2359328 | tf_op jit(solution)/shard_map/river_sums/ppermute | solution.py:637
  60.3 1.7 %add.19 = f32[4,1152,128]{2,1,0:T(8,128)} add(f32[4,1152,128]{2,1,0:T(8,128)S(1)} %get-tuple-element.66, f32[4,1152,128]{2,1,0:T(8,128)S(1)} %collective-permute-done.2) | non-fusion elementwise | flops 589824 | bytes 7077888 | tf_op jit(solution)/shard_map/river_sums/add | solution.py:639
  62.0 5.9 %collective-permute-done.3.refs_2_ = f32[1280,128]{1,0:T(8,128)S(1)} collective-permute-done((f32[1280,128]{1,0:T(8,128)S(1)}, f32[1280,128]{1,0:T(8,128)S(1)}, u32[]{:S(2)}, u32[]{:S(2)}) %collective-permute-start.3) | collective-permute-done | bytes 655392 | tf_op jit(solution)/shard_map/river_sums/ppermute | solution.py:638
  68.8 4.7 %all-to-all-start.1 = ((f32[4,1152,128]{2,1,0:T(8,128)}), f32[4,1152,128]{2,1,0:T(8,128)}, u32[]{:S(2)}, u32[]{:S(2)}) async-start(f32[4,1152,128]{2,1,0:T(8,128)} %add.19), calls=%async_computation.1 | async-start | bytes 4718592 | tf_op jit(solution)/shard_map/river_sums/all_to_all | solution.py:641
  74.4 1.1 copy-done.14
  75.5 1.1 copy-done.16
  76.6 1.0 copy-done.18
  79.0 1.1 copy-done.31
  81.7 1.5 copy-done.38
  83.2 26.3 %replies.1 = (f32[16,184,128]{2,1,0:T(8,128)S(1)}, f32[4,64,128]{2,1,0:T(8,128)S(1)}, f32[4,64,128]{2,1,0:T(8,128)S(1)}) custom-call(s32[12288]{0:T(1024)S(1)} %bitcast.22, s32[6144]{0:T(1024)S(1)} %bitcast.24, s32[3]{0:T(128)S(1)} %copy-done.26, s32[2,3]{1,0:T(2,128)S(1)} %bitcast.26, s32[3,2,1081]{2,1,0:T(2,128)S(1)} %copy-done.20, ...), custom_call_target="tpu_custom_call" | custom-call | flops 30000001024 | bytes 1000000 | tf_op jit(solution)/shard_map/replies/replies/pallas_call | solution.py:647
  109.6 1.3 collective-permute-done.8
  111.0 1.9 %collective-permute-start.10 = (f32[64,128]{1,0:T(8,128)S(1)}, f32[64,128]{1,0:T(8,128)S(1)}, u32[]{:S(2)}, u32[]{:S(2)}) collective-permute-start(f32[64,128]{1,0:T(8,128)S(1)} %get-tuple-element.94), channel_id=1, source_target_pairs={{0,32},{32,64},{64,96},{96,0},{1,33},{33,65},{65,97},{97,1},{2,34}... | collective-permute-start | bytes 98312 | tf_op jit(solution)/shard_map/turn_sums/ppermute | solution.py:493
  112.8 1.5 collective-permute-start.11
  114.3 2.1 %collective-permute-start.9 = (f32[64,128]{1,0:T(8,128)S(1)}, f32[64,128]{1,0:T(8,128)S(1)}, u32[]{:S(2)}, u32[]{:S(2)}) collective-permute-start(f32[64,128]{1,0:T(8,128)S(1)} %get-tuple-element.95), channel_id=1, source_target_pairs={{0,64},{32,96},{64,0},{96,32},{1,65},{33,97},{65,1},{97,33},{2,66}... | collective-permute-start | bytes 98312 | tf_op jit(solution)/shard_map/turn_sums/ppermute | solution.py:493
  116.7 3.0 %collective-permute-done.9 = f32[64,128]{1,0:T(8,128)S(1)} collective-permute-done((f32[64,128]{1,0:T(8,128)S(1)}, f32[64,128]{1,0:T(8,128)S(1)}, u32[]{:S(2)}, u32[]{:S(2)}) %collective-permute-start.9) | collective-permute-done | bytes 32800 | tf_op jit(solution)/shard_map/turn_sums/ppermute | solution.py:493
  119.7 1.9 %reduce_sum.9 = f32[1152,128]{1,0:T(8,128)S(1)} reduce(f32[4,1152,128]{2,1,0:T(8,128)} %all-to-all-done.1, f32[]{:T(128)} %constant.69.clone.1), dimensions={0}, to_apply=%region_0.0 | reduce | flops 442368 | bytes 2949124 | tf_op jit(solution)/shard_map/exchange/reduce_sum | solution.py:718
  121.7 28.5 %all_to_all.15.came_ref = f32[16,184,128]{2,1,0:T(8,128)S(1)} all-to-all(f32[16,184,128]{2,1,0:T(8,128)S(1)} %constant_dynamic-update-slice_fusion), channel_id=1, replica_groups=mesh['x'=4,'core'=2,'z'=4,'y'=4] {'z','y'}, dimensions={0} | all-to-all | bytes 3014656 | tf_op jit(solution)/shard_map/exchange/all_to_all | solution.py:721
  150.2 1.2 update.1
  (87 shorter events, 16.6 us)
Async XLA Ops:
  6.5 29.7 %copy-start.21 = (s32[3,16,128]{2,1,0:T(8,128)}, s32[3,16,128]{2,1,0:T(8,128)S(1)}, u32[]{:S(2)}) copy-start(s32[3,16,128]{2,1,0:T(8,128)S(1)} %get-tuple-element.61) | copy-start | bytes 73732
  6.5 30.9 %all-to-all-start = ((f32[16,80,128]{2,1,0:T(8,128)}), f32[16,80,128]{2,1,0:T(8,128)S(1)}, u32[]{:S(2)}, u32[]{:S(2)}) async-start(f32[16,80,128]{2,1,0:T(8,128)} %get-tuple-element.62), calls=%async_computation | async-start | bytes 1310720 | tf_op jit(solution)/shard_map/strategies/all_to_all | solution.py:541
  15.4 1.4 copy-start.12
  20.6 1.7 %copy-start.29 = (bf16[1152,1152]{1,0:T(8,128)(2,1)S(1)}, bf16[1152,1152]{1,0:T(8,128)(2,1)}, u32[]{:S(2)}) copy-start(bf16[1152,1152]{1,0:T(8,128)(2,1)} %constant.73.clone.disjoint_ref) | copy-start | bytes 7962628
  22.3 1.1 copy-start.30
  36.2 1.2 copy-start.37
  37.5 17.7 %collective-permute-start = (f32[1280,128]{1,0:T(8,128)S(1)}, f32[1280,128]{1,0:T(8,128)S(1)}, u32[]{:S(2)}, u32[]{:S(2)}) collective-permute-start(f32[1280,128]{1,0:T(8,128)S(1)} %bitcast.17), channel_id=1, source_target_pairs={{0,32},{32,64},{64,96},{96,0},{16,112},{48,16},{80,48},{112,80},{1... | collective-permute-start | bytes 1966088 | tf_op jit(solution)/shard_map/strategies/ppermute | solution.py:616
  38.9 16.3 %collective-permute-start.1 = (f32[1280,128]{1,0:T(8,128)S(1)}, f32[1280,128]{1,0:T(8,128)S(1)}, u32[]{:S(2)}, u32[]{:S(2)}) collective-permute-start(f32[1280,128]{1,0:T(8,128)S(1)} %bitcast.18), channel_id=1, source_target_pairs={{32,0},{64,32},{96,64},{0,96},{112,16},{16,48},{48,80},{80,112},{3... | collective-permute-start | bytes 1966088 | tf_op jit(solution)/shard_map/strategies/ppermute | solution.py:617
  40.7 2.0 %copy-start.36 = (f32[6,1152,128]{2,1,0:T(8,128)S(1)}, f32[6,1152,128]{2,1,0:T(8,128)}, u32[]{:S(2)}) copy-start(f32[6,1152,128]{2,1,0:T(8,128)} %get-tuple-element.74.delta_ref) | copy-start | bytes 10616836
  55.2 5.1 %collective-permute-start.2 = (f32[4,1152,128]{2,1,0:T(8,128)S(1)}, f32[4,1152,128]{2,1,0:T(8,128)S(1)}, u32[]{:S(2)}, u32[]{:S(2)}) collective-permute-start(f32[4,1152,128]{2,1,0:T(8,128)S(1)} %get-tuple-element.69), channel_id=1, source_target_pairs={{0,16},{16,0},{1,17},{17,1},{2,18},{18,2},{3,19},{19,3},{4,20},{20... | collective-permute-start | bytes 7077896 | tf_op jit(solution)/shard_map/river_sums/ppermute | solution.py:637
  56.1 11.8 %collective-permute-start.3 = (f32[1280,128]{1,0:T(8,128)S(1)}, f32[1280,128]{1,0:T(8,128)S(1)}, u32[]{:S(2)}, u32[]{:S(2)}) collective-permute-start(f32[1280,128]{1,0:T(8,128)S(1)} %collective-permute-done.refs_1_), channel_id=1, source_target_pairs={{0,32},{32,64},{64,96},{96,0},{16,112},{48,16},{80,48},{112,80},{1... | collective-permute-start | bytes 1966088 | tf_op jit(solution)/shard_map/river_sums/ppermute | solution.py:638
  56.4 17.1 %collective-permute-start.4 = (f32[1280,128]{1,0:T(8,128)S(1)}, f32[1280,128]{1,0:T(8,128)S(1)}, u32[]{:S(2)}, u32[]{:S(2)}) collective-permute-start(f32[1280,128]{1,0:T(8,128)S(1)} %bitcast.19), channel_id=1, source_target_pairs={{0,16},{16,0},{1,17},{17,1},{2,18},{18,2},{3,19},{19,3},{4,20},{20... | collective-permute-start | bytes 1966088 | tf_op jit(solution)/shard_map/river_sums/ppermute | solution.py:643
  57.8 16.5 %collective-permute-start.5 = (f32[1280,128]{1,0:T(8,128)S(1)}, f32[1280,128]{1,0:T(8,128)}, u32[]{:S(2)}, u32[]{:S(2)}) collective-permute-start(f32[1280,128]{1,0:T(8,128)S(1)} %collective-permute-done.refs_1_), channel_id=1, source_target_pairs={{0,16},{16,0},{1,17},{17,1},{2,18},{18,2},{3,19},{19,3},{4,20},{20... | collective-permute-start | bytes 1966088 | tf_op jit(solution)/shard_map/river_sums/ppermute | solution.py:643
  57.9 16.5 %collective-permute-start.7 = (f32[1280,128]{1,0:T(8,128)S(1)}, f32[1280,128]{1,0:T(8,128)}, u32[]{:S(2)}, u32[]{:S(2)}) collective-permute-start(f32[1280,128]{1,0:T(8,128)S(1)} %collective-permute-done.1.refs_3_), channel_id=1, source_target_pairs={{0,16},{16,0},{1,17},{17,1},{2,18},{18,2},{3,19},{19,3},{4,20},{20... | collective-permute-start | bytes 1966088 | tf_op jit(solution)/shard_map/river_sums/ppermute | solution.py:643
  61.9 12.4 %copy-start.9 = (s32[3,1081]{1,0:T(4,128)S(1)}, s32[3,1081]{1,0:T(4,128)}, u32[]{:S(2)}) copy-start(s32[3,1081]{1,0:T(4,128)} %trow_ref.1) | copy-start | bytes 38920
  61.9 12.4 %copy-start.24 = (s32[3,2]{0,1:T(2,128)S(1)}, s32[3,2]{0,1:T(2,128)}, u32[]{:S(2)}) copy-start(s32[3,2]{0,1:T(2,128)} %param.27) | copy-start | bytes 76
  61.9 12.4 %copy-start.26 = (s32[3]{0:T(128)S(1)}, s32[3]{0:T(128)}, u32[]{:S(2)}) copy-start(s32[3]{0:T(128)} %tcard_ref.3) | copy-start | bytes 40
  62.0 12.4 %copy-start.28 = (f32[64]{0:T(128)S(1)}, f32[64]{0:T(128)}, u32[]{:S(2)}) copy-start(f32[64]{0:T(128)} %param.31) | copy-start | bytes 772
  67.9 6.4 %collective-permute-start.6 = (f32[1280,128]{1,0:T(8,128)S(1)}, f32[1280,128]{1,0:T(8,128)}, u32[]{:S(2)}, u32[]{:S(2)}) collective-permute-start(f32[1280,128]{1,0:T(8,128)S(1)} %collective-permute-done.3.refs_2_), channel_id=1, source_target_pairs={{0,16},{16,0},{1,17},{17,1},{2,18},{18,2},{3,19},{19,3},{4,20},{20... | collective-permute-start | bytes 1966088 | tf_op jit(solution)/shard_map/river_sums/ppermute | solution.py:643
  68.8 50.9 %all-to-all-start.1 = ((f32[4,1152,128]{2,1,0:T(8,128)}), f32[4,1152,128]{2,1,0:T(8,128)}, u32[]{:S(2)}, u32[]{:S(2)}) async-start(f32[4,1152,128]{2,1,0:T(8,128)} %add.19), calls=%async_computation.1 | async-start | bytes 4718592 | tf_op jit(solution)/shard_map/river_sums/all_to_all | solution.py:641
  74.4 1.1 copy-start.14
  75.5 1.1 copy-start.16
  79.0 1.1 copy-start.31
  81.7 1.5 copy-start.38
  109.5 1.4 collective-permute-start.8
  111.0 5.4 %collective-permute-start.10 = (f32[64,128]{1,0:T(8,128)S(1)}, f32[64,128]{1,0:T(8,128)S(1)}, u32[]{:S(2)}, u32[]{:S(2)}) collective-permute-start(f32[64,128]{1,0:T(8,128)S(1)} %get-tuple-element.94), channel_id=1, source_target_pairs={{0,32},{32,64},{64,96},{96,0},{1,33},{33,65},{65,97},{97,1},{2,34}... | collective-permute-start | bytes 98312 | tf_op jit(solution)/shard_map/turn_sums/ppermute | solution.py:493
  112.8 3.9 %collective-permute-start.11 = (f32[64,128]{1,0:T(8,128)S(1)}, f32[64,128]{1,0:T(8,128)S(1)}, u32[]{:S(2)}, u32[]{:S(2)}) collective-permute-start(f32[64,128]{1,0:T(8,128)S(1)} %get-tuple-element.93), channel_id=1, source_target_pairs={{0,96},{32,0},{64,32},{96,64},{1,97},{33,1},{65,33},{97,65},{2,98}... | collective-permute-start | bytes 98312 | tf_op jit(solution)/shard_map/turn_sums/ppermute | solution.py:493
  114.3 5.4 %collective-permute-start.9 = (f32[64,128]{1,0:T(8,128)S(1)}, f32[64,128]{1,0:T(8,128)S(1)}, u32[]{:S(2)}, u32[]{:S(2)}) collective-permute-start(f32[64,128]{1,0:T(8,128)S(1)} %get-tuple-element.95), channel_id=1, source_target_pairs={{0,64},{32,96},{64,0},{96,32},{1,65},{33,97},{65,1},{97,33},{2,66}... | collective-permute-start | bytes 98312 | tf_op jit(solution)/shard_map/turn_sums/ppermute | solution.py:493
  121.6 28.5 %copy-start.1 = (bf16[256,256]{1,0:T(8,128)(2,1)S(1)}, bf16[256,256]{1,0:T(8,128)(2,1)}, u32[]{:S(2)}) copy-start(bf16[256,256]{1,0:T(8,128)(2,1)} %constant.71.clone.rperm_ref) | copy-start | bytes 393220
  121.7 28.5 %copy-start.3 = (f32[72,256]{1,0:T(8,128)S(1)}, f32[72,256]{1,0:T(8,128)}, u32[]{:S(2)}) copy-start(f32[72,256]{1,0:T(8,128)} %river_ref.3) | copy-start | bytes 221188
  121.7 28.5 %copy-start.6 = (bf16[128,128]{1,0:T(8,128)(2,1)S(1)}, bf16[128,128]{1,0:T(8,128)(2,1)}, u32[]{:S(2)}) copy-start(bf16[128,128]{1,0:T(8,128)(2,1)} %constant.72.clone.tperm_ref) | copy-start | bytes 98308
  121.7 28.5 %copy-start.11 = (f32[8,128]{1,0:T(8,128)S(1)}, f32[8,128]{1,0:T(8,128)}, u32[]{:S(2)}) copy-start(f32[8,128]{1,0:T(8,128)} %turn_ref.3) | copy-start | bytes 12292
  (21 other events, 16.7 us)
